TPU v7x, 256 devices: a whole 4x4x8 slice. The times are simulated.
256 devices in a mesh: seq: 8 (over z_hi, core), grp: 32 (over y, x, z_lo).
Axes of the slice: x: 4, y: 4, z: 8 (z_hi: 4, z_lo: 2; z = z_hi * 2 + z_lo), core: 2. Of those that a mesh axis runs over, the one named last changes fastest.
Arguments:
- query_first: bfloat16 [16384, 8192], P('seq', 'grp'), may hold values from -6 to 6
- key_first: bfloat16 [16384, 8192], P('seq', 'grp'), may hold values from -6 to 6
- value_first: bfloat16 [16384, 8192], P('seq', 'grp'), may hold values from -6 to 6
- query_second: bfloat16 [16384, 8192], P('seq', 'grp'), may hold values from -6 to 6
- key_second: bfloat16 [16384, 8192], P('seq', 'grp'), may hold values from -6 to 6
- cotangent: bfloat16 [16384, 8192], P('seq', 'grp'), may hold values from -6 to 6
- short_filter: bfloat16 [7, 8192], replicated, may hold values from -2 to 2
- medium_filter: bfloat16 [512, 128], replicated, may hold values from -0.5 to 0.5
Outputs:
- output_second: bfloat16 [16384, 8192], P('seq', 'grp')
- query_first_grad: bfloat16 [16384, 8192], P('seq', 'grp')
- key_first_grad: bfloat16 [16384, 8192], P('seq', 'grp')
- value_first_grad: bfloat16 [16384, 8192], P('seq', 'grp')
- query_second_grad: bfloat16 [16384, 8192], P('seq', 'grp')
- key_second_grad: bfloat16 [16384, 8192], P('seq', 'grp')
- short_filter_grad: float32 [7, 8192], replicated
- medium_filter_grad: float32 [512, 128], replicated
All inputs are finite; a program needn't handle non-finite values.
Results may differ from a plain program's by a relative error of at most 0.015.
Values may be sent and summed in bfloat16 or wider, within the bound.
No kernel may reach another device: no remote copies, remote signals or barrier semaphores. Data moves between devices by JAX's collectives and lax.ppermute only.
A program may use at most 64 MiB of HBM per device.

v0:
```python
import math

import jax
import jax.numpy as jnp
from jax import lax
from jax.sharding import PartitionSpec as P

GROUP = 16
SE_TAPS = 7
MR_TAPS = 128


def passed_along(value, axis, steps):
    count = lax.axis_size(axis)
    first, last = (max(0, -steps), min(count, count - steps))
    return lax.ppermute(value, axis, [(source, source + steps) for source in range(first, last)])


def widened(array):
    return array.astype(jnp.float32)


def narrowed(array):
    return array.astype(jnp.bfloat16)


def toeplitz_rows(coefs, offset):
    group_total = coefs.shape[0]
    span = MR_TAPS
    leading = jnp.zeros((group_total, span - offset), coefs.dtype)
    trailing = jnp.zeros((group_total, span + offset), coefs.dtype)
    line = jnp.concatenate([leading, coefs, trailing], axis=1)
    tiled = jnp.broadcast_to(line[:, None, :], (group_total, span, 3 * span)).reshape(
        group_total, 3 * span * span
    )
    skewed = tiled[:, span : span + span * (3 * span - 1)].reshape(group_total, span, 3 * span - 1)
    return skewed[:, :, : 2 * span]


def block_windows(extended):
    total_rows, chan_total = extended.shape
    block_total = total_rows // MR_TAPS - 1
    blocks = extended.reshape(block_total + 1, MR_TAPS, chan_total // GROUP, GROUP)
    return jnp.concatenate([blocks[:-1], blocks[1:]], axis=1)


def medium_apply(extended, matrix):
    total_rows, chan_total = extended.shape
    window = block_windows(extended)
    result = jnp.einsum("gik,bkgc->bigc", matrix, window, preferred_element_type=jnp.float32)
    return result.reshape(total_rows - MR_TAPS, chan_total)


def tap_gradients(grad_inner, extended):
    row_total, chan_total = grad_inner.shape
    group_total = chan_total // GROUP
    window = block_windows(extended)
    grad_blocks = grad_inner.reshape(row_total // MR_TAPS, MR_TAPS, group_total, GROUP)
    pairs = jnp.einsum("bigc,bkgc->gik", grad_blocks, window, preferred_element_type=jnp.float32)
    flat = pairs.reshape(group_total, 2 * MR_TAPS * MR_TAPS)
    flat = jnp.pad(flat, ((0, 0), (0, MR_TAPS)))
    skewed = flat.reshape(group_total, MR_TAPS, 2 * MR_TAPS + 1)
    sums = jnp.sum(skewed[:, :, 1 : MR_TAPS + 1], axis=1)
    return sums[:, ::-1]


def short_apply(extended, filt, count):
    rim = SE_TAPS - 1
    return sum(
        (
            widened(filt[shift_by])[None, :]
            * widened(extended[rim - shift_by : rim - shift_by + count])
            for shift_by in range(SE_TAPS)
        )
    )


def first_gate(short_ext, short_here, query_first, key_second):
    row_count = query_first.shape[0]
    inner_one = short_apply(short_ext, short_here, row_count)
    gated_one = narrowed(widened(query_first) * inner_one)
    product_two = narrowed(widened(key_second) * widened(gated_one))
    return (inner_one, gated_one, product_two)


def per_device(
    query_first,
    key_first,
    value_first,
    query_second,
    key_second,
    cotangent,
    short_filter,
    medium_filter,
):
    row_count, chan_count = query_first.shape
    group_count = chan_count // GROUP
    group_index = lax.axis_index("grp")
    short_here = lax.dynamic_slice_in_dim(short_filter, group_index * chan_count, chan_count, 1)
    medium_here = lax.dynamic_slice_in_dim(medium_filter, group_index * group_count, group_count, 0)
    causal_matrix = toeplitz_rows(medium_here[:, ::-1], -1)
    anti_matrix = toeplitz_rows(medium_here, 0)
    short_rim = SE_TAPS - 1
    medium_rim = MR_TAPS - 1
    zero_row = jnp.zeros((1, chan_count), jnp.bfloat16)
    product_one = narrowed(widened(key_first) * widened(value_first))
    short_prior = passed_along(product_one[row_count - short_rim :], "seq", 1)
    short_ext = jnp.concatenate([short_prior, product_one], axis=0)
    inner_one, gated_one, product_two = first_gate(short_ext, short_here, query_first, key_second)
    medium_prior = passed_along(product_two[row_count - medium_rim :], "seq", 1)
    medium_ext = jnp.concatenate([zero_row, medium_prior, product_two], axis=0)
    grad_inner_two = narrowed(widened(cotangent) * widened(query_second))
    medium_next = passed_along(grad_inner_two[:medium_rim], "seq", -1)
    inner_two = medium_apply(medium_ext, causal_matrix)
    output_two = narrowed(widened(query_second) * inner_two)
    grad_query_two = narrowed(widened(cotangent) * inner_two)
    grad_product_two = medium_apply(
        jnp.concatenate([grad_inner_two, medium_next, zero_row], axis=0), anti_matrix
    )
    grad_key_two = narrowed(grad_product_two * widened(gated_one))
    grad_gated_one = grad_product_two * widened(key_second)
    grad_query_one = narrowed(grad_gated_one * inner_one)
    grad_inner_one = narrowed(grad_gated_one * widened(query_first))
    short_next = passed_along(grad_inner_one[:short_rim], "seq", -1)
    trailing = jnp.concatenate([grad_inner_one, short_next], axis=0)
    grad_product_one = sum(
        (
            widened(short_here[shift_by])[None, :]
            * widened(trailing[shift_by : shift_by + row_count])
            for shift_by in range(SE_TAPS)
        )
    )
    grad_key_one = narrowed(grad_product_one * widened(value_first))
    grad_value_one = narrowed(grad_product_one * widened(key_first))
    short_part = jnp.stack(
        [
            jnp.sum(
                widened(grad_inner_one)
                * widened(short_ext[short_rim - shift_by : short_rim - shift_by + row_count]),
                axis=0,
            )
            for shift_by in range(SE_TAPS)
        ]
    )
    medium_part = tap_gradients(grad_inner_two, medium_ext)
    short_table = lax.dynamic_update_slice_in_dim(
        jnp.zeros(short_filter.shape, jnp.float32), short_part, group_index * chan_count, 1
    )
    medium_table = lax.dynamic_update_slice_in_dim(
        jnp.zeros(medium_filter.shape, jnp.float32), medium_part, group_index * group_count, 0
    )
    short_total, medium_total = lax.psum((short_table, medium_table), ("seq", "grp"))
    sequence_total = row_count * lax.axis_size("seq")
    short_grad = short_total * (1.0 / math.sqrt(sequence_total))
    medium_grad = medium_total * (1.0 / math.sqrt(sequence_total * GROUP))
    return (
        output_two,
        grad_query_one,
        grad_key_one,
        grad_value_one,
        grad_query_two,
        grad_key_two,
        short_grad,
        medium_grad,
    )


def solution(mesh):
    return jax.shard_map(
        per_device,
        mesh=mesh,
        in_specs=(
            P("seq", "grp"),
            P("seq", "grp"),
            P("seq", "grp"),
            P("seq", "grp"),
            P("seq", "grp"),
            P("seq", "grp"),
            P(),
            P(),
        ),
        out_specs=(
            P("seq", "grp"),
            P("seq", "grp"),
            P("seq", "grp"),
            P("seq", "grp"),
            P("seq", "grp"),
            P("seq", "grp"),
            P(),
            P(),
        ),
        check_vma=False,
    )
```

profile of v0, /device:TPU:2, one launch (start us, length us, event | category | flops | bytes accessed | tf_op | source)
XLA Modules:
  0.0 374.7 jit_solution(3664265734821889594)
XLA Ops:
  7.2 1.6 copy.20
  8.8 0.6 copy.19
  9.5 0.4 fusion.4
  9.9 0.1 slice.153
  10.0 1.7 collective-permute-start
  11.8 1.5 copy.24
  13.3 2.6 copy.16
  15.9 1.6 fusion.14
  17.6 1.4 collective-permute-start.2
  19.0 2.3 copy.18
  21.3 1.4 copy.17
  22.7 0.2 copy.44
  22.9 1.2 copy.25
  24.3 0.1 broadcast_in_dim.18
  24.4 0.9 copy.46
  25.4 1.3 slice.170
  26.6 5.6 %reshape.54 = bf16[16,128,383]{2,1,0:T(8,128)(2,1)} reshape(bf16[16,49024]{1,0:T(8,128)(2,1)} %slice.170) | data formatting | bytes 3137536 | tf_op jit(solution)/shard_map/reshape | solution.py:36
  32.4 0.1 broadcast_in_dim.17
  32.6 0.9 copy.42
  33.5 1.3 slice.166
  34.8 5.7 %reshape.51 = bf16[16,128,383]{2,1,0:T(8,128)(2,1)} reshape(bf16[16,49024]{1,0:T(8,128)(2,1)} %slice.166) | data formatting | bytes 3137536 | tf_op jit(solution)/shard_map/reshape | solution.py:36
  40.5 1.0 dynamic-slice_convert_fusion.6
  41.5 1.9 concatenate.29
  43.5 1.3 slice_bitcast_fusion.2
  44.8 0.2 copy.45
  45.0 0.3 copy.26
  45.3 0.9 copy-done.15
  46.2 0.3 copy-done.18
  46.4 0.7 fusion.35
  47.2 0.7 copy.27
  47.9 0.5 copy-done.8
  48.4 4.6 %fusion.13 = (bf16[2048,256]{0,1:T(8,128)(2,1)}, f32[2048,256]{0,1:T(8,128)S(1)}) fusion(f32[32,8,16,128]{3,2,1,0:T(8,128)S(1)} %bitcast.79, bf16[2048,256]{0,1:T(8,128)(2,1)S(1)} %copy-done.8, bf16[2048,256]{0,1:T(8,128)(2,1)S(1)} %fusion.4, bf16[6,256]{0,1:T(8,128)(2,1)S(1)} %collective-permute-done, f32[256]{0:T(256)S(1)} %bitcast.107, ...), kind=kLoop, calls=%fused_computation.49 | loop fusion | flops 23068672 | bytes 7350272 | tf_op jit(solution)/shard_map/convert_element_type | solution.py:24
  53.0 5.2 %fusion.28 = (f32[256]{0:T(256)S(1)}, f32[256]{0:T(256)S(1)}, f32[256]{0:T(256)S(1)}, f32[256]{0:T(256)S(1)}, f32[256]{0:T(256)S(1)}, /*index=5*/f32[256]{0:T(25...) fusion(bf16[2048,256]{0,1:T(8,128)(2,1)S(1)} %fusion.4, ...), kind=kLoop, calls=%fused_computation.64 | loop fusion | flops 27261184 | bytes 10496000 | tf_op jit(solution)/shard_map/reduce_sum | solution.py:137
  58.3 6.1 %collective-permute-start.1 = (bf16[127,256]{0,1:T(8,128)(2,1)S(1)}, bf16[127,256]{0,1:T(8,128)(2,1)S(1)}, u32[]{:S(2)}, u32[]{:S(2)}) collective-permute-start(bf16[127,256]{0,1:T(8,128)(2,1)S(1)} %slice.164), channel_id=1, source_target_pairs={{0,32},{32,64},{64,96},{96,128},{128,160},{160,192},{192,224},{1,3... | collective-permute-start | bytes 195080 | tf_op jit(solution)/shard_map/ppermute | solution.py:16
  64.4 1.3 collective-permute-start.3
  65.8 0.7 copy-done.20
  66.5 1.2 copy.41
  67.7 2.4 copy.30
  70.2 1.3 copy.34
  71.5 10.4 %fusion.3 = (bf16[2048,256]{0,1:T(8,128)(2,1)}, f32[2048,256]{0,1:T(8,128)S(1)}) fusion(bf16[2048,256]{0,1:T(8,128)(2,1)} %copy-done.7, bf16[6,256]{0,1:T(8,128)(2,1)S(1)} %collective-permute-done.3, bf16[2048,256]{0,1:T(8,128)(2,1)} %copy-done.9, f32[256]{0:T(256)S(1)} %bitcast.108, f32[256]{0:T(256)S(1)} %bitcast.98, f32[256]{0:T(256)S(1)} %bitcast.100, ...), kind=kLoop, calls=%fused_computation.39 | loop fusion | flops 21495808 | bytes 5253120 | tf_op jit(solution)/shard_map/convert_element_type | solution.py:24
  81.9 1.3 fusion.5
  83.2 2.3 copy.31
  85.6 1.3 copy.32
  86.9 1.8 concatenate.26
  88.7 1.3 slice_bitcast_fusion.5
  90.0 0.2 copy.40
  90.3 0.3 copy_dynamic-update-slice_fusion.1
  90.6 0.7 copy-done.11
  91.3 0.5 copy_dynamic-update-slice_fusion
  91.7 0.8 fusion.33
  92.6 0.6 copy-done.10
  93.1 0.7 convolution_bitcast_fusion
  93.8 2.0 copy.23
  95.8 1.2 copy.48
  97.1 0.1 pad.4
  97.2 3.7 reshape.57
  100.9 2.0 slice_reduce_fusion
  103.0 0.7 copy-done.19
  103.8 3.7 fusion.15
  107.4 2.3 copy.29
  109.7 1.3 copy.33
  111.0 253.5 %all-reduce.4.cloned.1.call-done = (f32[7,8192]{1,0:T(8,128)}, f32[512,128]{1,0:T(8,128)}) async-done(((f32[7,8192]{1,0:T(8,128)}, f32[512,128]{1,0:T(8,128)}), (f32[7,8192]{1,0:T(8,128)}, f32[512,128]{1,0:T(8,128)})) %all-reduce.4.cloned.1.call-update) | async-done | bytes 491536 | tf_op jit(solution)/shard_map/psum | solution.py:152
  364.5 1.7 broadcast_multiply_fusion.1
  366.2 1.7 broadcast_multiply_fusion
  (72 shorter events, 0.7 us)
Async XLA Ops:
  7.2 17.0 %copy-start = (bf16[512,128]{1,0:T(8,128)(2,1)S(1)}, bf16[512,128]{1,0:T(8,128)(2,1)}, u32[]{:S(2)}) copy-start(bf16[512,128]{1,0:T(8,128)(2,1)} %param.15) | copy-start | bytes 393220
  7.2 1.6 copy-start.16
  7.2 357.3 %all-reduce.4.cloned.1.call-start = ((), (), s32[]{:S(2)}) async-start(), calls=%async_computation | async-start | bytes 1048576 | tf_op jit(solution)/shard_map/psum | solution.py:152
  8.8 1.1 copy-start.5
  9.5 3.8 %copy-start.7 = (bf16[2048,256]{0,1:T(8,128)(2,1)}, bf16[2048,256]{0,1:T(8,128)(2,1)S(1)}, u32[]{:S(2)}) copy-start(bf16[2048,256]{0,1:T(8,128)(2,1)S(1)} %copy.19) | copy-start | bytes 3145732
  10.0 37.8 %collective-permute-start = (bf16[6,256]{0,1:T(8,128)(2,1)S(1)}, bf16[6,256]{0,1:T(8,128)(2,1)S(1)}, u32[]{:S(2)}, u32[]{:S(2)}) collective-permute-start(bf16[6,256]{0,1:T(8,128)(2,1)S(1)} %slice.153), channel_id=1, source_target_pairs={{0,32},{32,64},{64,96},{96,128},{128,160},{160,192},{192,224},{1,3... | collective-permute-start | bytes 9224 | tf_op jit(solution)/shard_map/ppermute | solution.py:16
  13.3 4.3 %copy-start.2 = (bf16[2048,256]{0,1:T(8,128)(2,1)}, bf16[2048,256]{0,1:T(8,128)(2,1)S(1)}, u32[]{:S(2)}) copy-start(bf16[2048,256]{0,1:T(8,128)(2,1)S(1)} %copy.24) | copy-start | bytes 3145732
  17.6 3.7 copy-start.17
  17.6 23.9 %collective-permute-start.2 = (bf16[127,256]{0,1:T(8,128)(2,1)S(1)}, bf16[127,256]{0,1:T(8,128)(2,1)S(1)}, u32[]{:S(2)}, u32[]{:S(2)}) collective-permute-start(bf16[127,256]{0,1:T(8,128)(2,1)S(1)} %slice.168), channel_id=1, source_target_pairs={{32,0},{64,32},{96,64},{128,96},{160,128},{192,160},{224,192},{33,... | collective-permute-start | bytes 195080 | tf_op jit(solution)/shard_map/ppermute | solution.py:16
  41.5 6.4 %copy-start.21 = (f32[1,256]{1,0:T(1,128)}, f32[1,256]{1,0:T(1,128)S(1)}, u32[]{:S(2)}) copy-start(f32[1,256]{1,0:T(1,128)S(1)} %get-tuple-element.38) | copy-start | bytes 3076
  41.5 6.4 %copy-start.23 = (f32[1,256]{1,0:T(1,128)}, f32[1,256]{1,0:T(1,128)S(1)}, u32[]{:S(2)}) copy-start(f32[1,256]{1,0:T(1,128)S(1)} %get-tuple-element.39) | copy-start | bytes 3076
  41.5 6.4 %copy-start.25 = (f32[1,256]{1,0:T(1,128)}, f32[1,256]{1,0:T(1,128)S(1)}, u32[]{:S(2)}) copy-start(f32[1,256]{1,0:T(1,128)S(1)} %get-tuple-element.40) | copy-start | bytes 3076
  44.7 1.4 copy-start.15
  44.8 1.7 copy-start.18
  47.2 1.2 copy-start.8
  48.4 4.6 %copy-start.14 = (bf16[2048,256]{0,1:T(8,128)(2,1)S(1)}, bf16[2048,256]{0,1:T(8,128)(2,1)}, u32[]{:S(2)}) copy-start(bf16[2048,256]{0,1:T(8,128)(2,1)} %copy.17) | copy-start | bytes 3145732
  58.2 6.2 %copy-start.9 = (bf16[2048,256]{0,1:T(8,128)(2,1)}, bf16[2048,256]{0,1:T(8,128)(2,1)S(1)}, u32[]{:S(2)}) copy-start(bf16[2048,256]{0,1:T(8,128)(2,1)S(1)} %get-tuple-element.25) | copy-start | bytes 3145732
  58.3 28.6 %collective-permute-start.1 = (bf16[127,256]{0,1:T(8,128)(2,1)S(1)}, bf16[127,256]{0,1:T(8,128)(2,1)S(1)}, u32[]{:S(2)}, u32[]{:S(2)}) collective-permute-start(bf16[127,256]{0,1:T(8,128)(2,1)S(1)} %slice.164), channel_id=1, source_target_pairs={{0,32},{32,64},{64,96},{96,128},{128,160},{160,192},{192,224},{1,3... | collective-permute-start | bytes 195080 | tf_op jit(solution)/shard_map/ppermute | solution.py:16
  64.4 7.0 %collective-permute-start.3 = (bf16[6,256]{0,1:T(8,128)(2,1)S(1)}, bf16[6,256]{0,1:T(8,128)(2,1)S(1)}, u32[]{:S(2)}, u32[]{:S(2)}) collective-permute-start(bf16[6,256]{0,1:T(8,128)(2,1)S(1)} %slice.172), channel_id=1, source_target_pairs={{32,0},{64,32},{96,64},{128,96},{160,128},{192,160},{224,192},{33,... | collective-permute-start | bytes 9224 | tf_op jit(solution)/shard_map/ppermute | solution.py:16
  65.8 0.7 copy-start.20
  66.5 3.7 copy-start.12
  67.7 3.8 %copy-start.22 = (f32[1,256]{1,0:T(1,128)S(1)}, f32[1,256]{1,0:T(1,128)}, u32[]{:S(2)}) copy-start(f32[1,256]{1,0:T(1,128)} %copy-done.21) | copy-start | bytes 3076
  67.7 3.8 %copy-start.24 = (f32[1,256]{1,0:T(1,128)S(1)}, f32[1,256]{1,0:T(1,128)}, u32[]{:S(2)}) copy-start(f32[1,256]{1,0:T(1,128)} %copy-done.23) | copy-start | bytes 3076
  67.7 3.8 %copy-start.26 = (f32[1,256]{1,0:T(1,128)S(1)}, f32[1,256]{1,0:T(1,128)}, u32[]{:S(2)}) copy-start(f32[1,256]{1,0:T(1,128)} %copy-done.25) | copy-start | bytes 3076
  71.5 10.4 %copy-start.6 = (bf16[2048,256]{0,1:T(8,128)(2,1)S(1)}, bf16[2048,256]{0,1:T(8,128)(2,1)}, u32[]{:S(2)}) copy-start(bf16[2048,256]{0,1:T(8,128)(2,1)} %copy-done.5) | copy-start | bytes 3145732
  83.2 2.4 copy-start.13
  90.0 1.2 copy-start.11
  91.7 1.4 copy-start.10
  97.2 6.5 %copy-start.4 = (bf16[2048,256]{0,1:T(8,128)(2,1)S(1)}, bf16[2048,256]{0,1:T(8,128)(2,1)}, u32[]{:S(2)}) copy-start(bf16[2048,256]{0,1:T(8,128)(2,1)} %copy.16) | copy-start | bytes 3145732
  100.9 2.9 copy-start.3
  103.0 0.7 copy-start.19
  107.4 260.4 %copy-start.1 = (bf16[512,128]{1,0:T(8,128)(2,1)S(1)}, bf16[512,128]{1,0:T(8,128)(2,1)}, u32[]{:S(2)}) copy-start(bf16[512,128]{1,0:T(8,128)(2,1)} %param.15) | copy-start | bytes 393220
Sparse Core Ops, SparseCore 0:
  103.9 260.5 all-reduce.3
where the time goes:
time: 375 us
  waiting for transfers between devices  253 us (67%)
  local copies, waits for them, and re-layouts  60.2 us (16%)
  other arithmetic  33.7 us (9%)
  between operations  14.5 us (4%)
  starting transfers between devices  10.6 us (3%)
    psum x1, waiting for transfers between devices, per_device(): lax.psum((short_table, medium_table), ('seq', 'grp'))  253 us
    unnamed x76, local copies, waits for them, and re-layouts  33.3 us
    convert_element_type x6, other arithmetic, narrowed(): return array.astype(jnp.bfloat16)  22 us
    reshape x2, local copies, waits for them, and re-layouts, toeplitz_rows(): tiled[:, span:span + span * (3 * span - 1)]  11.3 us
    ppermute x4, starting transfers between devices, passed_along(): lax.ppermute(value, axis, [(source, source + steps) for source in range(f...  10.5 us
  transfers between devices with their start and end apart: 5, of which 1 were waited for; matrix products, arithmetic and copies ran while one was open for 16% of the time, Pallas kernels for 0%

commit v1 on v0

v1 whole, which is shorter than its diff:
```python
import functools
import math

import jax
import jax.numpy as jnp
from jax import lax
from jax.experimental import pallas as pl
from jax.experimental.pallas import tpu as pltpu
from jax.sharding import PartitionSpec as P

GROUP = 16
SE_TAPS = 7
MR_TAPS = 128
BLOCK = 128
LANES = 128
RIM = 8
HALO = 16
VMEM_LIMIT = 63 * 1024 * 1024


def widened(array):
    return array.astype(jnp.float32)


def narrowed(array):
    return array.astype(jnp.bfloat16)


def passed_along(value, axis, steps):
    count = lax.axis_size(axis)
    first, last = (max(0, -steps), min(count, count - steps))
    return lax.ppermute(value, axis, [(source, source + steps) for source in range(first, last)])


def rows_of(index, count):
    return pl.ds(pl.multiple_of(index * count, count), count)


def short_causal(prior, here, taps):
    ext = jnp.concatenate([prior, here], axis=0)
    total = taps[0:1] * here
    for shift_by in range(1, SE_TAPS):
        total += taps[shift_by : shift_by + 1] * pltpu.roll(ext, shift_by, 0)[RIM:]
    return total


def upper_lower(coefs):
    line = jnp.concatenate([coefs, jnp.zeros_like(coefs)], axis=1)
    table = jnp.broadcast_to(line, (BLOCK, 2 * BLOCK))
    return narrowed(pltpu.roll(table, 0, 1, stride=1, stride_axis=0))


def dotted(left, right, dims):
    return lax.dot_general(left, right, (dims, ((), ())), preferred_element_type=jnp.float32)


def turned(tile):
    return tile.T.reshape(LANES // GROUP, GROUP, BLOCK)


def rims_kernel(
    key_tail, value_tail, query_tail, key_two_tail,
    cotangent_head, query_two_head, query_head, key_two_head,
    short_ref, medium_ref, tail_ref, head_ref,
):
    taps = widened(short_ref[...])
    start = 2 * BLOCK - BLOCK - HALO
    product_one = widened(key_tail[start:]) * widened(value_tail[start:])
    inner_one = short_causal(product_one[RIM:HALO], product_one[HALO:], taps)
    product_two = widened(key_two_tail[BLOCK:]) * (widened(query_tail[BLOCK:]) * inner_one)
    tail_ref[:HALO] = narrowed(product_one[BLOCK:])
    tail_ref[HALO:] = narrowed(product_two)
    grad_inner = narrowed(
        widened(cotangent_head[: BLOCK + HALO]) * widened(query_two_head[: BLOCK + HALO])
    )
    head_ref[:BLOCK] = grad_inner[:BLOCK]
    wide = widened(grad_inner)
    chan_count = wide.shape[1]
    group_count = chan_count // GROUP
    owner = lax.broadcasted_iota(jnp.int32, (group_count, chan_count), 1) // GROUP
    spread = narrowed(widened(owner == lax.broadcasted_iota(jnp.int32, owner.shape, 0)))
    coefs = dotted(widened(medium_ref[...]).T, widened(spread), ((1,), (0,)))
    row = lax.broadcasted_iota(jnp.int32, (HALO, chan_count), 0)
    grad_product = jnp.zeros((HALO, chan_count), jnp.float32)
    for shift_by in range(SE_TAPS - 1):
        moved = wide[:BLOCK]
        if shift_by:
            moved = pltpu.roll(wide, BLOCK + HALO - shift_by, 0)[:BLOCK]
        line = jnp.sum(coefs * moved, axis=0, keepdims=True)
        grad_product = jnp.where(row == shift_by, line, grad_product)
    head_ref[BLOCK:] = narrowed(
        grad_product * widened(key_two_head[...]) * widened(query_head[...])
    )


def gradient_kernel(
    query_ref, key_ref, value_ref, query_two_ref, key_two_ref, cotangent_ref,
    short_ref, medium_ref, tail_ref, head_ref,
    query_grad_ref, key_two_grad_ref, product_ref, grad_inner_ref, parts_ref,
    inner_ref, first_ref, later_ref, turned_ref, back_ref,
):
    row_count = query_ref.shape[0]
    block_count = row_count // BLOCK
    group_count = LANES // GROUP
    taps = widened(short_ref[...])
    sequence_total = row_count * lax.axis_size("seq")

    product_ref[:, :GROUP, :] = turned(tail_ref[HALO:])
    turned_ref[:, block_count * GROUP :, :] = turned(head_ref[:BLOCK])
    grad_inner_ref[row_count:] = head_ref[BLOCK:]

    def forward(index, _):
        rows = rows_of(index, BLOCK)
        product_one = widened(key_ref[rows]) * widened(value_ref[rows])
        first_ref[pl.ds(pl.multiple_of(index * BLOCK + RIM, RIM), BLOCK)] = product_one
        inner_one = taps[0:1] * product_one
        for shift_by in range(1, SE_TAPS):
            inner_one += (
                taps[shift_by : shift_by + 1]
                * first_ref[pl.ds(index * BLOCK + RIM - shift_by, BLOCK)]
            )
        inner_ref[rows] = inner_one
        product_two = narrowed(
            widened(key_two_ref[rows]) * (widened(query_ref[rows]) * inner_one)
        )
        product_ref[:, rows_of(index + 1, GROUP), :] = turned(product_two)
        grad_inner_two = narrowed(widened(cotangent_ref[rows]) * widened(query_two_ref[rows]))
        turned_ref[:, rows_of(index, GROUP), :] = turned(grad_inner_two)
        return 0

    first_ref[:RIM] = widened(tail_ref[RIM:HALO])
    lax.fori_loop(0, block_count, forward, 0)

    span = block_count * GROUP
    flip_row = lax.broadcasted_iota(jnp.int32, (BLOCK, BLOCK), 0)
    flip_lane = lax.broadcasted_iota(jnp.int32, (BLOCK, BLOCK), 1)
    flip = narrowed(widened(flip_row + flip_lane == BLOCK - 1))
    medium_scale = 1.0 / math.sqrt(sequence_total * GROUP)
    for group in range(group_count):
        bands = upper_lower(widened(medium_ref[group : group + 1]))
        window = jnp.concatenate(
            [turned_ref[group, :span], turned_ref[group, GROUP : GROUP + span]], axis=1
        )
        back_ref[group] = narrowed(dotted(window, bands, ((1,), (1,))))
        flipped = narrowed(dotted(flip, product_ref[group, GROUP:], ((1,), (1,))))
        pairs = dotted(flipped, window, ((1,), (0,)))
        pairs = pltpu.roll(pairs, BLOCK + 1, 1, stride=1, stride_axis=0)
        line = jnp.sum(pairs[:, :BLOCK], axis=0, keepdims=True) * medium_scale
        parts_ref[:, RIM + group : RIM + group + 1, :] = jnp.broadcast_to(
            line[None], (parts_ref.shape[0], 1, LANES)
        )

    def backward(step, sums):
        index = block_count - 1 - step
        rows = rows_of(index, BLOCK)
        turned_back = back_ref[:, rows_of(index, GROUP), :].reshape(LANES, BLOCK)
        grad_product = widened(turned_back.T)
        inner_one = inner_ref[rows]
        query = widened(query_ref[rows])
        key_two_grad_ref[rows] = narrowed(grad_product * (query * inner_one))
        grad_gated = grad_product * widened(key_two_ref[rows])
        query_grad_ref[rows] = narrowed(grad_gated * inner_one)
        grad_inner = grad_gated * query
        grad_inner_ref[rows] = narrowed(grad_inner)
        later_ref[rows] = grad_inner
        product_one = first_ref[pl.ds(pl.multiple_of(index * BLOCK + RIM, RIM), BLOCK)]
        moved = [grad_inner] + [
            later_ref[pl.ds(index * BLOCK + shift_by, BLOCK)] for shift_by in range(1, SE_TAPS)
        ]
        return [
            total + jnp.sum((product_one * other).reshape(BLOCK // RIM, RIM, LANES), axis=0)
            for total, other in zip(sums, moved)
        ]

    later_ref[row_count:] = widened(head_ref[BLOCK:])[:RIM]
    sums = lax.fori_loop(
        0, block_count, backward, [jnp.zeros((RIM, LANES), jnp.float32)] * SE_TAPS
    )
    short_scale = 1.0 / math.sqrt(sequence_total)
    lines = [jnp.sum(total, axis=0, keepdims=True) * short_scale for total in sums]
    lines = jnp.concatenate(lines + [jnp.zeros_like(lines[0])], axis=0)
    parts_ref[:, :RIM, :] = jnp.broadcast_to(lines[None], (parts_ref.shape[0], RIM, LANES))


def medium_kernel(
    product_ref, query_two_ref, cotangent_ref, medium_ref, output_ref, query_grad_ref, inner_ref
):
    block_count = query_two_ref.shape[0] // BLOCK
    span = block_count * GROUP
    for group in range(LANES // GROUP):
        bands = upper_lower(widened(medium_ref[group : group + 1]))
        inner_ref[group] = narrowed(
            dotted(product_ref[group, :span], bands[:, BLOCK:], ((1,), (0,)))
            + dotted(product_ref[group, GROUP:], bands[:, :BLOCK], ((1,), (0,)))
        )

    def one_block(index, _):
        rows = rows_of(index, BLOCK)
        inner_two = widened(inner_ref[:, rows_of(index, GROUP), :].reshape(LANES, BLOCK).T)
        output_ref[rows] = narrowed(widened(query_two_ref[rows]) * inner_two)
        query_grad_ref[rows] = narrowed(widened(cotangent_ref[rows]) * inner_two)
        return 0

    lax.fori_loop(0, block_count, one_block, 0)


def short_kernel(
    grad_inner_ref, key_ref, value_ref, short_ref, key_grad_ref, value_grad_ref, later_ref
):
    taps = widened(short_ref[...])
    block_count = key_ref.shape[0] // BLOCK

    row_count = key_ref.shape[0]
    later_ref[row_count:] = widened(grad_inner_ref[row_count:])[:RIM]

    def one_block(step, _):
        index = block_count - 1 - step
        rows = rows_of(index, BLOCK)
        here = widened(grad_inner_ref[rows])
        later_ref[rows] = here
        total = taps[0:1] * here
        for shift_by in range(1, SE_TAPS):
            total += (
                taps[shift_by : shift_by + 1] * later_ref[pl.ds(index * BLOCK + shift_by, BLOCK)]
            )
        key_grad_ref[rows] = narrowed(total * widened(value_ref[rows]))
        value_grad_ref[rows] = narrowed(total * widened(key_ref[rows]))
        return 0

    lax.fori_loop(0, block_count, one_block, 0)


def unpack_kernel(table_ref, short_ref, medium_ref):
    chan_count = table_ref.shape[2]
    groups = LANES // GROUP
    for place in range(table_ref.shape[0]):
        piece = widened(table_ref[place])
        short_ref[:, place * chan_count : (place + 1) * chan_count] = piece[:SE_TAPS]
        for half in range(chan_count // LANES):
            first = (place * (chan_count // LANES) + half) * groups
            medium_ref[first : first + groups] = piece[RIM:, half * LANES : (half + 1) * LANES]


def gather_groups(count):
    run = min(8, count)
    near = [list(range(first, first + run)) for first in range(0, count, run)]
    far = [list(range(first, count, run)) for first in range(run)]
    return near, far


def params():
    return pltpu.CompilerParams(vmem_limit_bytes=VMEM_LIMIT)


def cost(flops, size):
    return pl.CostEstimate(flops=flops, bytes_accessed=size, transcendentals=0)


def per_device(
    query_first,
    key_first,
    value_first,
    query_second,
    key_second,
    cotangent,
    short_filter,
    medium_filter,
):
    row_count, chan_count = query_first.shape
    group_count = chan_count // GROUP
    block_count = row_count // BLOCK
    halves = chan_count // LANES
    half_groups = LANES // GROUP
    group_index = lax.axis_index("grp")
    short_here = lax.dynamic_slice_in_dim(short_filter, group_index * chan_count, chan_count, 1)
    medium_here = lax.dynamic_slice_in_dim(medium_filter, group_index * group_count, group_count, 0)
    sds = jax.ShapeDtypeStruct
    wide = sds((row_count, chan_count), jnp.bfloat16)
    size = row_count * chan_count * 2

    last = row_count // (2 * BLOCK) - 1
    tail_spec = pl.BlockSpec((2 * BLOCK, chan_count), lambda i: (last, 0))
    head_spec = pl.BlockSpec((2 * BLOCK, chan_count), lambda i: (0, 0))
    rim_spec = pl.BlockSpec((HALO, chan_count), lambda i: (0, 0))
    halo_spec = pl.BlockSpec((HALO + BLOCK, chan_count), lambda i: (0, 0))
    halo = sds((HALO + BLOCK, chan_count), jnp.bfloat16)
    tail, head = pl.pallas_call(
        rims_kernel,
        grid=(1,),
        out_shape=(halo, halo),
        in_specs=[tail_spec] * 4
        + [head_spec] * 2
        + [rim_spec] * 2
        + [
            pl.BlockSpec((SE_TAPS, chan_count), lambda i: (0, 0)),
            pl.BlockSpec((group_count, MR_TAPS), lambda i: (0, 0)),
        ],
        out_specs=(halo_spec, halo_spec),
        compiler_params=params(),
        cost_estimate=cost(2 * 6 * 2 * BLOCK * chan_count * 16, size),
        name="rims",
    )(
        key_first, value_first, query_first, key_second,
        cotangent, query_second, query_first, key_second,
        short_here, medium_here,
    )
    tail = passed_along(tail, "seq", 1)
    head = passed_along(head, "seq", -1)

    full_spec = pl.BlockSpec((row_count, LANES), lambda i: (0, i))
    short_spec = pl.BlockSpec((SE_TAPS, LANES), lambda i: (0, i))
    medium_spec = pl.BlockSpec((half_groups, MR_TAPS), lambda i: (i, 0))
    half_halo = pl.BlockSpec((HALO + BLOCK, LANES), lambda i: (0, i))
    lines = (block_count + 1) * GROUP
    product_spec = pl.BlockSpec((half_groups, lines, BLOCK), lambda i: (i, 0, 0))
    inner_spec = pl.BlockSpec((row_count + HALO, LANES), lambda i: (0, i))
    seq_count = lax.axis_size("seq")
    parts_spec = pl.BlockSpec((seq_count, 2 * RIM, LANES), lambda i: (0, 0, i))
    query_first_grad, key_second_grad, product_two, grad_inner_one, parts = pl.pallas_call(
        gradient_kernel,
        grid=(halves,),
        out_shape=(
            wide,
            wide,
            sds((group_count, lines, BLOCK), jnp.bfloat16),
            sds((row_count + HALO, chan_count), jnp.bfloat16),
            sds((seq_count, 2 * RIM, chan_count), jnp.float32),
        ),
        in_specs=[full_spec] * 6 + [short_spec, medium_spec, half_halo, half_halo],
        out_specs=(full_spec, full_spec, product_spec, inner_spec, parts_spec),
        scratch_shapes=[
            pltpu.VMEM((row_count, LANES), jnp.float32),
            pltpu.VMEM((row_count + RIM, LANES), jnp.float32),
            pltpu.VMEM((row_count + RIM, LANES), jnp.float32),
            pltpu.VMEM((half_groups, lines, BLOCK), jnp.bfloat16),
            pltpu.VMEM((half_groups, lines - GROUP, BLOCK), jnp.bfloat16),
        ],
        compiler_params=params(),
        cost_estimate=cost(100 * row_count * chan_count, 10 * size),
        name="gradients",
    )(
        query_first, key_first, value_first, query_second, key_second, cotangent,
        short_here, medium_here, tail, head,
    )

    partials = lax.all_to_all(parts, "seq", 0, 0)

    output_second, query_second_grad = pl.pallas_call(
        medium_kernel,
        grid=(halves,),
        out_shape=(wide, wide),
        in_specs=[product_spec, full_spec, full_spec, medium_spec],
        out_specs=(full_spec, full_spec),
        scratch_shapes=[pltpu.VMEM((half_groups, lines - GROUP, BLOCK), jnp.bfloat16)],
        compiler_params=params(),
        cost_estimate=cost(40 * row_count * chan_count, 5 * size),
        name="medium_outputs",
    )(product_two, query_second, cotangent, medium_here)
    partials, output_second, query_second_grad = lax.optimization_barrier(
        (partials, output_second, query_second_grad)
    )
    sums = narrowed(jnp.sum(partials, axis=0))
    near, far = gather_groups(lax.axis_size("grp"))
    copies = jnp.broadcast_to(sums[None], (len(near[0]), *sums.shape))
    table = lax.all_to_all(copies, "grp", 0, 0, axis_index_groups=near)
    copies = jnp.broadcast_to(table[None], (len(far[0]), *table.shape))
    table = lax.all_to_all(copies, "grp", 0, 0, axis_index_groups=far)
    table = table.reshape(-1, *sums.shape)
    key_first_grad, value_first_grad = pl.pallas_call(
        short_kernel,
        grid=(halves,),
        out_shape=(wide, wide),
        in_specs=[inner_spec, full_spec, full_spec, short_spec],
        out_specs=(full_spec, full_spec),
        scratch_shapes=[pltpu.VMEM((row_count + RIM, LANES), jnp.float32)],
        compiler_params=params(),
        cost_estimate=cost(40 * row_count * chan_count, 5 * size),
        name="short_outputs",
    )(grad_inner_one, key_first, value_first, short_here)

    short_grad, medium_grad = pl.pallas_call(
        unpack_kernel,
        out_shape=(
            sds(short_filter.shape, jnp.float32),
            sds(medium_filter.shape, jnp.float32),
        ),
        compiler_params=params(),
        name="unpack",
    )(table)
    return (
        output_second,
        query_first_grad,
        key_first_grad,
        value_first_grad,
        query_second_grad,
        key_second_grad,
        short_grad,
        medium_grad,
    )


def solution(mesh):
    return jax.shard_map(
        per_device,
        mesh=mesh,
        in_specs=(
            *(P("seq", "grp"),) * 6,
            P(None, None),
            P(None, None),
        ),
        out_specs=(*(P("seq", "grp"),) * 6, P(None, None), P(None, None)),
        check_vma=False,
    )
```

time: 375 us -> 73.5 us (0.20)
  waiting for transfers between devices: 253 us -> 11.2 us
  local copies, waits for them, and re-layouts: 60.2 us -> 3.99 us
  other arithmetic: 33.7 us -> 0.01 us
  Pallas kernels: 0 us -> 28.3 us
  between operations: 14.5 us -> 0.7 us
  blocking collectives: 0 us -> 10.1 us
  starting transfers between devices: 10.6 us -> 18.8 us
    psum x1 -> x0, waiting for transfers between devices: 253 us -> none  [per_device(): lax.psum((short_table, medium_table), ('seq', 'grp'))]
    unnamed x76 -> x8, local copies, waits for them, and re-layouts: 33.3 us -> 1.35 us
    pallas_call x0 -> x5, Pallas kernels: none -> 28.3 us  [the longest x1 14.4 us: per_device(): pl.pallas_call(gradient_kernel, grid=(halves,), out_shape=(wide, wide, sd...]
    convert_element_type x6 -> x0, other arithmetic: 22 us -> none  [narrowed(): return array.astype(jnp.bfloat16)]
    all_to_all x0 -> x2, starting transfers between devices: none -> 15.8 us  [the longest x1 11.3 us: per_device(): partials = lax.all_to_all(parts, 'seq', 0, 0)]
    reshape x3 -> x0, local copies, waits for them, and re-layouts: 14.9 us -> none  [the longest x2 11.3 us: toeplitz_rows(): tiled[:, span:span + span * (3 * span - 1)]]
    all_to_all x0 -> x1, blocking collectives: none -> 10.1 us  [per_device(): table = lax.all_to_all(copies, 'grp', 0, 0, axis_index_groups=near)]
    ppermute x4 -> x2, starting transfers between devices: 10.5 us -> 3.02 us  [passed_along(): lax.ppermute(value, axis, [(source, source + steps) for source in range(f...]
  transfers between devices with their start and end apart: 5 -> 4, of which waited for: 1 -> 3; matrix products, arithmetic and copies ran while one was open for 16% -> 0% of each run, Pallas kernels for 0% -> 13%
where the time goes in v1:
time: 73.5 us; the launch traced here: 73.1 us
  Pallas kernels  28.3 us (39%)
  starting transfers between devices  18.8 us (26%)
  waiting for transfers between devices  11.2 us (15%)
  blocking collectives  10.1 us (14%)
  local copies, waits for them, and re-layouts  3.99 us (5%)
    pallas_call x1, Pallas kernels, per_device(): pl.pallas_call(gradient_kernel, grid=(halves,), out_shape=(wide, wide, sd...  14.4 us
    all_to_all x1, starting transfers between devices, per_device(): partials = lax.all_to_all(parts, 'seq', 0, 0)  11.3 us
    all_to_all x1, blocking collectives, per_device(): table = lax.all_to_all(copies, 'grp', 0, 0, axis_index_groups=near)  10.1 us
    pallas_call x1, Pallas kernels, per_device(): pl.pallas_call(medium_kernel, grid=(halves,), out_shape=(wide, wide), in_...  5.83 us
    ppermute x2, waiting for transfers between devices, passed_along(): lax.ppermute(value, axis, [(source, source + steps) for source in range(f...  5.1 us
    all_to_all x1, starting transfers between devices, per_device(): table = lax.all_to_all(copies, 'grp', 0, 0, axis_index_groups=far)  4.46 us
    pallas_call x1, Pallas kernels, per_device(): pl.pallas_call(short_kernel, grid=(halves,), out_shape=(wide, wide), in_s...  3.95 us
    all_to_all x1, waiting for transfers between devices, per_device(): partials = lax.all_to_all(parts, 'seq', 0, 0)  3.41 us
  transfers between devices with their start and end apart: 4, of which 3 were waited for; matrix products, arithmetic and copies ran while one was open for 0% of the time, Pallas kernels for 13%

profile of v1, /device:TPU:2, one launch (start us, length us, event | category | flops | bytes accessed | tf_op | source)
XLA Modules:
  0.0 73.1 jit_solution(635114701152393132)
XLA Ops:
  0.6 0.0 copy-start
  0.7 1.3 %constant_dynamic-slice_fusion.1.short_ref = bf16[7,256]{1,0:T(8,128)(2,1)} fusion(bf16[7,8192]{1,0:T(8,128)(2,1)} %param.14, s32[]{:T(128)S(6)} %select_n.6), kind=kLoop, calls=%fused_computation.1 | loop fusion | bytes 7172 | tf_op jit(solution)/shard_map/dynamic_slice | solution.py:275
  2.0 0.0 copy-done
  2.0 0.6 constant_dynamic-slice_fusion.medium_ref
  2.6 2.3 %rims.1 = (bf16[144,256]{1,0:T(8,128)(2,1)}, bf16[144,256]{1,0:T(8,128)(2,1)}) custom-call(bf16[2048,256]{1,0:T(8,128)(2,1)} %key_ref.3, bf16[2048,256]{1,0:T(8,128)(2,1)} %value_ref.3, bf16[2048,256]{1,0:T(8,128)(2,1)} %query_ref.1, bf16[2048,256]{1,0:T(8,128)(2,1)} %key_two_ref.1, bf16[2048,256]{1,0:T(8,128)(2,1)} %cotangent_ref.3, ...), custom_call_target="tpu_custom_call" | custom-call | flops 12582912 | bytes 1048576 | tf_op jit(solution)/shard_map/rims/pallas_call | solution.py:287
  4.9 1.7 %collective-permute-start = (bf16[144,256]{1,0:T(8,128)(2,1)}, bf16[144,256]{1,0:T(8,128)(2,1)S(1)}, u32[]{:S(2)}, u32[]{:S(2)}) collective-permute-start(bf16[144,256]{1,0:T(8,128)(2,1)} %get-tuple-element.24), channel_id=1, source_target_pairs={{0,32},{32,64},{64,96},{96,128},{128,160},{160,192},{192,224},{1,3... | collective-permute-start | bytes 221192 | tf_op jit(solution)/shard_map/ppermute | solution.py:32
  6.6 1.3 %collective-permute-start.1 = (bf16[144,256]{1,0:T(8,128)(2,1)}, bf16[144,256]{1,0:T(8,128)(2,1)S(1)}, u32[]{:S(2)}, u32[]{:S(2)}) collective-permute-start(bf16[144,256]{1,0:T(8,128)(2,1)} %get-tuple-element.25), channel_id=1, source_target_pairs={{32,0},{64,32},{96,64},{128,96},{160,128},{192,160},{224,192},{33,... | collective-permute-start | bytes 221192 | tf_op jit(solution)/shard_map/ppermute | solution.py:32
  7.9 0.0 collective-permute-done.tail_ref
  7.9 0.0 copy-start.2
  7.9 5.1 %collective-permute-done.1.head_ref = bf16[144,256]{1,0:T(8,128)(2,1)S(1)} collective-permute-done((bf16[144,256]{1,0:T(8,128)(2,1)}, bf16[144,256]{1,0:T(8,128)(2,1)S(1)}, u32[]{:S(2)}, u32[]{:S(2)}) %collective-permute-start.1) | collective-permute-done | bytes 73760 | tf_op jit(solution)/shard_map/ppermute | solution.py:32
  13.0 0.0 copy-done.2
  13.0 0.0 copy-start.3
  13.0 0.6 copy-done.3
  13.7 14.4 %gradients.1 = (bf16[2048,256]{1,0:T(8,128)(2,1)}, bf16[2048,256]{1,0:T(8,128)(2,1)}, bf16[16,272,128]{2,1,0:T(8,128)(2,1)}, bf16[2064,256]{1,0:T(8,128)(2,1)}, f32[8,16,256]{2,1,0:T(8,128)}) custom-call(bf16[2048,256]{1,0:T(8,128)(2,1)} %query_ref.1, bf16[2048,256]{1,0:T(8,128)(2,1)} %key_ref.3, bf16[2048,256]{1,0:T(8,128)(2,1)} %value_ref.3, ...), custom_call_target="tpu_custom_call" | custom-call | flops 52428800 | bytes 10485760 | tf_op jit(solution)/shard_map/gradients/pallas_call | solution.py:319
  28.1 11.3 %all-to-all-start = ((f32[8,16,256]{2,1,0:T(8,128)}), f32[8,16,256]{2,1,0:T(8,128)S(1)}, u32[]{:S(2)}, u32[]{:S(2)}) async-start(f32[8,16,256]{2,1,0:T(8,128)} %get-tuple-element.26), calls=%async_computation | async-start | bytes 262144 | tf_op jit(solution)/shard_map/all_to_all | solution.py:346
  39.4 5.8 %medium_outputs.1 = (bf16[2048,256]{1,0:T(8,128)(2,1)}, bf16[2048,256]{1,0:T(8,128)(2,1)}) custom-call(bf16[16,272,128]{2,1,0:T(8,128)(2,1)} %get-tuple-element.27.product_ref, bf16[2048,256]{1,0:T(8,128)(2,1)} %query_two_ref.3, bf16[2048,256]{1,0:T(8,128)(2,1)} %cotangent_ref.3, bf16[16,128]{1,0:T(8,128)(2,1)} %constant_dynamic-slice_fusion.medium_ref), custom_call_target="tpu_custom_call" | custom-call | flops 20971520 | bytes 5242880 | tf_op jit(solution)/shard_map/medium_outputs/pallas_call | solution.py:348
  45.2 3.4 %all-to-all-done = f32[8,16,256]{2,1,0:T(8,128)S(1)} async-done(((f32[8,16,256]{2,1,0:T(8,128)}), f32[8,16,256]{2,1,0:T(8,128)S(1)}, u32[]{:S(2)}, u32[]{:S(2)}) %all-to-all-start) | async-done | bytes 131104 | tf_op jit(solution)/shard_map/all_to_all | solution.py:346
  48.6 10.1 %all_to_all.15 = bf16[8,16,256]{2,1,0:T(8,128)(2,1)S(1)} all-to-all(bf16[8,16,256]{2,1,0:T(8,128)(2,1)S(1)} %broadcast_in_dim.4), channel_id=1, replica_groups={{0,1,2,3,4,5,6,7},{8,9,10,11,12,13,14,15},{16,17,18,19,20,21,22,23},{24..., dimensions={0} | all-to-all | bytes 131072 | tf_op jit(solution)/shard_map/all_to_all | solution.py:365
  58.7 0.7 broadcast_in_dim.5
  59.5 4.5 %all-to-all-start.2 = ((bf16[4,8,16,256]{3,2,1,0:T(8,128)(2,1)}), bf16[4,8,16,256]{3,2,1,0:T(8,128)(2,1)S(1)}, u32[]{:S(2)}, u32[]{:S(2)}) async-start(bf16[4,8,16,256]{3,2,1,0:T(8,128)(2,1)} %broadcast_in_dim.5), calls=%async_computation.2 | async-start | bytes 524288 | tf_op jit(solution)/shard_map/all_to_all | solution.py:367
  63.9 4.0 %short_outputs.1 = (bf16[2048,256]{1,0:T(8,128)(2,1)}, bf16[2048,256]{1,0:T(8,128)(2,1)}) custom-call(bf16[2064,256]{1,0:T(8,128)(2,1)} %get-tuple-element.32.grad_inner_ref, bf16[2048,256]{1,0:T(8,128)(2,1)} %key_ref.3, bf16[2048,256]{1,0:T(8,128)(2,1)} %value_ref.3, bf16[7,256]{1,0:T(8,128)(2,1)} %constant_dynamic-slice_fusion.1.short_ref), custom_call_target="tpu_custom_call" | custom-call | flops 20971520 | bytes 5242880 | tf_op jit(solution)/shard_map/short_outputs/pallas_call | solution.py:369
  67.9 2.7 %all-to-all-done.2 = bf16[4,8,16,256]{3,2,1,0:T(8,128)(2,1)S(1)} async-done(((bf16[4,8,16,256]{3,2,1,0:T(8,128)(2,1)}), bf16[4,8,16,256]{3,2,1,0:T(8,128)(2,1)S(1)}, u32[]{:S(2)}, u32[]{:S(2)}) %all-to-all-start.2) | async-done | bytes 262176 | tf_op jit(solution)/shard_map/all_to_all | solution.py:367
  70.6 0.0 copy-start.1
  70.6 0.7 copy-done.1
  71.3 1.8 %unpack.1 = (f32[7,8192]{1,0:T(8,128)}, f32[512,128]{1,0:T(8,128)}) custom-call(bf16[32,16,256]{2,1,0:T(8,128)(2,1)} %bitcast.1), custom_call_target="tpu_custom_call" | custom-call | tf_op jit(solution)/shard_map/unpack/pallas_call | solution.py:381
  (2 shorter events, 0.0 us)
Async XLA Ops:
  0.6 1.3 %copy-start = (bf16[512,128]{1,0:T(8,128)(2,1)S(1)}, bf16[512,128]{1,0:T(8,128)(2,1)}, u32[]{:S(2)}) copy-start(bf16[512,128]{1,0:T(8,128)(2,1)} %param.15) | copy-start | bytes 393220
  4.9 3.0 %collective-permute-start = (bf16[144,256]{1,0:T(8,128)(2,1)}, bf16[144,256]{1,0:T(8,128)(2,1)S(1)}, u32[]{:S(2)}, u32[]{:S(2)}) collective-permute-start(bf16[144,256]{1,0:T(8,128)(2,1)} %get-tuple-element.24), channel_id=1, source_target_pairs={{0,32},{32,64},{64,96},{96,128},{128,160},{160,192},{192,224},{1,3... | collective-permute-start | bytes 221192 | tf_op jit(solution)/shard_map/ppermute | solution.py:32
  6.6 6.4 %collective-permute-start.1 = (bf16[144,256]{1,0:T(8,128)(2,1)}, bf16[144,256]{1,0:T(8,128)(2,1)S(1)}, u32[]{:S(2)}, u32[]{:S(2)}) collective-permute-start(bf16[144,256]{1,0:T(8,128)(2,1)} %get-tuple-element.25), channel_id=1, source_target_pairs={{32,0},{64,32},{96,64},{128,96},{160,128},{192,160},{224,192},{33,... | collective-permute-start | bytes 221192 | tf_op jit(solution)/shard_map/ppermute | solution.py:32
  7.9 5.1 %copy-start.2 = (bf16[144,256]{1,0:T(8,128)(2,1)}, bf16[144,256]{1,0:T(8,128)(2,1)S(1)}, u32[]{:S(2)}) copy-start(bf16[144,256]{1,0:T(8,128)(2,1)S(1)} %collective-permute-done.tail_ref) | copy-start | bytes 221188
  13.0 0.6 copy-start.3
  28.1 20.5 %all-to-all-start = ((f32[8,16,256]{2,1,0:T(8,128)}), f32[8,16,256]{2,1,0:T(8,128)S(1)}, u32[]{:S(2)}, u32[]{:S(2)}) async-start(f32[8,16,256]{2,1,0:T(8,128)} %get-tuple-element.26), calls=%async_computation | async-start | bytes 262144 | tf_op jit(solution)/shard_map/all_to_all | solution.py:346
  59.5 11.1 %all-to-all-start.2 = ((bf16[4,8,16,256]{3,2,1,0:T(8,128)(2,1)}), bf16[4,8,16,256]{3,2,1,0:T(8,128)(2,1)S(1)}, u32[]{:S(2)}, u32[]{:S(2)}) async-start(bf16[4,8,16,256]{3,2,1,0:T(8,128)(2,1)} %broadcast_in_dim.5), calls=%async_computation.2 | async-start | bytes 524288 | tf_op jit(solution)/shard_map/all_to_all | solution.py:367
  70.6 0.7 copy-start.1

commit v2 on v1

v2 whole, which is shorter than its diff:
```python
import functools
import math

import jax
import jax.numpy as jnp
from jax import lax
from jax.experimental import pallas as pl
from jax.experimental.pallas import tpu as pltpu
from jax.sharding import PartitionSpec as P

GROUP = 16
SE_TAPS = 7
MR_TAPS = 128
BLOCK = 128
LANES = 128
RIM = 8
CHUNK = 256
HALO = 16
VMEM_LIMIT = 63 * 1024 * 1024


def widened(array):
    return array.astype(jnp.float32)


def narrowed(array):
    return array.astype(jnp.bfloat16)


def passed_along(value, axis, steps):
    count = lax.axis_size(axis)
    first, last = (max(0, -steps), min(count, count - steps))
    return lax.ppermute(value, axis, [(source, source + steps) for source in range(first, last)])


def rows_of(index, count):
    return pl.ds(pl.multiple_of(index * count, count), count)


def short_causal(prior, here, taps):
    ext = jnp.concatenate([prior, here], axis=0)
    total = taps[0:1] * here
    for shift_by in range(1, SE_TAPS):
        total += taps[shift_by : shift_by + 1] * pltpu.roll(ext, shift_by, 0)[RIM:]
    return total


def upper_lower(coefs):
    line = jnp.concatenate([coefs, jnp.zeros_like(coefs)], axis=1)
    table = jnp.broadcast_to(line, (BLOCK, 2 * BLOCK))
    return narrowed(pltpu.roll(table, 0, 1, stride=1, stride_axis=0))


def dotted(left, right, dims):
    return lax.dot_general(left, right, (dims, ((), ())), preferred_element_type=jnp.float32)


def identity(count):
    row = lax.broadcasted_iota(jnp.int32, (count, count), 0)
    lane = lax.broadcasted_iota(jnp.int32, (count, count), 1)
    return narrowed(widened(row == lane))


def turned(tile, unit):
    flat = narrowed(dotted(unit, tile, ((1,), (1,))))
    return flat.reshape(tile.shape[1] // GROUP, GROUP, tile.shape[0])


def rims_kernel(
    place_ref,
    key_tail, value_tail, query_tail, key_two_tail,
    cotangent_head, query_two_head, query_head, key_two_head,
    short_ref, medium_ref, tail_ref, head_ref,
):
    taps = widened(short_ref[...])
    start = 2 * BLOCK - BLOCK - HALO
    product_one = widened(key_tail[start:]) * widened(value_tail[start:])
    inner_one = short_causal(product_one[RIM:HALO], product_one[HALO:], taps)
    product_two = widened(key_two_tail[BLOCK:]) * (widened(query_tail[BLOCK:]) * inner_one)
    tail_ref[:HALO] = narrowed(product_one[BLOCK:])
    tail_ref[HALO:] = narrowed(product_two)
    grad_inner = narrowed(
        widened(cotangent_head[: BLOCK + HALO]) * widened(query_two_head[: BLOCK + HALO])
    )
    head_ref[:BLOCK] = grad_inner[:BLOCK]
    wide = widened(grad_inner)
    chan_count = wide.shape[1]
    group_count = chan_count // GROUP
    owner = lax.broadcasted_iota(jnp.int32, (group_count, chan_count), 1) // GROUP
    spread = narrowed(widened(owner == lax.broadcasted_iota(jnp.int32, owner.shape, 0)))
    coefs = dotted(widened(medium_ref[...]).T, widened(spread), ((1,), (0,)))
    row = lax.broadcasted_iota(jnp.int32, (HALO, chan_count), 0)
    grad_product = jnp.zeros((HALO, chan_count), jnp.float32)
    for shift_by in range(SE_TAPS - 1):
        moved = wide[:BLOCK]
        if shift_by:
            moved = pltpu.roll(wide, BLOCK + HALO - shift_by, 0)[:BLOCK]
        line = jnp.sum(coefs * moved, axis=0, keepdims=True)
        grad_product = jnp.where(row == shift_by, line, grad_product)
    head_ref[BLOCK:] = narrowed(
        grad_product * widened(key_two_head[...]) * widened(query_head[...])
    )


def main_kernel(
    place_ref,
    query_any, key_any, value_any, query_two_any, key_two_any, cotangent_any,
    short_ref, medium_ref, tail_ref, head_ref,
    output_any, query_grad_any, key_grad_any, value_grad_any, query_two_grad_any, key_two_grad_any,
    parts_ref,
    query_ref, key_ref, value_ref, query_two_ref, key_two_ref, cotangent_ref,
    output_ref, query_grad_ref, key_grad_ref, value_grad_ref, query_two_grad_ref, key_two_grad_ref,
    inner_ref, gated_ref, first_ref, later_ref, pair_ref, product_ref, turned_ref, back_ref, ahead_ref,
    sums_ref, in_sems, out_sems,
):
    row_count, chan_count = query_ref.shape
    group_count = chan_count // GROUP
    chunk_count = row_count // CHUNK
    span = row_count // BLOCK * GROUP
    halves = chan_count // LANES
    steps = CHUNK // BLOCK
    taps = widened(short_ref[...])
    sequence_total = row_count * lax.axis_size("seq")
    sources = (key_any, value_any, query_any, key_two_any, cotangent_any, query_two_any)
    buffers = (key_ref, value_ref, query_ref, key_two_ref, cotangent_ref, query_two_ref)
    results = (
        output_ref, query_grad_ref, key_grad_ref, value_grad_ref, query_two_grad_ref, key_two_grad_ref
    )
    targets = (
        output_any, query_grad_any, key_grad_any, value_grad_any, query_two_grad_any, key_two_grad_any
    )

    def copies_in(chunk):
        rows = rows_of(chunk, CHUNK)
        return [
            pltpu.make_async_copy(source.at[rows], buffer.at[rows], in_sems.at[place, chunk])
            for place, (source, buffer) in enumerate(zip(sources, buffers))
        ]

    def copies_out(chunk):
        rows = rows_of(chunk, CHUNK)
        return [
            pltpu.make_async_copy(result.at[rows], target.at[rows], out_sems.at[place, chunk])
            for place, (result, target) in enumerate(zip(results, targets))
        ]

    def start_in(chunk, _):
        for copy in copies_in(chunk):
            copy.start()
        return 0

    lax.fori_loop(0, chunk_count, start_in, 0)

    unit = identity(chan_count)
    small_unit = unit[:BLOCK, :BLOCK]
    product_ref[:, :GROUP, :] = turned(tail_ref[HALO:], unit)
    turned_ref[:, span:, :] = turned(head_ref[:BLOCK], unit)
    for half in range(halves):
        lanes = slice(half * LANES, (half + 1) * LANES)
        first_ref[half, :RIM] = widened(tail_ref[:HALO, lanes])[RIM:]
        later_ref[half, row_count:] = widened(head_ref[BLOCK:, lanes])[:RIM]

    def forward(chunk, _):
        for copy in copies_in(chunk):
            copy.wait()
        for step in range(steps):
            index = chunk * steps + step
            rows = rows_of(index, BLOCK)
            local = slice(step * BLOCK, (step + 1) * BLOCK)
            for half in range(halves):
                lanes = slice(half * LANES, (half + 1) * LANES)
                product_one = widened(key_ref[rows, lanes] * value_ref[rows, lanes])
                first_ref[half, pl.ds(pl.multiple_of(index * BLOCK + RIM, RIM), BLOCK)] = product_one
                inner_one = taps[0:1, lanes] * product_one
                for shift_by in range(1, SE_TAPS):
                    inner_one += (
                        taps[shift_by : shift_by + 1, lanes]
                        * first_ref[half, pl.ds(index * BLOCK + RIM - shift_by, BLOCK)]
                    )
                inner_one = narrowed(inner_one)
                gated = query_ref[rows, lanes] * inner_one
                inner_ref[rows, lanes] = inner_one
                gated_ref[rows, lanes] = gated
                pair_ref[0, local, lanes] = key_two_ref[rows, lanes] * gated
                pair_ref[1, local, lanes] = cotangent_ref[rows, lanes] * query_two_ref[rows, lanes]
        product_two = turned(pair_ref[0], unit)
        grad_inner_two = turned(pair_ref[1], unit)
        for step in range(steps):
            index = chunk * steps + step
            local = slice(step * BLOCK, (step + 1) * BLOCK)
            product_ref[:, rows_of(index + 1, GROUP), :] = product_two[:, :, local]
            turned_ref[:, rows_of(index, GROUP), :] = grad_inner_two[:, :, local]
        return 0

    lax.fori_loop(0, chunk_count, forward, 0)

    flip_row = lax.broadcasted_iota(jnp.int32, (BLOCK, BLOCK), 0)
    flip_lane = lax.broadcasted_iota(jnp.int32, (BLOCK, BLOCK), 1)
    flip = narrowed(widened(flip_row + flip_lane == BLOCK - 1))
    medium_scale = 1.0 / math.sqrt(sequence_total * GROUP)
    for group in range(group_count):
        bands = upper_lower(widened(medium_ref[group : group + 1]))
        window = jnp.concatenate(
            [turned_ref[group, :span], turned_ref[group, GROUP : GROUP + span]], axis=1
        )
        back_ref[group] = narrowed(dotted(window, bands, ((1,), (1,))))
        earlier = jnp.concatenate([product_ref[group, :span], product_ref[group, GROUP:]], axis=1)
        causal = jnp.concatenate([bands[:, BLOCK:], bands[:, :BLOCK]], axis=0)
        ahead_ref[group] = narrowed(dotted(earlier, causal, ((1,), (0,))))
        flipped = narrowed(dotted(flip, product_ref[group, GROUP:], ((1,), (1,))))
        pairs = dotted(flipped, window, ((1,), (0,)))
        pairs = pltpu.roll(pairs, BLOCK + 1, 1, stride=1, stride_axis=0)
        line = jnp.sum(pairs[:, :BLOCK], axis=0, keepdims=True) * medium_scale
        half, row = group * GROUP // LANES, RIM + group % (LANES // GROUP)
        parts_ref[:, row : row + 1, half * LANES : (half + 1) * LANES] = jnp.broadcast_to(
            line[None], (parts_ref.shape[0], 1, LANES)
        )

    sums_ref[...] = jnp.zeros_like(sums_ref)

    def backward(turn, _):
        chunk = chunk_count - 1 - turn
        for step in reversed(range(steps)):
            index = chunk * steps + step
            rows = rows_of(index, BLOCK)
            lines = rows_of(index, GROUP)
            back = back_ref[:, lines, :].reshape(chan_count, BLOCK)
            ahead = ahead_ref[:, lines, :].reshape(chan_count, BLOCK)
            back = narrowed(dotted(small_unit, back, ((1,), (1,))))
            ahead = narrowed(dotted(small_unit, ahead, ((1,), (1,))))
            output_ref[rows] = query_two_ref[rows] * ahead
            query_two_grad_ref[rows] = cotangent_ref[rows] * ahead
            key_two_grad_ref[rows] = back * gated_ref[rows]
            grad_gated = back * key_two_ref[rows]
            query_grad_ref[rows] = grad_gated * inner_ref[rows]
            grad_inner = widened(grad_gated * query_ref[rows])
            for half in range(halves):
                lanes = slice(half * LANES, (half + 1) * LANES)
                here = grad_inner[:, lanes]
                later_ref[half, rows] = here
                product_one = first_ref[half, pl.ds(pl.multiple_of(index * BLOCK + RIM, RIM), BLOCK)]
                total = jnp.zeros_like(here)
                for shift_by in range(SE_TAPS):
                    moved = here
                    if shift_by:
                        moved = later_ref[half, pl.ds(index * BLOCK + shift_by, BLOCK)]
                    total += taps[shift_by : shift_by + 1, lanes] * moved
                    sums_ref[half, shift_by] += jnp.sum(
                        (product_one * moved).reshape(BLOCK // RIM, RIM, LANES), axis=0
                    )
                total = narrowed(total)
                key_grad_ref[rows, lanes] = total * value_ref[rows, lanes]
                value_grad_ref[rows, lanes] = total * key_ref[rows, lanes]
        for copy in copies_out(chunk):
            copy.start()
        return 0

    lax.fori_loop(0, chunk_count, backward, 0)

    short_scale = 1.0 / math.sqrt(sequence_total)
    for half in range(halves):
        lines = [
            jnp.sum(sums_ref[half, shift_by], axis=0, keepdims=True) * short_scale
            for shift_by in range(SE_TAPS)
        ]
        lines = jnp.concatenate(lines + [jnp.zeros_like(lines[0])], axis=0)
        parts_ref[:, :RIM, half * LANES : (half + 1) * LANES] = jnp.broadcast_to(
            lines[None], (parts_ref.shape[0], RIM, LANES)
        )

    def wait_out(chunk, _):
        for copy in copies_out(chunk):
            copy.wait()
        return 0

    lax.fori_loop(0, chunk_count, wait_out, 0)


def unpack_kernel(table_ref, short_ref, medium_ref):
    chan_count = table_ref.shape[2]
    groups = LANES // GROUP
    for place in range(table_ref.shape[0]):
        piece = widened(table_ref[place])
        short_ref[:, place * chan_count : (place + 1) * chan_count] = piece[:SE_TAPS]
        for half in range(chan_count // LANES):
            first = (place * (chan_count // LANES) + half) * groups
            medium_ref[first : first + groups] = piece[RIM:, half * LANES : (half + 1) * LANES]


def params():
    return pltpu.CompilerParams(vmem_limit_bytes=VMEM_LIMIT)


def cost(flops, size):
    return pl.CostEstimate(flops=flops, bytes_accessed=size, transcendentals=0)


def per_device(
    query_first,
    key_first,
    value_first,
    query_second,
    key_second,
    cotangent,
    short_filter,
    medium_filter,
):
    row_count, chan_count = query_first.shape
    group_count = chan_count // GROUP
    place = lax.axis_index("grp").astype(jnp.int32).reshape(1)
    sds = jax.ShapeDtypeStruct
    wide = sds((row_count, chan_count), jnp.bfloat16)
    size = row_count * chan_count * 2

    last = row_count // (2 * BLOCK) - 1
    tail_spec = pl.BlockSpec((2 * BLOCK, chan_count), lambda i, at: (last, 0))
    head_spec = pl.BlockSpec((2 * BLOCK, chan_count), lambda i, at: (0, 0))
    rim_spec = pl.BlockSpec((HALO, chan_count), lambda i, at: (0, 0))
    halo_spec = pl.BlockSpec((HALO + BLOCK, chan_count), lambda i, at: (0, 0))
    short_spec = pl.BlockSpec((SE_TAPS, chan_count), lambda i, at: (0, at[0]))
    medium_spec = pl.BlockSpec((group_count, MR_TAPS), lambda i, at: (at[0], 0))
    halo = sds((HALO + BLOCK, chan_count), jnp.bfloat16)
    tail, head = pl.pallas_call(
        rims_kernel,
        grid_spec=pltpu.PrefetchScalarGridSpec(
            num_scalar_prefetch=1,
            grid=(1,),
            in_specs=[tail_spec] * 4 + [head_spec] * 2 + [rim_spec] * 2 + [short_spec, medium_spec],
            out_specs=(halo_spec, halo_spec),
        ),
        out_shape=(halo, halo),
        compiler_params=params(),
        cost_estimate=cost(2 * 6 * 2 * BLOCK * chan_count * 16, size),
        name="rims",
    )(
        place,
        key_first, value_first, query_first, key_second,
        cotangent, query_second, query_first, key_second,
        short_filter, medium_filter,
    )
    tail = passed_along(tail, "seq", 1)
    head = passed_along(head, "seq", -1)

    any_spec = pl.BlockSpec(memory_space=pl.ANY)
    seq_count = lax.axis_size("seq")
    lines = (row_count // BLOCK + 1) * GROUP
    halves = chan_count // LANES
    stream = pltpu.VMEM((row_count, chan_count), jnp.bfloat16)
    turned_stream = pltpu.VMEM((group_count, lines, BLOCK), jnp.bfloat16)
    results = pl.pallas_call(
        main_kernel,
        grid_spec=pltpu.PrefetchScalarGridSpec(
            num_scalar_prefetch=1,
            grid=(1,),
            in_specs=[any_spec] * 6 + [short_spec, medium_spec, halo_spec, halo_spec],
            out_specs=(any_spec,) * 6
            + (pl.BlockSpec((seq_count, 2 * RIM, chan_count), lambda i, at: (0, 0, 0)),),
            scratch_shapes=[stream] * 14
            + [pltpu.VMEM((halves, row_count + RIM, LANES), jnp.float32)] * 2
            + [pltpu.VMEM((2, CHUNK, chan_count), jnp.bfloat16)]
            + [turned_stream] * 2
            + [pltpu.VMEM((group_count, lines - GROUP, BLOCK), jnp.bfloat16)] * 2
            + [pltpu.VMEM((halves, SE_TAPS, RIM, LANES), jnp.float32)]
            + [pltpu.SemaphoreType.DMA((6, row_count // CHUNK))] * 2,
        ),
        out_shape=(wide,) * 6 + (sds((seq_count, 2 * RIM, chan_count), jnp.float32),),
        compiler_params=params(),
        cost_estimate=cost(100 * row_count * chan_count, 12 * size),
        name="main",
    )(
        place,
        query_first, key_first, value_first, query_second, key_second, cotangent,
        short_filter, medium_filter, tail, head,
    )
    (
        output_second,
        query_first_grad,
        key_first_grad,
        value_first_grad,
        query_second_grad,
        key_second_grad,
        parts,
    ) = results

    sums = narrowed(jnp.sum(lax.all_to_all(parts, "seq", 0, 0), axis=0))
    copies = jnp.broadcast_to(sums[None], (lax.axis_size("grp"), *sums.shape))
    table = lax.all_to_all(copies, "grp", 0, 0)
    short_grad, medium_grad = pl.pallas_call(
        unpack_kernel,
        out_shape=(
            sds(short_filter.shape, jnp.float32),
            sds(medium_filter.shape, jnp.float32),
        ),
        compiler_params=params(),
        name="unpack",
    )(table)
    return (
        output_second,
        query_first_grad,
        key_first_grad,
        value_first_grad,
        query_second_grad,
        key_second_grad,
        short_grad,
        medium_grad,
    )


def solution(mesh):
    return jax.shard_map(
        per_device,
        mesh=mesh,
        in_specs=(
            *(P("seq", "grp"),) * 6,
            P(None, None),
            P(None, None),
        ),
        out_specs=(*(P("seq", "grp"),) * 6, P(None, None), P(None, None)),
        check_vma=False,
    )
```

time: 73.5 us -> 65.5 us (0.89)
  blocking collectives: 10.1 us -> 36.9 us
  starting transfers between devices: 18.8 us -> 3.02 us
  Pallas kernels: 28.3 us -> 18.8 us
  waiting for transfers between devices: 11.2 us -> 5.11 us
  local copies, waits for them, and re-layouts: 3.99 us -> 0.66 us
    all_to_all x1 -> x2, blocking collectives: 10.1 us -> 36.9 us  [the longest x1 20.5 us: per_device(): sums = narrowed(jnp.sum(lax.all_to_all(parts, 'seq', 0, 0), axis=0))]
    all_to_all x2 -> x0, starting transfers between devices: 15.8 us -> none  [the longest x1 11.3 us: per_device(): partials = lax.all_to_all(parts, 'seq', 0, 0)]
    pallas_call x4 -> x2, Pallas kernels: 26.5 us -> 17 us  [the longest x1 14.7 us: per_device(): pl.pallas_call(main_kernel, grid_spec=pltpu.PrefetchScalarGridSpec(num_sc...]
    all_to_all x2 -> x0, waiting for transfers between devices: 6.14 us -> none  [the longest x1 3.41 us: per_device(): partials = lax.all_to_all(parts, 'seq', 0, 0)]
    dynamic_slice x2 -> x0, local copies, waits for them, and re-layouts: 1.91 us -> none  [the longest x1 1.32 us: per_device(): lax.dynamic_slice_in_dim(short_filter, group_index * chan_count, chan_cou...]
  transfers between devices with their start and end apart: 4 -> 2, of which waited for: 3 -> 1; matrix products, arithmetic and copies ran while one was open for 0% -> 0% of each run, Pallas kernels for 13% -> 0%
where the time goes in v2:
time: 65.5 us; the launch traced here: 65.1 us
  blocking collectives  36.9 us (56%)
  Pallas kernels  18.8 us (29%)
  waiting for transfers between devices  5.11 us (8%)
  starting transfers between devices  3.02 us (5%)
  between operations  0.69 us (1%)
  local copies, waits for them, and re-layouts  0.66 us (1%)
    all_to_all x1, blocking collectives, per_device(): sums = narrowed(jnp.sum(lax.all_to_all(parts, 'seq', 0, 0), axis=0))  20.5 us
    all_to_all x1, blocking collectives, per_device(): table = lax.all_to_all(copies, 'grp', 0, 0)  16.3 us
    pallas_call x1, Pallas kernels, per_device(): pl.pallas_call(main_kernel, grid_spec=pltpu.PrefetchScalarGridSpec(num_sc...  14.7 us
    ppermute x2, waiting for transfers between devices, passed_along(): lax.ppermute(value, axis, [(source, source + steps) for source in range(f...  5.11 us
    ppermute x2, starting transfers between devices, passed_along(): lax.ppermute(value, axis, [(source, source + steps) for source in range(f...  3.02 us
    pallas_call x1, Pallas kernels, per_device(): pl.pallas_call(rims_kernel, grid_spec=pltpu.PrefetchScalarGridSpec(num_sc...  2.3 us
    pallas_call x1, Pallas kernels, per_device(): pl.pallas_call(unpack_kernel, out_shape=(sds(short_filter.shape, jnp.floa...  1.77 us
  transfers between devices with their start and end apart: 2, of which 1 were waited for; matrix products, arithmetic and copies ran while one was open for 0% of the time, Pallas kernels for 0%

profile of v2, /device:TPU:2, one launch (start us, length us, event | category | flops | bytes accessed | tf_op | source)
XLA Modules:
  0.0 65.1 jit_solution(5659862020440056239)
XLA Ops:
  0.6 2.3 %rims.1 = (bf16[144,256]{1,0:T(8,128)(2,1)}, bf16[144,256]{1,0:T(8,128)(2,1)}) custom-call(s32[1]{0:T(128)} %bitcast.place_ref, bf16[2048,256]{1,0:T(8,128)(2,1)} %key_any.1, bf16[2048,256]{1,0:T(8,128)(2,1)} %value_any.1, bf16[2048,256]{1,0:T(8,128)(2,1)} %query_any.1, bf16[2048,256]{1,0:T(8,128)(2,1)} %key_two_any.1, bf16[2048,256]{1,0:T(8,128)(2,1)} %cotangent_any.1, ...), custom_call_target="tpu_custom_call" | custom-call | flops 12582912 | bytes 1048576 | tf_op jit(solution)/shard_map/rims/pallas_call | solution.py:323
  2.9 1.7 %collective-permute-start = (bf16[144,256]{1,0:T(8,128)(2,1)}, bf16[144,256]{1,0:T(8,128)(2,1)S(1)}, u32[]{:S(2)}, u32[]{:S(2)}) collective-permute-start(bf16[144,256]{1,0:T(8,128)(2,1)} %get-tuple-element.19), channel_id=1, source_target_pairs={{0,32},{32,64},{64,96},{96,128},{128,160},{160,192},{192,224},{1,3... | collective-permute-start | bytes 221192 | tf_op jit(solution)/shard_map/ppermute | solution.py:33
  4.7 1.3 %collective-permute-start.1 = (bf16[144,256]{1,0:T(8,128)(2,1)}, bf16[144,256]{1,0:T(8,128)(2,1)S(1)}, u32[]{:S(2)}, u32[]{:S(2)}) collective-permute-start(bf16[144,256]{1,0:T(8,128)(2,1)} %get-tuple-element.20), channel_id=1, source_target_pairs={{32,0},{64,32},{96,64},{128,96},{160,128},{192,160},{224,192},{33,... | collective-permute-start | bytes 221192 | tf_op jit(solution)/shard_map/ppermute | solution.py:33
  6.0 0.0 collective-permute-done.tail_ref
  6.0 0.0 copy-start
  6.0 5.1 %collective-permute-done.1.head_ref = bf16[144,256]{1,0:T(8,128)(2,1)S(1)} collective-permute-done((bf16[144,256]{1,0:T(8,128)(2,1)}, bf16[144,256]{1,0:T(8,128)(2,1)S(1)}, u32[]{:S(2)}, u32[]{:S(2)}) %collective-permute-start.1) | collective-permute-done | bytes 73760 | tf_op jit(solution)/shard_map/ppermute | solution.py:33
  11.1 0.0 copy-done
  11.1 0.0 copy-start.1
  11.1 0.6 copy-done.1
  11.7 14.7 %main.1 = (bf16[2048,256]{1,0:T(8,128)(2,1)}, bf16[2048,256]{1,0:T(8,128)(2,1)}, bf16[2048,256]{1,0:T(8,128)(2,1)}, bf16[2048,256]{1,0:T(8,128)(2,1)}, bf16[2048...) custom-call(s32[1]{0:T(128)} %bitcast.place_ref, bf16[2048,256]{1,0:T(8,128)(2,1)} %query_any.1, ...), custom_call_target="tpu_custom_call" | custom-call | flops 52428800 | bytes 12582912 | tf_op jit(solution)/shard_map/main/pallas_call | solution.py:350
  26.4 20.5 %all_to_all.10 = f32[8,16,256]{2,1,0:T(8,128)S(1)} all-to-all(f32[8,16,256]{2,1,0:T(8,128)} %get-tuple-element.27), channel_id=1, replica_groups=mesh['seq'=8,'grp'=32] {'seq'}, dimensions={0} | all-to-all | bytes 262144 | tf_op jit(solution)/shard_map/all_to_all | solution.py:385
  47.0 16.3 %all_to_all.11.table_ref = bf16[32,16,256]{2,1,0:T(8,128)(2,1)} all-to-all(bf16[32,16,256]{2,1,0:T(8,128)(2,1)S(1)} %broadcast_in_dim.2), channel_id=1, replica_groups=mesh['seq'=8,'grp'=32] {'grp'}, dimensions={0} | all-to-all | bytes 524288 | tf_op jit(solution)/shard_map/all_to_all | solution.py:387
  63.3 1.8 %unpack.1 = (f32[7,8192]{1,0:T(8,128)}, f32[512,128]{1,0:T(8,128)}) custom-call(bf16[32,16,256]{2,1,0:T(8,128)(2,1)} %all_to_all.11.table_ref), custom_call_target="tpu_custom_call" | custom-call | tf_op jit(solution)/shard_map/unpack/pallas_call | solution.py:388
  (2 shorter events, 0.0 us)
Async XLA Ops:
  2.9 3.0 %collective-permute-start = (bf16[144,256]{1,0:T(8,128)(2,1)}, bf16[144,256]{1,0:T(8,128)(2,1)S(1)}, u32[]{:S(2)}, u32[]{:S(2)}) collective-permute-start(bf16[144,256]{1,0:T(8,128)(2,1)} %get-tuple-element.19), channel_id=1, source_target_pairs={{0,32},{32,64},{64,96},{96,128},{128,160},{160,192},{192,224},{1,3... | collective-permute-start | bytes 221192 | tf_op jit(solution)/shard_map/ppermute | solution.py:33
  4.7 6.4 %collective-permute-start.1 = (bf16[144,256]{1,0:T(8,128)(2,1)}, bf16[144,256]{1,0:T(8,128)(2,1)S(1)}, u32[]{:S(2)}, u32[]{:S(2)}) collective-permute-start(bf16[144,256]{1,0:T(8,128)(2,1)} %get-tuple-element.20), channel_id=1, source_target_pairs={{32,0},{64,32},{96,64},{128,96},{160,128},{192,160},{224,192},{33,... | collective-permute-start | bytes 221192 | tf_op jit(solution)/shard_map/ppermute | solution.py:33
  6.0 5.1 %copy-start = (bf16[144,256]{1,0:T(8,128)(2,1)}, bf16[144,256]{1,0:T(8,128)(2,1)S(1)}, u32[]{:S(2)}) copy-start(bf16[144,256]{1,0:T(8,128)(2,1)S(1)} %collective-permute-done.tail_ref) | copy-start | bytes 221188
  11.1 0.6 copy-start.1

commit v3 on v2

--- a/solution.py
+++ b/solution.py
@@ -102,16 +102,45 @@
     )
 
 
-def main_kernel(
+def copies_of(pairs, sems, chunk, size):
+    rows = rows_of(chunk, size)
+    return [
+        pltpu.make_async_copy(source.at[rows], target.at[rows], sems.at[place, chunk])
+        for place, (source, target) in enumerate(pairs)
+    ]
+
+
+def started(pairs, sems, chunk, size):
+    for place, copy in enumerate(copies_of(pairs, sems, chunk, size)):
+        copy.start(priority=place % 2)
+
+
+def awaited(pairs, sems, chunk, size):
+    for copy in copies_of(pairs, sems, chunk, size):
+        copy.wait()
+
+
+def each(count, body):
+    def step(index, _):
+        body(index)
+        return 0
+
+    lax.fori_loop(0, count, step, 0)
+
+
+def shifted(scratch, half, index, shift_by):
+    return scratch[half, pl.ds(index * BLOCK + shift_by, BLOCK)]
+
+
+def gradient_kernel(
     place_ref,
     query_any, key_any, value_any, query_two_any, key_two_any, cotangent_any,
     short_ref, medium_ref, tail_ref, head_ref,
-    output_any, query_grad_any, key_grad_any, value_grad_any, query_two_grad_any, key_two_grad_any,
-    parts_ref,
+    query_grad_any, key_two_grad_any, grad_inner_any, product_any, parts_ref,
     query_ref, key_ref, value_ref, query_two_ref, key_two_ref, cotangent_ref,
-    output_ref, query_grad_ref, key_grad_ref, value_grad_ref, query_two_grad_ref, key_two_grad_ref,
-    inner_ref, gated_ref, first_ref, later_ref, pair_ref, product_ref, turned_ref, back_ref, ahead_ref,
-    sums_ref, in_sems, out_sems,
+    query_grad_ref, key_two_grad_ref, grad_inner_ref,
+    inner_ref, gated_ref, first_ref, later_ref, pair_ref, product_ref, turned_ref, back_ref,
+    coefs_ref, lines_ref, sums_ref, in_sems, out_sems, product_sem,
 ):
     row_count, chan_count = query_ref.shape
     group_count = chan_count // GROUP
@@ -121,38 +150,20 @@
     steps = CHUNK // BLOCK
     taps = widened(short_ref[...])
     sequence_total = row_count * lax.axis_size("seq")
-    sources = (key_any, value_any, query_any, key_two_any, cotangent_any, query_two_any)
-    buffers = (key_ref, value_ref, query_ref, key_two_ref, cotangent_ref, query_two_ref)
-    results = (
-        output_ref, query_grad_ref, key_grad_ref, value_grad_ref, query_two_grad_ref, key_two_grad_ref
-    )
-    targets = (
-        output_any, query_grad_any, key_grad_any, value_grad_any, query_two_grad_any, key_two_grad_any
-    )
-
-    def copies_in(chunk):
-        rows = rows_of(chunk, CHUNK)
-        return [
-            pltpu.make_async_copy(source.at[rows], buffer.at[rows], in_sems.at[place, chunk])
-            for place, (source, buffer) in enumerate(zip(sources, buffers))
-        ]
-
-    def copies_out(chunk):
-        rows = rows_of(chunk, CHUNK)
-        return [
-            pltpu.make_async_copy(result.at[rows], target.at[rows], out_sems.at[place, chunk])
-            for place, (result, target) in enumerate(zip(results, targets))
-        ]
-
-    def start_in(chunk, _):
-        for copy in copies_in(chunk):
-            copy.start()
-        return 0
-
-    lax.fori_loop(0, chunk_count, start_in, 0)
+    loads = (
+        (key_any, key_ref), (value_any, value_ref), (query_any, query_ref),
+        (key_two_any, key_two_ref), (cotangent_any, cotangent_ref), (query_two_any, query_two_ref),
+    )
+    saves = (
+        (query_grad_ref, query_grad_any),
+        (key_two_grad_ref, key_two_grad_any),
+        (grad_inner_ref, grad_inner_any),
+    )
+    each(chunk_count, lambda chunk: started(loads, in_sems, chunk, CHUNK))
 
     unit = identity(chan_count)
     small_unit = unit[:BLOCK, :BLOCK]
+    coefs_ref[...] = widened(medium_ref[...])
     product_ref[:, :GROUP, :] = turned(tail_ref[HALO:], unit)
     turned_ref[:, span:, :] = turned(head_ref[:BLOCK], unit)
     for half in range(halves):
@@ -160,9 +171,8 @@
         first_ref[half, :RIM] = widened(tail_ref[:HALO, lanes])[RIM:]
         later_ref[half, row_count:] = widened(head_ref[BLOCK:, lanes])[:RIM]
 
-    def forward(chunk, _):
-        for copy in copies_in(chunk):
-            copy.wait()
+    def forward(chunk, slot):
+        awaited(loads, in_sems, chunk, CHUNK)
         for step in range(steps):
             index = chunk * steps + step
             rows = rows_of(index, BLOCK)
@@ -173,107 +183,199 @@
                 first_ref[half, pl.ds(pl.multiple_of(index * BLOCK + RIM, RIM), BLOCK)] = product_one
                 inner_one = taps[0:1, lanes] * product_one
                 for shift_by in range(1, SE_TAPS):
-                    inner_one += (
-                        taps[shift_by : shift_by + 1, lanes]
-                        * first_ref[half, pl.ds(index * BLOCK + RIM - shift_by, BLOCK)]
+                    inner_one += taps[shift_by : shift_by + 1, lanes] * shifted(
+                        first_ref, half, index, RIM - shift_by
                     )
                 inner_one = narrowed(inner_one)
                 gated = query_ref[rows, lanes] * inner_one
                 inner_ref[rows, lanes] = inner_one
                 gated_ref[rows, lanes] = gated
-                pair_ref[0, local, lanes] = key_two_ref[rows, lanes] * gated
-                pair_ref[1, local, lanes] = cotangent_ref[rows, lanes] * query_two_ref[rows, lanes]
-        product_two = turned(pair_ref[0], unit)
-        grad_inner_two = turned(pair_ref[1], unit)
+                pair_ref[slot, 0, local, lanes] = key_two_ref[rows, lanes] * gated
+                pair_ref[slot, 1, local, lanes] = cotangent_ref[rows, lanes] * query_two_ref[rows, lanes]
+        product_two = turned(pair_ref[slot, 0], unit)
+        grad_inner_two = turned(pair_ref[slot, 1], unit)
         for step in range(steps):
             index = chunk * steps + step
             local = slice(step * BLOCK, (step + 1) * BLOCK)
             product_ref[:, rows_of(index + 1, GROUP), :] = product_two[:, :, local]
             turned_ref[:, rows_of(index, GROUP), :] = grad_inner_two[:, :, local]
-        return 0
-
-    lax.fori_loop(0, chunk_count, forward, 0)
+
+    slots = pair_ref.shape[0]
+
+    def forward_pair(turn):
+        for slot in range(slots):
+            forward(turn * slots + slot, slot)
+
+    each(chunk_count // slots, forward_pair)
+    product_copy = pltpu.make_async_copy(product_ref, product_any, product_sem)
+    product_copy.start()
 
     flip_row = lax.broadcasted_iota(jnp.int32, (BLOCK, BLOCK), 0)
     flip_lane = lax.broadcasted_iota(jnp.int32, (BLOCK, BLOCK), 1)
     flip = narrowed(widened(flip_row + flip_lane == BLOCK - 1))
     medium_scale = 1.0 / math.sqrt(sequence_total * GROUP)
-    for group in range(group_count):
-        bands = upper_lower(widened(medium_ref[group : group + 1]))
-        window = jnp.concatenate(
-            [turned_ref[group, :span], turned_ref[group, GROUP : GROUP + span]], axis=1
-        )
-        back_ref[group] = narrowed(dotted(window, bands, ((1,), (1,))))
-        earlier = jnp.concatenate([product_ref[group, :span], product_ref[group, GROUP:]], axis=1)
-        causal = jnp.concatenate([bands[:, BLOCK:], bands[:, :BLOCK]], axis=0)
-        ahead_ref[group] = narrowed(dotted(earlier, causal, ((1,), (0,))))
-        flipped = narrowed(dotted(flip, product_ref[group, GROUP:], ((1,), (1,))))
-        pairs = dotted(flipped, window, ((1,), (0,)))
-        pairs = pltpu.roll(pairs, BLOCK + 1, 1, stride=1, stride_axis=0)
-        line = jnp.sum(pairs[:, :BLOCK], axis=0, keepdims=True) * medium_scale
-        half, row = group * GROUP // LANES, RIM + group % (LANES // GROUP)
-        parts_ref[:, row : row + 1, half * LANES : (half + 1) * LANES] = jnp.broadcast_to(
-            line[None], (parts_ref.shape[0], 1, LANES)
-        )
-
+
+    batch = 4
+
+    def medium_batch(turn):
+        groups = [turn * batch + place for place in range(batch)]
+        bands = [upper_lower(coefs_ref[pl.ds(group, 1)]) for group in groups]
+        flipped = [
+            narrowed(dotted(flip, product_ref[group, GROUP:], ((1,), (1,)))) for group in groups
+        ]
+        windows = [
+            jnp.concatenate(
+                [turned_ref[group, :span], turned_ref[group, GROUP : GROUP + span]], axis=1
+            )
+            for group in groups
+        ]
+        pairs = [
+            dotted(left, window, ((1,), (0,))) for left, window in zip(flipped, windows)
+        ]
+        backs = [
+            narrowed(dotted(window, band, ((1,), (1,)))) for window, band in zip(windows, bands)
+        ]
+        for group, back in zip(groups, backs):
+            back_ref[group] = back
+        for group, pair in zip(groups, pairs):
+            pair = pltpu.roll(pair, BLOCK + 1, 1, stride=1, stride_axis=0)
+            lines_ref[pl.ds(group, 1)] = (
+                jnp.sum(pair[:, :BLOCK], axis=0, keepdims=True) * medium_scale
+            )
+
+    each(group_count // batch, medium_batch)
     sums_ref[...] = jnp.zeros_like(sums_ref)
 
-    def backward(turn, _):
+    def backward(turn):
         chunk = chunk_count - 1 - turn
         for step in reversed(range(steps)):
             index = chunk * steps + step
             rows = rows_of(index, BLOCK)
-            lines = rows_of(index, GROUP)
-            back = back_ref[:, lines, :].reshape(chan_count, BLOCK)
-            ahead = ahead_ref[:, lines, :].reshape(chan_count, BLOCK)
+            back = back_ref[:, rows_of(index, GROUP), :].reshape(chan_count, BLOCK)
             back = narrowed(dotted(small_unit, back, ((1,), (1,))))
-            ahead = narrowed(dotted(small_unit, ahead, ((1,), (1,))))
-            output_ref[rows] = query_two_ref[rows] * ahead
-            query_two_grad_ref[rows] = cotangent_ref[rows] * ahead
             key_two_grad_ref[rows] = back * gated_ref[rows]
             grad_gated = back * key_two_ref[rows]
             query_grad_ref[rows] = grad_gated * inner_ref[rows]
-            grad_inner = widened(grad_gated * query_ref[rows])
+            grad_inner = grad_gated * query_ref[rows]
+            grad_inner_ref[rows] = grad_inner
+            grad_inner = widened(grad_inner)
             for half in range(halves):
                 lanes = slice(half * LANES, (half + 1) * LANES)
                 here = grad_inner[:, lanes]
                 later_ref[half, rows] = here
                 product_one = first_ref[half, pl.ds(pl.multiple_of(index * BLOCK + RIM, RIM), BLOCK)]
-                total = jnp.zeros_like(here)
                 for shift_by in range(SE_TAPS):
-                    moved = here
-                    if shift_by:
-                        moved = later_ref[half, pl.ds(index * BLOCK + shift_by, BLOCK)]
-                    total += taps[shift_by : shift_by + 1, lanes] * moved
+                    moved = shifted(later_ref, half, index, shift_by) if shift_by else here
                     sums_ref[half, shift_by] += jnp.sum(
                         (product_one * moved).reshape(BLOCK // RIM, RIM, LANES), axis=0
                     )
-                total = narrowed(total)
-                key_grad_ref[rows, lanes] = total * value_ref[rows, lanes]
-                value_grad_ref[rows, lanes] = total * key_ref[rows, lanes]
-        for copy in copies_out(chunk):
-            copy.start()
-        return 0
-
-    lax.fori_loop(0, chunk_count, backward, 0)
+        started(saves, out_sems, chunk, CHUNK)
+
+    each(chunk_count, backward)
 
     short_scale = 1.0 / math.sqrt(sequence_total)
+    per_half = LANES // GROUP
     for half in range(halves):
         lines = [
             jnp.sum(sums_ref[half, shift_by], axis=0, keepdims=True) * short_scale
             for shift_by in range(SE_TAPS)
         ]
-        lines = jnp.concatenate(lines + [jnp.zeros_like(lines[0])], axis=0)
-        parts_ref[:, :RIM, half * LANES : (half + 1) * LANES] = jnp.broadcast_to(
-            lines[None], (parts_ref.shape[0], RIM, LANES)
+        lines += [jnp.zeros_like(lines[0]), lines_ref[half * per_half : (half + 1) * per_half]]
+        lines = jnp.concatenate(lines, axis=0)
+        parts_ref[:, :, half * LANES : (half + 1) * LANES] = jnp.broadcast_to(
+            lines[None], (parts_ref.shape[0], *lines.shape)
         )
-
-    def wait_out(chunk, _):
-        for copy in copies_out(chunk):
-            copy.wait()
-        return 0
-
-    lax.fori_loop(0, chunk_count, wait_out, 0)
+    product_copy.wait()
+    each(chunk_count, lambda chunk: awaited(saves, out_sems, chunk, CHUNK))
+
+
+def medium_kernel(
+    place_ref, product_any, query_two_any, cotangent_any, medium_ref, output_any, query_grad_any,
+    product_ref, query_two_ref, cotangent_ref, output_ref, query_grad_ref, ahead_ref, coefs_ref,
+    product_sems, in_sems, out_sems,
+):
+    row_count, chan_count = query_two_ref.shape
+    chunk_count = row_count // CHUNK
+    steps = CHUNK // BLOCK
+    span = row_count // BLOCK * GROUP
+    batch_count = product_sems.shape[1]
+    batch = chan_count // GROUP // batch_count
+    products = ((product_any, product_ref),)
+    loads = ((query_two_any, query_two_ref), (cotangent_any, cotangent_ref))
+    saves = ((output_ref, output_any), (query_grad_ref, query_grad_any))
+    each(batch_count, lambda turn: started(products, product_sems, turn, batch))
+    each(chunk_count, lambda chunk: started(loads, in_sems, chunk, CHUNK))
+    unit = identity(BLOCK)
+    coefs_ref[...] = widened(medium_ref[...])
+
+    def medium_batch(turn):
+        groups = [turn * batch + place for place in range(batch)]
+        bands = [upper_lower(coefs_ref[pl.ds(group, 1)]) for group in groups]
+        awaited(products, product_sems, turn, batch)
+        aheads = []
+        for group, band in zip(groups, bands):
+            earlier = jnp.concatenate([product_ref[group, :span], product_ref[group, GROUP:]], axis=1)
+            causal = jnp.concatenate([band[:, BLOCK:], band[:, :BLOCK]], axis=0)
+            aheads.append(narrowed(dotted(earlier, causal, ((1,), (0,)))))
+        for group, ahead in zip(groups, aheads):
+            ahead_ref[group] = ahead
+
+    each(batch_count, medium_batch)
+
+    def one_chunk(chunk):
+        awaited(loads, in_sems, chunk, CHUNK)
+        for step in range(steps):
+            index = chunk * steps + step
+            rows = rows_of(index, BLOCK)
+            ahead = ahead_ref[:, rows_of(index, GROUP), :].reshape(chan_count, BLOCK)
+            ahead = narrowed(dotted(unit, ahead, ((1,), (1,))))
+            output_ref[rows] = query_two_ref[rows] * ahead
+            query_grad_ref[rows] = cotangent_ref[rows] * ahead
+        started(saves, out_sems, chunk, CHUNK)
+
+    each(chunk_count, one_chunk)
+    each(chunk_count, lambda chunk: awaited(saves, out_sems, chunk, CHUNK))
+
+
+def short_kernel(
+    place_ref, grad_inner_any, key_any, value_any, short_ref, head_ref, key_grad_any, value_grad_any,
+    grad_inner_ref, key_ref, value_ref, key_grad_ref, value_grad_ref, later_ref,
+    in_sems, out_sems,
+):
+    row_count, chan_count = key_ref.shape
+    chunk_count = row_count // CHUNK
+    steps = CHUNK // BLOCK
+    halves = chan_count // LANES
+    taps = widened(short_ref[...])
+    loads = ((grad_inner_any, grad_inner_ref), (key_any, key_ref), (value_any, value_ref))
+    saves = ((key_grad_ref, key_grad_any), (value_grad_ref, value_grad_any))
+    each(chunk_count, lambda turn: started(loads, in_sems, chunk_count - 1 - turn, CHUNK))
+    for half in range(halves):
+        lanes = slice(half * LANES, (half + 1) * LANES)
+        later_ref[half, row_count:] = widened(head_ref[:, lanes])[:RIM]
+
+    def backward(turn):
+        chunk = chunk_count - 1 - turn
+        awaited(loads, in_sems, chunk, CHUNK)
+        for step in reversed(range(steps)):
+            index = chunk * steps + step
+            rows = rows_of(index, BLOCK)
+            for half in range(halves):
+                lanes = slice(half * LANES, (half + 1) * LANES)
+                here = widened(grad_inner_ref[rows, lanes])
+                later_ref[half, rows] = here
+                total = taps[0:1, lanes] * here
+                for shift_by in range(1, SE_TAPS):
+                    total += taps[shift_by : shift_by + 1, lanes] * shifted(
+                        later_ref, half, index, shift_by
+                    )
+                total = narrowed(total)
+                key_grad_ref[rows, lanes] = total * value_ref[rows, lanes]
+                value_grad_ref[rows, lanes] = total * key_ref[rows, lanes]
+        started(saves, out_sems, chunk, CHUNK)
+
+    each(chunk_count, backward)
+    each(chunk_count, lambda chunk: awaited(saves, out_sems, chunk, CHUNK))
 
 
 def unpack_kernel(table_ref, short_ref, medium_ref):
@@ -345,53 +447,101 @@
     seq_count = lax.axis_size("seq")
     lines = (row_count // BLOCK + 1) * GROUP
     halves = chan_count // LANES
+    chunk_count = row_count // CHUNK
+    batch_count = 4
     stream = pltpu.VMEM((row_count, chan_count), jnp.bfloat16)
     turned_stream = pltpu.VMEM((group_count, lines, BLOCK), jnp.bfloat16)
-    results = pl.pallas_call(
-        main_kernel,
+    mixed_stream = pltpu.VMEM((group_count, lines - GROUP, BLOCK), jnp.bfloat16)
+    shifting = pltpu.VMEM((halves, row_count + RIM, LANES), jnp.float32)
+    coefs = pltpu.VMEM((group_count, MR_TAPS), jnp.float32)
+    query_first_grad, key_second_grad, grad_inner_one, product_two, parts = pl.pallas_call(
+        gradient_kernel,
         grid_spec=pltpu.PrefetchScalarGridSpec(
             num_scalar_prefetch=1,
             grid=(1,),
             in_specs=[any_spec] * 6 + [short_spec, medium_spec, halo_spec, halo_spec],
-            out_specs=(any_spec,) * 6
+            out_specs=(any_spec,) * 4
             + (pl.BlockSpec((seq_count, 2 * RIM, chan_count), lambda i, at: (0, 0, 0)),),
-            scratch_shapes=[stream] * 14
-            + [pltpu.VMEM((halves, row_count + RIM, LANES), jnp.float32)] * 2
-            + [pltpu.VMEM((2, CHUNK, chan_count), jnp.bfloat16)]
+            scratch_shapes=[stream] * 11
+            + [shifting] * 2
+            + [pltpu.VMEM((2, 2, CHUNK, chan_count), jnp.bfloat16)]
             + [turned_stream] * 2
-            + [pltpu.VMEM((group_count, lines - GROUP, BLOCK), jnp.bfloat16)] * 2
+            + [mixed_stream]
+            + [coefs, coefs]
             + [pltpu.VMEM((halves, SE_TAPS, RIM, LANES), jnp.float32)]
-            + [pltpu.SemaphoreType.DMA((6, row_count // CHUNK))] * 2,
-        ),
-        out_shape=(wide,) * 6 + (sds((seq_count, 2 * RIM, chan_count), jnp.float32),),
+            + [
+                pltpu.SemaphoreType.DMA((6, chunk_count)),
+                pltpu.SemaphoreType.DMA((3, chunk_count)),
+                pltpu.SemaphoreType.DMA,
+            ],
+        ),
+        out_shape=(wide,) * 3
+        + (
+            sds((group_count, lines, BLOCK), jnp.bfloat16),
+            sds((seq_count, 2 * RIM, chan_count), jnp.float32),
+        ),
         compiler_params=params(),
-        cost_estimate=cost(100 * row_count * chan_count, 12 * size),
-        name="main",
+        cost_estimate=cost(100 * row_count * chan_count, 10 * size),
+        name="gradients",
     )(
         place,
         query_first, key_first, value_first, query_second, key_second, cotangent,
         short_filter, medium_filter, tail, head,
     )
-    (
-        output_second,
-        query_first_grad,
-        key_first_grad,
-        value_first_grad,
-        query_second_grad,
-        key_second_grad,
-        parts,
-    ) = results
-
-    sums = narrowed(jnp.sum(lax.all_to_all(parts, "seq", 0, 0), axis=0))
+    partials = lax.all_to_all(parts, "seq", 0, 0)
+    output_second, query_second_grad = pl.pallas_call(
+        medium_kernel,
+        grid_spec=pltpu.PrefetchScalarGridSpec(
+            num_scalar_prefetch=1,
+            grid=(1,),
+            in_specs=[any_spec] * 3 + [medium_spec],
+            out_specs=(any_spec,) * 2,
+            scratch_shapes=[turned_stream]
+            + [stream] * 4
+            + [mixed_stream, coefs]
+            + [
+                pltpu.SemaphoreType.DMA((1, batch_count)),
+                pltpu.SemaphoreType.DMA((2, chunk_count)),
+                pltpu.SemaphoreType.DMA((2, chunk_count)),
+            ],
+        ),
+        out_shape=(wide,) * 2,
+        compiler_params=params(),
+        cost_estimate=cost(40 * row_count * chan_count, 5 * size),
+        name="medium_outputs",
+    )(place, product_two, query_second, cotangent, medium_filter)
+    partials, output_second, query_second_grad = lax.optimization_barrier(
+        (partials, output_second, query_second_grad)
+    )
+    sums = narrowed(jnp.sum(partials, axis=0))
     copies = jnp.broadcast_to(sums[None], (lax.axis_size("grp"), *sums.shape))
     table = lax.all_to_all(copies, "grp", 0, 0)
+    rim_halo_spec = pl.BlockSpec((HALO, chan_count), lambda i, at: (BLOCK // HALO, 0))
+    key_first_grad, value_first_grad = pl.pallas_call(
+        short_kernel,
+        grid_spec=pltpu.PrefetchScalarGridSpec(
+            num_scalar_prefetch=1,
+            grid=(1,),
+            in_specs=[any_spec] * 3 + [short_spec, rim_halo_spec],
+            out_specs=(any_spec,) * 2,
+            scratch_shapes=[stream] * 5
+            + [shifting]
+            + [
+                pltpu.SemaphoreType.DMA((3, chunk_count)),
+                pltpu.SemaphoreType.DMA((2, chunk_count)),
+            ],
+        ),
+        out_shape=(wide,) * 2,
+        compiler_params=params(),
+        cost_estimate=cost(40 * row_count * chan_count, 5 * size),
+        name="short_outputs",
+    )(place, grad_inner_one, key_first, value_first, short_filter, head)
     short_grad, medium_grad = pl.pallas_call(
         unpack_kernel,
         out_shape=(
             sds(short_filter.shape, jnp.float32),
             sds(medium_filter.shape, jnp.float32),
         ),
-        compiler_params=params(),
         name="unpack",
     )(table)
     return (

time: 65.5 us -> 66.7 us (1.018)
  blocking collectives: 36.9 us -> 0 us
  starting transfers between devices: 3.02 us -> 22.5 us
  Pallas kernels: 18.8 us -> 29 us
  waiting for transfers between devices: 5.11 us -> 11.8 us
  local copies, waits for them, and re-layouts: 0.66 us -> 2.07 us
    all_to_all x2 -> x0, blocking collectives: 36.9 us -> none  [the longest x1 20.5 us: per_device(): sums = narrowed(jnp.sum(lax.all_to_all(parts, 'seq', 0, 0), axis=0))]
    all_to_all x0 -> x2, starting transfers between devices: none -> 19.5 us  [the longest x1 11.3 us: per_device(): partials = lax.all_to_all(parts, 'seq', 0, 0)]
    pallas_call x1 -> x3, Pallas kernels: 14.7 us -> 24.9 us  [the longest x1 14.2 us: per_device(): pl.pallas_call(gradient_kernel, grid_spec=pltpu.PrefetchScalarGridSpec(nu...]
    all_to_all x0 -> x2, waiting for transfers between devices: none -> 6.69 us  [the longest x1 3.41 us: per_device(): partials = lax.all_to_all(parts, 'seq', 0, 0)]
    unnamed x4 -> x6, local copies, waits for them, and re-layouts: 0.64 us -> 1.34 us
    broadcast_in_dim x1, local copies, waits for them, and re-layouts: 0.02 us -> 0.72 us  [per_device(): copies = jnp.broadcast_to(sums[None], (lax.axis_size('grp'), *sums.shape))]
  transfers between devices with their start and end apart: 2 -> 4, of which waited for: 1 -> 3; matrix products, arithmetic and copies ran while one was open for 0% -> 0% of each run, Pallas kernels for 0% -> 16%
where the time goes in v3:
time: 66.7 us; the launch traced here: 66.1 us
  Pallas kernels  29 us (43%)
  starting transfers between devices  22.5 us (34%)
  waiting for transfers between devices  11.8 us (18%)
  local copies, waits for them, and re-layouts  2.07 us (3%)
  between operations  0.71 us (1%)
    pallas_call x1, Pallas kernels, per_device(): pl.pallas_call(gradient_kernel, grid_spec=pltpu.PrefetchScalarGridSpec(nu...  14.2 us
    all_to_all x1, starting transfers between devices, per_device(): partials = lax.all_to_all(parts, 'seq', 0, 0)  11.3 us
    all_to_all x1, starting transfers between devices, per_device(): table = lax.all_to_all(copies, 'grp', 0, 0)  8.22 us
    pallas_call x1, Pallas kernels, per_device(): pl.pallas_call(medium_kernel, grid_spec=pltpu.PrefetchScalarGridSpec(num_...  5.82 us
    ppermute x2, waiting for transfers between devices, passed_along(): lax.ppermute(value, axis, [(source, source + steps) for source in range(f...  5.1 us
    pallas_call x1, Pallas kernels, per_device(): pl.pallas_call(short_kernel, grid_spec=pltpu.PrefetchScalarGridSpec(num_s...  4.92 us
    all_to_all x1, waiting for transfers between devices, per_device(): partials = lax.all_to_all(parts, 'seq', 0, 0)  3.41 us
    all_to_all x1, waiting for transfers between devices, per_device(): table = lax.all_to_all(copies, 'grp', 0, 0)  3.28 us
  transfers between devices with their start and end apart: 4, of which 3 were waited for; matrix products, arithmetic and copies ran while one was open for 0% of the time, Pallas kernels for 16%

profile of v3, /device:TPU:2, one launch (start us, length us, event | category | flops | bytes accessed | tf_op | source)
XLA Modules:
  0.0 66.1 jit_solution(13661996006248707500)
XLA Ops:
  0.6 2.3 %rims.1 = (bf16[144,256]{1,0:T(8,128)(2,1)}, bf16[144,256]{1,0:T(8,128)(2,1)}) custom-call(s32[1]{0:T(128)} %bitcast.place_ref, bf16[2048,256]{1,0:T(8,128)(2,1)} %key_any.3, bf16[2048,256]{1,0:T(8,128)(2,1)} %value_any.3, bf16[2048,256]{1,0:T(8,128)(2,1)} %query_any.1, bf16[2048,256]{1,0:T(8,128)(2,1)} %key_two_any.1, bf16[2048,256]{1,0:T(8,128)(2,1)} %cotangent_any.3, ...), custom_call_target="tpu_custom_call" | custom-call | flops 12582912 | bytes 1048576 | tf_op jit(solution)/shard_map/rims/pallas_call | solution.py:425
  2.9 1.7 %collective-permute-start = (bf16[144,256]{1,0:T(8,128)(2,1)}, bf16[144,256]{1,0:T(8,128)(2,1)S(1)}, u32[]{:S(2)}, u32[]{:S(2)}) collective-permute-start(bf16[144,256]{1,0:T(8,128)(2,1)} %get-tuple-element.24), channel_id=1, source_target_pairs={{0,32},{32,64},{64,96},{96,128},{128,160},{160,192},{192,224},{1,3... | collective-permute-start | bytes 221192 | tf_op jit(solution)/shard_map/ppermute | solution.py:33
  4.7 1.3 %collective-permute-start.1 = (bf16[144,256]{1,0:T(8,128)(2,1)}, bf16[144,256]{1,0:T(8,128)(2,1)S(1)}, u32[]{:S(2)}, u32[]{:S(2)}) collective-permute-start(bf16[144,256]{1,0:T(8,128)(2,1)} %get-tuple-element.25), channel_id=1, source_target_pairs={{32,0},{64,32},{96,64},{128,96},{160,128},{192,160},{224,192},{33,... | collective-permute-start | bytes 221192 | tf_op jit(solution)/shard_map/ppermute | solution.py:33
  6.0 0.0 collective-permute-done.tail_ref
  6.0 0.0 copy-start.2
  6.0 5.1 %collective-permute-done.1.head_ref = bf16[144,256]{1,0:T(8,128)(2,1)S(1)} collective-permute-done((bf16[144,256]{1,0:T(8,128)(2,1)}, bf16[144,256]{1,0:T(8,128)(2,1)S(1)}, u32[]{:S(2)}, u32[]{:S(2)}) %collective-permute-start.1) | collective-permute-done | bytes 73760 | tf_op jit(solution)/shard_map/ppermute | solution.py:33
  11.1 0.0 copy-done.2
  11.1 0.0 copy-start.1
  11.1 0.6 copy-done.1
  11.7 14.2 %gradients.1 = (bf16[2048,256]{1,0:T(8,128)(2,1)}, bf16[2048,256]{1,0:T(8,128)(2,1)}, bf16[2048,256]{1,0:T(8,128)(2,1)}, bf16[16,272,128]{2,1,0:T(8,128)(2,1)}, f32[8,16,256]{2,1,0:T(8,128)}) custom-call(s32[1]{0:T(128)} %bitcast.place_ref, bf16[2048,256]{1,0:T(8,128)(2,1)} %query_any.1, bf16[2048,256]{1,0:T(8,128)(2,1)} %key_any.3, ...), custom_call_target="tpu_custom_call" | custom-call | flops 52428800 | bytes 10485760 | tf_op jit(solution)/shard_map/gradients/pallas_call | solution.py:457
  25.9 11.3 %all-to-all-start = ((f32[8,16,256]{2,1,0:T(8,128)}), f32[8,16,256]{2,1,0:T(8,128)S(1)}, u32[]{:S(2)}, u32[]{:S(2)}) async-start(f32[8,16,256]{2,1,0:T(8,128)} %get-tuple-element.26), calls=%async_computation | async-start | bytes 262144 | tf_op jit(solution)/shard_map/all_to_all | solution.py:491
  37.2 5.8 %medium_outputs.1 = (bf16[2048,256]{1,0:T(8,128)(2,1)}, bf16[2048,256]{1,0:T(8,128)(2,1)}) custom-call(s32[1]{0:T(128)} %bitcast.place_ref, bf16[16,272,128]{2,1,0:T(8,128)(2,1)} %get-tuple-element.27.product_any, bf16[2048,256]{1,0:T(8,128)(2,1)} %query_two_any.3, bf16[2048,256]{1,0:T(8,128)(2,1)} %cotangent_any.3, bf16[512,128]{1,0:T(8,128)(2,1)} %medium_ref.5), custom_call_target="tpu_custom_call" | custom-call | flops 20971520 | bytes 5242880 | tf_op jit(solution)/shard_map/medium_outputs/pallas_call | solution.py:492
  43.0 3.4 %all-to-all-done = f32[8,16,256]{2,1,0:T(8,128)S(1)} async-done(((f32[8,16,256]{2,1,0:T(8,128)}), f32[8,16,256]{2,1,0:T(8,128)S(1)}, u32[]{:S(2)}, u32[]{:S(2)}) %all-to-all-start) | async-done | bytes 131104 | tf_op jit(solution)/shard_map/all_to_all | solution.py:491
  46.5 0.7 %broadcast_in_dim.2 = bf16[32,16,256]{2,1,0:T(8,128)(2,1)} broadcast(bf16[16,256]{1,0:T(8,128)(2,1)S(1)} %reduce_sum.9), dimensions={1,2} | broadcast | bytes 270336 | tf_op jit(solution)/shard_map/broadcast_in_dim | solution.py:517
  47.2 8.2 %all-to-all-start.1 = ((bf16[32,16,256]{2,1,0:T(8,128)(2,1)}), bf16[32,16,256]{2,1,0:T(8,128)(2,1)S(1)}, u32[]{:S(2)}, u32[]{:S(2)}) async-start(bf16[32,16,256]{2,1,0:T(8,128)(2,1)} %broadcast_in_dim.2), calls=%async_computation.1 | async-start | bytes 524288 | tf_op jit(solution)/shard_map/all_to_all | solution.py:518
  55.4 4.9 %short_outputs.1 = (bf16[2048,256]{1,0:T(8,128)(2,1)}, bf16[2048,256]{1,0:T(8,128)(2,1)}) custom-call(s32[1]{0:T(128)} %bitcast.place_ref, bf16[2048,256]{1,0:T(8,128)(2,1)} %get-tuple-element.32.grad_inner_any, bf16[2048,256]{1,0:T(8,128)(2,1)} %key_any.3, bf16[2048,256]{1,0:T(8,128)(2,1)} %value_any.3, bf16[7,8192]{1,0:T(8,128)(2,1)} %short_ref.5, ...), custom_call_target="tpu_custom_call" | custom-call | flops 20971520 | bytes 5242880 | tf_op jit(solution)/shard_map/short_outputs/pallas_call | solution.py:520
  60.3 3.3 %all-to-all-done.1.table_ref = bf16[32,16,256]{2,1,0:T(8,128)(2,1)S(1)} async-done(((bf16[32,16,256]{2,1,0:T(8,128)(2,1)}), bf16[32,16,256]{2,1,0:T(8,128)(2,1)S(1)}, u32[]{:S(2)}, u32[]{:S(2)}) %all-to-all-start.1) | async-done | bytes 262176 | tf_op jit(solution)/shard_map/all_to_all | solution.py:518
  63.6 0.0 copy-start
  63.6 0.7 %copy-done = bf16[32,16,256]{2,1,0:T(8,128)(2,1)} copy-done((bf16[32,16,256]{2,1,0:T(8,128)(2,1)}, bf16[32,16,256]{2,1,0:T(8,128)(2,1)S(1)}, u32[]{:S(2)}) %copy-start) | copy-done | bytes 262168
  64.3 1.8 %unpack.1 = (f32[7,8192]{1,0:T(8,128)}, f32[512,128]{1,0:T(8,128)}) custom-call(bf16[32,16,256]{2,1,0:T(8,128)(2,1)} %copy-done), custom_call_target="tpu_custom_call" | custom-call | tf_op jit(solution)/shard_map/unpack/pallas_call | solution.py:539
  (1 shorter events, 0.0 us)
Async XLA Ops:
  2.9 3.0 %collective-permute-start = (bf16[144,256]{1,0:T(8,128)(2,1)}, bf16[144,256]{1,0:T(8,128)(2,1)S(1)}, u32[]{:S(2)}, u32[]{:S(2)}) collective-permute-start(bf16[144,256]{1,0:T(8,128)(2,1)} %get-tuple-element.24), channel_id=1, source_target_pairs={{0,32},{32,64},{64,96},{96,128},{128,160},{160,192},{192,224},{1,3... | collective-permute-start | bytes 221192 | tf_op jit(solution)/shard_map/ppermute | solution.py:33
  4.7 6.4 %collective-permute-start.1 = (bf16[144,256]{1,0:T(8,128)(2,1)}, bf16[144,256]{1,0:T(8,128)(2,1)S(1)}, u32[]{:S(2)}, u32[]{:S(2)}) collective-permute-start(bf16[144,256]{1,0:T(8,128)(2,1)} %get-tuple-element.25), channel_id=1, source_target_pairs={{32,0},{64,32},{96,64},{128,96},{160,128},{192,160},{224,192},{33,... | collective-permute-start | bytes 221192 | tf_op jit(solution)/shard_map/ppermute | solution.py:33
  6.0 5.1 %copy-start.2 = (bf16[144,256]{1,0:T(8,128)(2,1)}, bf16[144,256]{1,0:T(8,128)(2,1)S(1)}, u32[]{:S(2)}) copy-start(bf16[144,256]{1,0:T(8,128)(2,1)S(1)} %collective-permute-done.tail_ref) | copy-start | bytes 221188
  11.1 0.6 copy-start.1
  25.9 20.5 %all-to-all-start = ((f32[8,16,256]{2,1,0:T(8,128)}), f32[8,16,256]{2,1,0:T(8,128)S(1)}, u32[]{:S(2)}, u32[]{:S(2)}) async-start(f32[8,16,256]{2,1,0:T(8,128)} %get-tuple-element.26), calls=%async_computation | async-start | bytes 262144 | tf_op jit(solution)/shard_map/all_to_all | solution.py:491
  47.2 16.4 %all-to-all-start.1 = ((bf16[32,16,256]{2,1,0:T(8,128)(2,1)}), bf16[32,16,256]{2,1,0:T(8,128)(2,1)S(1)}, u32[]{:S(2)}, u32[]{:S(2)}) async-start(bf16[32,16,256]{2,1,0:T(8,128)(2,1)} %broadcast_in_dim.2), calls=%async_computation.1 | async-start | bytes 524288 | tf_op jit(solution)/shard_map/all_to_all | solution.py:518
  63.6 0.7 %copy-start = (bf16[32,16,256]{2,1,0:T(8,128)(2,1)}, bf16[32,16,256]{2,1,0:T(8,128)(2,1)S(1)}, u32[]{:S(2)}) copy-start(bf16[32,16,256]{2,1,0:T(8,128)(2,1)S(1)} %all-to-all-done.1.table_ref) | copy-start | bytes 786436

commit v4 on v2

--- a/solution.py
+++ b/solution.py
@@ -102,6 +102,10 @@
     )
 
 
+def window(scratch, start, count):
+    return [scratch[pl.ds(start + place, RIM, stride=CHUNK // RIM)] for place in range(count)]
+
+
 def main_kernel(
     place_ref,
     query_any, key_any, value_any, query_two_any, key_two_any, cotangent_any,
@@ -110,8 +114,8 @@
     parts_ref,
     query_ref, key_ref, value_ref, query_two_ref, key_two_ref, cotangent_ref,
     output_ref, query_grad_ref, key_grad_ref, value_grad_ref, query_two_grad_ref, key_two_grad_ref,
-    inner_ref, gated_ref, first_ref, later_ref, pair_ref, product_ref, turned_ref, back_ref, ahead_ref,
-    sums_ref, in_sems, out_sems,
+    inner_ref, gated_ref, first_ref, later_ref, mixed_ref, pair_ref, product_ref, turned_ref, back_ref, ahead_ref,
+    coefs_ref, lines_ref, sums_ref, in_sems, out_sems,
 ):
     row_count, chan_count = query_ref.shape
     group_count = chan_count // GROUP
@@ -151,6 +155,7 @@
 
     lax.fori_loop(0, chunk_count, start_in, 0)
 
+    coefs_ref[...] = widened(medium_ref[...])
     unit = identity(chan_count)
     small_unit = unit[:BLOCK, :BLOCK]
     product_ref[:, :GROUP, :] = turned(tail_ref[HALO:], unit)
@@ -158,31 +163,32 @@
     for half in range(halves):
         lanes = slice(half * LANES, (half + 1) * LANES)
         first_ref[half, :RIM] = widened(tail_ref[:HALO, lanes])[RIM:]
-        later_ref[half, row_count:] = widened(head_ref[BLOCK:, lanes])[:RIM]
+        later_ref[half, row_count : row_count + RIM] = widened(head_ref[BLOCK:, lanes])[:RIM]
+
+    registers = CHUNK // RIM
 
     def forward(chunk, _):
         for copy in copies_in(chunk):
             copy.wait()
-        for step in range(steps):
-            index = chunk * steps + step
-            rows = rows_of(index, BLOCK)
-            local = slice(step * BLOCK, (step + 1) * BLOCK)
-            for half in range(halves):
-                lanes = slice(half * LANES, (half + 1) * LANES)
-                product_one = widened(key_ref[rows, lanes] * value_ref[rows, lanes])
-                first_ref[half, pl.ds(pl.multiple_of(index * BLOCK + RIM, RIM), BLOCK)] = product_one
-                inner_one = taps[0:1, lanes] * product_one
+        rows = rows_of(chunk, CHUNK)
+        for half in range(halves):
+            lanes = slice(half * LANES, (half + 1) * LANES)
+            first, mixed = first_ref.at[half], mixed_ref.at[half]
+            start = pl.multiple_of(chunk * CHUNK + RIM, RIM)
+            first[pl.ds(start, CHUNK)] = widened(key_ref[rows, lanes] * value_ref[rows, lanes])
+            rim = SE_TAPS - 1
+            moved = window(first, start - rim, registers + rim)
+            for place in range(registers):
+                total = taps[0:1, lanes] * moved[place + rim]
                 for shift_by in range(1, SE_TAPS):
-                    inner_one += (
-                        taps[shift_by : shift_by + 1, lanes]
-                        * first_ref[half, pl.ds(index * BLOCK + RIM - shift_by, BLOCK)]
-                    )
-                inner_one = narrowed(inner_one)
-                gated = query_ref[rows, lanes] * inner_one
-                inner_ref[rows, lanes] = inner_one
-                gated_ref[rows, lanes] = gated
-                pair_ref[0, local, lanes] = key_two_ref[rows, lanes] * gated
-                pair_ref[1, local, lanes] = cotangent_ref[rows, lanes] * query_two_ref[rows, lanes]
+                    total += taps[shift_by : shift_by + 1, lanes] * moved[place + rim - shift_by]
+                mixed[pl.ds(place, RIM, stride=registers)] = total
+            inner_one = narrowed(mixed[:CHUNK])
+            gated = query_ref[rows, lanes] * inner_one
+            inner_ref[rows, lanes] = inner_one
+            gated_ref[rows, lanes] = gated
+            pair_ref[0, :, lanes] = key_two_ref[rows, lanes] * gated
+            pair_ref[1, :, lanes] = cotangent_ref[rows, lanes] * query_two_ref[rows, lanes]
         product_two = turned(pair_ref[0], unit)
         grad_inner_two = turned(pair_ref[1], unit)
         for step in range(steps):
@@ -198,24 +204,40 @@
     flip_lane = lax.broadcasted_iota(jnp.int32, (BLOCK, BLOCK), 1)
     flip = narrowed(widened(flip_row + flip_lane == BLOCK - 1))
     medium_scale = 1.0 / math.sqrt(sequence_total * GROUP)
-    for group in range(group_count):
-        bands = upper_lower(widened(medium_ref[group : group + 1]))
-        window = jnp.concatenate(
-            [turned_ref[group, :span], turned_ref[group, GROUP : GROUP + span]], axis=1
-        )
-        back_ref[group] = narrowed(dotted(window, bands, ((1,), (1,))))
-        earlier = jnp.concatenate([product_ref[group, :span], product_ref[group, GROUP:]], axis=1)
-        causal = jnp.concatenate([bands[:, BLOCK:], bands[:, :BLOCK]], axis=0)
-        ahead_ref[group] = narrowed(dotted(earlier, causal, ((1,), (0,))))
-        flipped = narrowed(dotted(flip, product_ref[group, GROUP:], ((1,), (1,))))
-        pairs = dotted(flipped, window, ((1,), (0,)))
-        pairs = pltpu.roll(pairs, BLOCK + 1, 1, stride=1, stride_axis=0)
-        line = jnp.sum(pairs[:, :BLOCK], axis=0, keepdims=True) * medium_scale
-        half, row = group * GROUP // LANES, RIM + group % (LANES // GROUP)
-        parts_ref[:, row : row + 1, half * LANES : (half + 1) * LANES] = jnp.broadcast_to(
-            line[None], (parts_ref.shape[0], 1, LANES)
-        )
-
+    batch = 4
+
+    def medium_batch(turn, _):
+        groups = [turn * batch + place for place in range(batch)]
+        bands = [upper_lower(coefs_ref[pl.ds(group, 1)]) for group in groups]
+        flipped = [
+            narrowed(dotted(flip, product_ref[group, GROUP:], ((1,), (1,)))) for group in groups
+        ]
+        windows = [
+            jnp.concatenate(
+                [turned_ref[group, :span], turned_ref[group, GROUP : GROUP + span]], axis=1
+            )
+            for group in groups
+        ]
+        pairs = [dotted(left, view, ((1,), (0,))) for left, view in zip(flipped, windows)]
+        backs = [
+            narrowed(dotted(view, band, ((1,), (1,)))) for view, band in zip(windows, bands)
+        ]
+        aheads = []
+        for group, band in zip(groups, bands):
+            earlier = jnp.concatenate([product_ref[group, :span], product_ref[group, GROUP:]], axis=1)
+            causal = jnp.concatenate([band[:, BLOCK:], band[:, :BLOCK]], axis=0)
+            aheads.append(narrowed(dotted(earlier, causal, ((1,), (0,)))))
+        for group, back, ahead in zip(groups, backs, aheads):
+            back_ref[group] = back
+            ahead_ref[group] = ahead
+        for group, pair in zip(groups, pairs):
+            pair = pltpu.roll(pair, BLOCK + 1, 1, stride=1, stride_axis=0)
+            lines_ref[pl.ds(group, 1)] = (
+                jnp.sum(pair[:, :BLOCK], axis=0, keepdims=True) * medium_scale
+            )
+        return 0
+
+    lax.fori_loop(0, group_count // batch, medium_batch, 0)
     sums_ref[...] = jnp.zeros_like(sums_ref)
 
     def backward(turn, _):
@@ -235,22 +257,27 @@
             query_grad_ref[rows] = grad_gated * inner_ref[rows]
             grad_inner = widened(grad_gated * query_ref[rows])
             for half in range(halves):
-                lanes = slice(half * LANES, (half + 1) * LANES)
-                here = grad_inner[:, lanes]
-                later_ref[half, rows] = here
-                product_one = first_ref[half, pl.ds(pl.multiple_of(index * BLOCK + RIM, RIM), BLOCK)]
-                total = jnp.zeros_like(here)
-                for shift_by in range(SE_TAPS):
-                    moved = here
-                    if shift_by:
-                        moved = later_ref[half, pl.ds(index * BLOCK + shift_by, BLOCK)]
-                    total += taps[shift_by : shift_by + 1, lanes] * moved
-                    sums_ref[half, shift_by] += jnp.sum(
-                        (product_one * moved).reshape(BLOCK // RIM, RIM, LANES), axis=0
-                    )
-                total = narrowed(total)
-                key_grad_ref[rows, lanes] = total * value_ref[rows, lanes]
-                value_grad_ref[rows, lanes] = total * key_ref[rows, lanes]
+                later_ref[half, rows] = grad_inner[:, half * LANES : (half + 1) * LANES]
+        rows = rows_of(chunk, CHUNK)
+        for half in range(halves):
+            lanes = slice(half * LANES, (half + 1) * LANES)
+            first, later, mixed = first_ref.at[half], later_ref.at[half], mixed_ref.at[half]
+            start = pl.multiple_of(chunk * CHUNK, CHUNK)
+            moved = window(later, start, registers + SE_TAPS - 1)
+            sums = [sums_ref[half, shift_by] for shift_by in range(SE_TAPS)]
+            for place in range(registers):
+                here = first[pl.ds(start + RIM + place, RIM, stride=registers)]
+                total = taps[0:1, lanes] * moved[place]
+                sums[0] += here * moved[place]
+                for shift_by in range(1, SE_TAPS):
+                    total += taps[shift_by : shift_by + 1, lanes] * moved[place + shift_by]
+                    sums[shift_by] += here * moved[place + shift_by]
+                mixed[pl.ds(place, RIM, stride=registers)] = total
+            for shift_by in range(SE_TAPS):
+                sums_ref[half, shift_by] = sums[shift_by]
+            total = narrowed(mixed[:CHUNK])
+            key_grad_ref[rows, lanes] = total * value_ref[rows, lanes]
+            value_grad_ref[rows, lanes] = total * key_ref[rows, lanes]
         for copy in copies_out(chunk):
             copy.start()
         return 0
@@ -258,14 +285,16 @@
     lax.fori_loop(0, chunk_count, backward, 0)
 
     short_scale = 1.0 / math.sqrt(sequence_total)
+    per_half = LANES // GROUP
     for half in range(halves):
         lines = [
             jnp.sum(sums_ref[half, shift_by], axis=0, keepdims=True) * short_scale
             for shift_by in range(SE_TAPS)
         ]
-        lines = jnp.concatenate(lines + [jnp.zeros_like(lines[0])], axis=0)
-        parts_ref[:, :RIM, half * LANES : (half + 1) * LANES] = jnp.broadcast_to(
-            lines[None], (parts_ref.shape[0], RIM, LANES)
+        lines += [jnp.zeros_like(lines[0]), lines_ref[half * per_half : (half + 1) * per_half]]
+        lines = jnp.concatenate(lines, axis=0)
+        parts_ref[:, :, half * LANES : (half + 1) * LANES] = jnp.broadcast_to(
+            lines[None], (parts_ref.shape[0], *lines.shape)
         )
 
     def wait_out(chunk, _):
@@ -287,8 +316,8 @@
             medium_ref[first : first + groups] = piece[RIM:, half * LANES : (half + 1) * LANES]
 
 
-def params():
-    return pltpu.CompilerParams(vmem_limit_bytes=VMEM_LIMIT)
+def params(limit=VMEM_LIMIT):
+    return pltpu.CompilerParams(vmem_limit_bytes=limit)
 
 
 def cost(flops, size):
@@ -356,10 +385,12 @@
             out_specs=(any_spec,) * 6
             + (pl.BlockSpec((seq_count, 2 * RIM, chan_count), lambda i, at: (0, 0, 0)),),
             scratch_shapes=[stream] * 14
-            + [pltpu.VMEM((halves, row_count + RIM, LANES), jnp.float32)] * 2
+            + [pltpu.VMEM((halves, row_count + 2 * RIM + CHUNK // RIM, LANES), jnp.float32)] * 2
+            + [pltpu.VMEM((halves, CHUNK + CHUNK // RIM, LANES), jnp.float32)]
             + [pltpu.VMEM((2, CHUNK, chan_count), jnp.bfloat16)]
             + [turned_stream] * 2
             + [pltpu.VMEM((group_count, lines - GROUP, BLOCK), jnp.bfloat16)] * 2
+            + [pltpu.VMEM((group_count, MR_TAPS), jnp.float32)] * 2
             + [pltpu.VMEM((halves, SE_TAPS, RIM, LANES), jnp.float32)]
             + [pltpu.SemaphoreType.DMA((6, row_count // CHUNK))] * 2,
         ),
@@ -391,7 +422,7 @@
             sds(short_filter.shape, jnp.float32),
             sds(medium_filter.shape, jnp.float32),
         ),
-        compiler_params=params(),
+        compiler_params=params(16 * 1024 * 1024),
         name="unpack",
     )(table)
     return (

time: 65.5 us -> 69.6 us (1.063)
  Pallas kernels: 18.8 us -> 23 us
    pallas_call x1, Pallas kernels: 14.7 us -> 19.9 us  [per_device(): pl.pallas_call(main_kernel, grid_spec=pltpu.PrefetchScalarGridSpec(num_sc...]
    pallas_call x1, Pallas kernels: 1.77 us -> 0.82 us  [per_device(): pl.pallas_call(unpack_kernel, out_shape=(sds(short_filter.shape, jnp.floa...]
where the time goes in v4:
time: 69.6 us; the launch traced here: 69.2 us
  blocking collectives  36.8 us (53%)
  Pallas kernels  23 us (33%)
  waiting for transfers between devices  5.11 us (7%)
  starting transfers between devices  3.02 us (4%)
    all_to_all x1, blocking collectives, per_device(): sums = narrowed(jnp.sum(lax.all_to_all(parts, 'seq', 0, 0), axis=0))  20.5 us
    pallas_call x1, Pallas kernels, per_device(): pl.pallas_call(main_kernel, grid_spec=pltpu.PrefetchScalarGridSpec(num_sc...  19.9 us
    all_to_all x1, blocking collectives, per_device(): table = lax.all_to_all(copies, 'grp', 0, 0)  16.2 us
    ppermute x2, waiting for transfers between devices, passed_along(): lax.ppermute(value, axis, [(source, source + steps) for source in range(f...  5.11 us
    ppermute x2, starting transfers between devices, passed_along(): lax.ppermute(value, axis, [(source, source + steps) for source in range(f...  3.02 us
    pallas_call x1, Pallas kernels, per_device(): pl.pallas_call(rims_kernel, grid_spec=pltpu.PrefetchScalarGridSpec(num_sc...  2.3 us
  transfers between devices with their start and end apart: 2, of which 1 were waited for; matrix products, arithmetic and copies ran while one was open for 0% of the time, Pallas kernels for 0%

profile of v4, /device:TPU:2, one launch (start us, length us, event | category | flops | bytes accessed | tf_op | source)
XLA Modules:
  0.0 69.2 jit_solution(3450108678574734058)
XLA Ops:
  0.6 2.3 %rims.1 = (bf16[144,256]{1,0:T(8,128)(2,1)}, bf16[144,256]{1,0:T(8,128)(2,1)}) custom-call(s32[1]{0:T(128)} %bitcast.place_ref, bf16[2048,256]{1,0:T(8,128)(2,1)} %key_any.1, bf16[2048,256]{1,0:T(8,128)(2,1)} %value_any.1, bf16[2048,256]{1,0:T(8,128)(2,1)} %query_any.1, bf16[2048,256]{1,0:T(8,128)(2,1)} %key_two_any.1, bf16[2048,256]{1,0:T(8,128)(2,1)} %cotangent_any.1, ...), custom_call_target="tpu_custom_call" | custom-call | flops 12582912 | bytes 1048576 | tf_op jit(solution)/shard_map/rims/pallas_call | solution.py:352
  2.9 1.7 %collective-permute-start = (bf16[144,256]{1,0:T(8,128)(2,1)}, bf16[144,256]{1,0:T(8,128)(2,1)S(1)}, u32[]{:S(2)}, u32[]{:S(2)}) collective-permute-start(bf16[144,256]{1,0:T(8,128)(2,1)} %get-tuple-element.19), channel_id=1, source_target_pairs={{0,32},{32,64},{64,96},{96,128},{128,160},{160,192},{192,224},{1,3... | collective-permute-start | bytes 221192 | tf_op jit(solution)/shard_map/ppermute | solution.py:33
  4.7 1.3 %collective-permute-start.1 = (bf16[144,256]{1,0:T(8,128)(2,1)}, bf16[144,256]{1,0:T(8,128)(2,1)S(1)}, u32[]{:S(2)}, u32[]{:S(2)}) collective-permute-start(bf16[144,256]{1,0:T(8,128)(2,1)} %get-tuple-element.20), channel_id=1, source_target_pairs={{32,0},{64,32},{96,64},{128,96},{160,128},{192,160},{224,192},{33,... | collective-permute-start | bytes 221192 | tf_op jit(solution)/shard_map/ppermute | solution.py:33
  6.0 0.0 collective-permute-done.tail_ref
  6.0 0.0 copy-start
  6.0 5.1 %collective-permute-done.1.head_ref = bf16[144,256]{1,0:T(8,128)(2,1)S(1)} collective-permute-done((bf16[144,256]{1,0:T(8,128)(2,1)}, bf16[144,256]{1,0:T(8,128)(2,1)S(1)}, u32[]{:S(2)}, u32[]{:S(2)}) %collective-permute-start.1) | collective-permute-done | bytes 73760 | tf_op jit(solution)/shard_map/ppermute | solution.py:33
  11.1 0.0 copy-done
  11.1 0.0 copy-start.1
  11.1 0.6 copy-done.1
  11.7 19.9 %main.1 = (bf16[2048,256]{1,0:T(8,128)(2,1)}, bf16[2048,256]{1,0:T(8,128)(2,1)}, bf16[2048,256]{1,0:T(8,128)(2,1)}, bf16[2048,256]{1,0:T(8,128)(2,1)}, bf16[2048...) custom-call(s32[1]{0:T(128)} %bitcast.place_ref, bf16[2048,256]{1,0:T(8,128)(2,1)} %query_any.1, ...), custom_call_target="tpu_custom_call" | custom-call | flops 52428800 | bytes 12582912 | tf_op jit(solution)/shard_map/main/pallas_call | solution.py:379
  31.6 20.5 %all_to_all.10 = f32[8,16,256]{2,1,0:T(8,128)S(1)} all-to-all(f32[8,16,256]{2,1,0:T(8,128)} %get-tuple-element.27), channel_id=1, replica_groups=mesh['seq'=8,'grp'=32] {'seq'}, dimensions={0} | all-to-all | bytes 262144 | tf_op jit(solution)/shard_map/all_to_all | solution.py:416
  52.2 16.2 %all_to_all.11.table_ref = bf16[32,16,256]{2,1,0:T(8,128)(2,1)S(1)} all-to-all(bf16[32,16,256]{2,1,0:T(8,128)(2,1)S(1)} %broadcast_in_dim.2), channel_id=1, replica_groups=mesh['seq'=8,'grp'=32] {'grp'}, dimensions={0} | all-to-all | bytes 524288 | tf_op jit(solution)/shard_map/all_to_all | solution.py:418
  68.4 0.8 %unpack.1 = (f32[7,8192]{1,0:T(8,128)}, f32[512,128]{1,0:T(8,128)}) custom-call(bf16[32,16,256]{2,1,0:T(8,128)(2,1)S(1)} %all_to_all.11.table_ref), custom_call_target="tpu_custom_call" | custom-call | tf_op jit(solution)/shard_map/unpack/pallas_call | solution.py:419
  (2 shorter events, 0.0 us)
Async XLA Ops:
  2.9 3.0 %collective-permute-start = (bf16[144,256]{1,0:T(8,128)(2,1)}, bf16[144,256]{1,0:T(8,128)(2,1)S(1)}, u32[]{:S(2)}, u32[]{:S(2)}) collective-permute-start(bf16[144,256]{1,0:T(8,128)(2,1)} %get-tuple-element.19), channel_id=1, source_target_pairs={{0,32},{32,64},{64,96},{96,128},{128,160},{160,192},{192,224},{1,3... | collective-permute-start | bytes 221192 | tf_op jit(solution)/shard_map/ppermute | solution.py:33
  4.7 6.4 %collective-permute-start.1 = (bf16[144,256]{1,0:T(8,128)(2,1)}, bf16[144,256]{1,0:T(8,128)(2,1)S(1)}, u32[]{:S(2)}, u32[]{:S(2)}) collective-permute-start(bf16[144,256]{1,0:T(8,128)(2,1)} %get-tuple-element.20), channel_id=1, source_target_pairs={{32,0},{64,32},{96,64},{128,96},{160,128},{192,160},{224,192},{33,... | collective-permute-start | bytes 221192 | tf_op jit(solution)/shard_map/ppermute | solution.py:33
  6.0 5.1 %copy-start = (bf16[144,256]{1,0:T(8,128)(2,1)}, bf16[144,256]{1,0:T(8,128)(2,1)S(1)}, u32[]{:S(2)}) copy-start(bf16[144,256]{1,0:T(8,128)(2,1)S(1)} %collective-permute-done.tail_ref) | copy-start | bytes 221188
  11.1 0.6 copy-start.1

commit v5 on v2

--- a/solution.py
+++ b/solution.py
@@ -15,6 +15,7 @@
 LANES = 128
 RIM = 8
 CHUNK = 256
+AHEAD = 4
 HALO = 16
 VMEM_LIMIT = 63 * 1024 * 1024
 
@@ -110,8 +111,8 @@
     parts_ref,
     query_ref, key_ref, value_ref, query_two_ref, key_two_ref, cotangent_ref,
     output_ref, query_grad_ref, key_grad_ref, value_grad_ref, query_two_grad_ref, key_two_grad_ref,
-    inner_ref, gated_ref, first_ref, later_ref, pair_ref, product_ref, turned_ref, back_ref, ahead_ref,
-    sums_ref, in_sems, out_sems,
+    inner_ref, gated_ref, first_ref, later_ref, even_ref, odd_ref, product_ref, turned_ref, back_ref, ahead_ref,
+    coefs_ref, lines_ref, sums_ref, in_sems, out_sems,
 ):
     row_count, chan_count = query_ref.shape
     group_count = chan_count // GROUP
@@ -144,13 +145,14 @@
             for place, (result, target) in enumerate(zip(results, targets))
         ]
 
-    def start_in(chunk, _):
+    def start_in(chunk):
         for copy in copies_in(chunk):
             copy.start()
-        return 0
-
-    lax.fori_loop(0, chunk_count, start_in, 0)
-
+
+    for chunk in range(min(AHEAD, chunk_count)):
+        start_in(chunk)
+
+    coefs_ref[...] = widened(medium_ref[...])
     unit = identity(chan_count)
     small_unit = unit[:BLOCK, :BLOCK]
     product_ref[:, :GROUP, :] = turned(tail_ref[HALO:], unit)
@@ -160,7 +162,7 @@
         first_ref[half, :RIM] = widened(tail_ref[:HALO, lanes])[RIM:]
         later_ref[half, row_count:] = widened(head_ref[BLOCK:, lanes])[:RIM]
 
-    def forward(chunk, _):
+    def forward(chunk, pair_ref):
         for copy in copies_in(chunk):
             copy.wait()
         for step in range(steps):
@@ -183,6 +185,8 @@
                 gated_ref[rows, lanes] = gated
                 pair_ref[0, local, lanes] = key_two_ref[rows, lanes] * gated
                 pair_ref[1, local, lanes] = cotangent_ref[rows, lanes] * query_two_ref[rows, lanes]
+
+    def turn(chunk, pair_ref):
         product_two = turned(pair_ref[0], unit)
         grad_inner_two = turned(pair_ref[1], unit)
         for step in range(steps):
@@ -190,44 +194,83 @@
             local = slice(step * BLOCK, (step + 1) * BLOCK)
             product_ref[:, rows_of(index + 1, GROUP), :] = product_two[:, :, local]
             turned_ref[:, rows_of(index, GROUP), :] = grad_inner_two[:, :, local]
+
+    def forward_pair(count, _):
+        chunk = 2 * count
+        for place in range(2):
+
+            @pl.when(chunk + AHEAD + place < chunk_count)
+            def _():
+                start_in(chunk + AHEAD + place)
+
+        turn(chunk, even_ref)
+        forward(chunk + 1, odd_ref)
+        turn(chunk + 1, odd_ref)
+        forward(chunk + 2, even_ref)
         return 0
 
-    lax.fori_loop(0, chunk_count, forward, 0)
+    forward(0, even_ref)
+    lax.fori_loop(0, chunk_count // 2 - 1, forward_pair, 0)
+    turn(chunk_count - 2, even_ref)
+    forward(chunk_count - 1, odd_ref)
+    turn(chunk_count - 1, odd_ref)
 
     flip_row = lax.broadcasted_iota(jnp.int32, (BLOCK, BLOCK), 0)
     flip_lane = lax.broadcasted_iota(jnp.int32, (BLOCK, BLOCK), 1)
     flip = narrowed(widened(flip_row + flip_lane == BLOCK - 1))
     medium_scale = 1.0 / math.sqrt(sequence_total * GROUP)
-    for group in range(group_count):
-        bands = upper_lower(widened(medium_ref[group : group + 1]))
-        window = jnp.concatenate(
-            [turned_ref[group, :span], turned_ref[group, GROUP : GROUP + span]], axis=1
-        )
-        back_ref[group] = narrowed(dotted(window, bands, ((1,), (1,))))
-        earlier = jnp.concatenate([product_ref[group, :span], product_ref[group, GROUP:]], axis=1)
-        causal = jnp.concatenate([bands[:, BLOCK:], bands[:, :BLOCK]], axis=0)
-        ahead_ref[group] = narrowed(dotted(earlier, causal, ((1,), (0,))))
-        flipped = narrowed(dotted(flip, product_ref[group, GROUP:], ((1,), (1,))))
-        pairs = dotted(flipped, window, ((1,), (0,)))
-        pairs = pltpu.roll(pairs, BLOCK + 1, 1, stride=1, stride_axis=0)
-        line = jnp.sum(pairs[:, :BLOCK], axis=0, keepdims=True) * medium_scale
-        half, row = group * GROUP // LANES, RIM + group % (LANES // GROUP)
-        parts_ref[:, row : row + 1, half * LANES : (half + 1) * LANES] = jnp.broadcast_to(
-            line[None], (parts_ref.shape[0], 1, LANES)
-        )
-
+    batch = 4
+
+    def medium_batch(turn, _):
+        groups = [turn * batch + place for place in range(batch)]
+        bands = [upper_lower(coefs_ref[pl.ds(group, 1)]) for group in groups]
+        flipped = [
+            narrowed(dotted(flip, product_ref[group, GROUP:], ((1,), (1,)))) for group in groups
+        ]
+        windows = [
+            jnp.concatenate(
+                [turned_ref[group, :span], turned_ref[group, GROUP : GROUP + span]], axis=1
+            )
+            for group in groups
+        ]
+        pairs = [dotted(left, view, ((1,), (0,))) for left, view in zip(flipped, windows)]
+        backs = [
+            narrowed(dotted(view, band, ((1,), (1,)))) for view, band in zip(windows, bands)
+        ]
+        aheads = []
+        for group, band in zip(groups, bands):
+            earlier = jnp.concatenate([product_ref[group, :span], product_ref[group, GROUP:]], axis=1)
+            causal = jnp.concatenate([band[:, BLOCK:], band[:, :BLOCK]], axis=0)
+            aheads.append(narrowed(dotted(earlier, causal, ((1,), (0,)))))
+        for group, back, ahead in zip(groups, backs, aheads):
+            back_ref[group] = back
+            ahead_ref[group] = ahead
+        for group, pair in zip(groups, pairs):
+            pair = pltpu.roll(pair, BLOCK + 1, 1, stride=1, stride_axis=0)
+            lines_ref[pl.ds(group, 1)] = (
+                jnp.sum(pair[:, :BLOCK], axis=0, keepdims=True) * medium_scale
+            )
+        return 0
+
+    lax.fori_loop(0, group_count // batch, medium_batch, 0)
     sums_ref[...] = jnp.zeros_like(sums_ref)
 
-    def backward(turn, _):
-        chunk = chunk_count - 1 - turn
+    def unturn(chunk, pair_ref):
+        for step in range(steps):
+            lines = rows_of(chunk * steps + step, GROUP)
+            local = slice(step * BLOCK, (step + 1) * BLOCK)
+            back = back_ref[:, lines, :].reshape(chan_count, BLOCK)
+            ahead = ahead_ref[:, lines, :].reshape(chan_count, BLOCK)
+            pair_ref[0, local] = narrowed(dotted(small_unit, back, ((1,), (1,))))
+            pair_ref[1, local] = narrowed(dotted(small_unit, ahead, ((1,), (1,))))
+
+    def backward(chunk, pair_ref):
         for step in reversed(range(steps)):
             index = chunk * steps + step
             rows = rows_of(index, BLOCK)
-            lines = rows_of(index, GROUP)
-            back = back_ref[:, lines, :].reshape(chan_count, BLOCK)
-            ahead = ahead_ref[:, lines, :].reshape(chan_count, BLOCK)
-            back = narrowed(dotted(small_unit, back, ((1,), (1,))))
-            ahead = narrowed(dotted(small_unit, ahead, ((1,), (1,))))
+            local = slice(step * BLOCK, (step + 1) * BLOCK)
+            back = pair_ref[0, local]
+            ahead = pair_ref[1, local]
             output_ref[rows] = query_two_ref[rows] * ahead
             query_two_grad_ref[rows] = cotangent_ref[rows] * ahead
             key_two_grad_ref[rows] = back * gated_ref[rows]
@@ -253,20 +296,30 @@
                 value_grad_ref[rows, lanes] = total * key_ref[rows, lanes]
         for copy in copies_out(chunk):
             copy.start()
+
+    def backward_pair(count, _):
+        chunk = chunk_count - 1 - 2 * count
+        unturn(chunk - 1, even_ref)
+        backward(chunk, odd_ref)
+        unturn(chunk - 2, odd_ref)
+        backward(chunk - 1, even_ref)
         return 0
 
-    lax.fori_loop(0, chunk_count, backward, 0)
+    unturn(chunk_count - 1, odd_ref)
+    lax.fori_loop(0, chunk_count // 2 - 1, backward_pair, 0)
+    unturn(0, even_ref)
+    backward(1, odd_ref)
+    backward(0, even_ref)
 
     short_scale = 1.0 / math.sqrt(sequence_total)
+    per_half = LANES // GROUP
     for half in range(halves):
         lines = [
             jnp.sum(sums_ref[half, shift_by], axis=0, keepdims=True) * short_scale
             for shift_by in range(SE_TAPS)
         ]
-        lines = jnp.concatenate(lines + [jnp.zeros_like(lines[0])], axis=0)
-        parts_ref[:, :RIM, half * LANES : (half + 1) * LANES] = jnp.broadcast_to(
-            lines[None], (parts_ref.shape[0], RIM, LANES)
-        )
+        lines += [jnp.zeros_like(lines[0]), lines_ref[half * per_half : (half + 1) * per_half]]
+        parts_ref[:, half * LANES : (half + 1) * LANES] = jnp.concatenate(lines, axis=0)
 
     def wait_out(chunk, _):
         for copy in copies_out(chunk):
@@ -287,8 +340,8 @@
             medium_ref[first : first + groups] = piece[RIM:, half * LANES : (half + 1) * LANES]
 
 
-def params():
-    return pltpu.CompilerParams(vmem_limit_bytes=VMEM_LIMIT)
+def params(limit=VMEM_LIMIT):
+    return pltpu.CompilerParams(vmem_limit_bytes=limit)
 
 
 def cost(flops, size):
@@ -354,16 +407,17 @@
             grid=(1,),
             in_specs=[any_spec] * 6 + [short_spec, medium_spec, halo_spec, halo_spec],
             out_specs=(any_spec,) * 6
-            + (pl.BlockSpec((seq_count, 2 * RIM, chan_count), lambda i, at: (0, 0, 0)),),
+            + (pl.BlockSpec((2 * RIM, chan_count), lambda i, at: (0, 0)),),
             scratch_shapes=[stream] * 14
             + [pltpu.VMEM((halves, row_count + RIM, LANES), jnp.float32)] * 2
-            + [pltpu.VMEM((2, CHUNK, chan_count), jnp.bfloat16)]
+            + [pltpu.VMEM((2, CHUNK, chan_count), jnp.bfloat16)] * 2
             + [turned_stream] * 2
             + [pltpu.VMEM((group_count, lines - GROUP, BLOCK), jnp.bfloat16)] * 2
+            + [pltpu.VMEM((group_count, MR_TAPS), jnp.float32)] * 2
             + [pltpu.VMEM((halves, SE_TAPS, RIM, LANES), jnp.float32)]
             + [pltpu.SemaphoreType.DMA((6, row_count // CHUNK))] * 2,
         ),
-        out_shape=(wide,) * 6 + (sds((seq_count, 2 * RIM, chan_count), jnp.float32),),
+        out_shape=(wide,) * 6 + (sds((2 * RIM, chan_count), jnp.float32),),
         compiler_params=params(),
         cost_estimate=cost(100 * row_count * chan_count, 12 * size),
         name="main",
@@ -382,7 +436,12 @@
         parts,
     ) = results
 
-    sums = narrowed(jnp.sum(lax.all_to_all(parts, "seq", 0, 0), axis=0))
+    distance = 1
+    while distance < seq_count:
+        swaps = [(place, place ^ distance) for place in range(seq_count)]
+        parts = parts + lax.ppermute(parts, "seq", swaps)
+        distance *= 2
+    sums = narrowed(parts)
     copies = jnp.broadcast_to(sums[None], (lax.axis_size("grp"), *sums.shape))
     table = lax.all_to_all(copies, "grp", 0, 0)
     short_grad, medium_grad = pl.pallas_call(
@@ -391,7 +450,7 @@
             sds(short_filter.shape, jnp.float32),
             sds(medium_filter.shape, jnp.float32),
         ),
-        compiler_params=params(),
+        compiler_params=params(16 * 1024 * 1024),
         name="unpack",
     )(table)
     return (

time: 65.5 us -> 65.8 us (level)
  blocking collectives: 36.9 us -> 15.6 us
  starting transfers between devices: 3.02 us -> 16.1 us
  waiting for transfers between devices: 5.11 us -> 13 us
  other arithmetic: 0.01 us -> 0.73 us
    all_to_all x1 -> x0, blocking collectives: 20.5 us -> none  [per_device(): sums = narrowed(jnp.sum(lax.all_to_all(parts, 'seq', 0, 0), axis=0))]
    ppermute x0 -> x3, starting transfers between devices: none -> 13.1 us  [per_device(): parts = parts + lax.ppermute(parts, 'seq', swaps)]
    ppermute x0 -> x3, waiting for transfers between devices: none -> 7.92 us  [per_device(): parts = parts + lax.ppermute(parts, 'seq', swaps)]
    pallas_call x1, Pallas kernels: 1.77 us -> 0.82 us  [per_device(): pl.pallas_call(unpack_kernel, out_shape=(sds(short_filter.shape, jnp.floa...]
    add x0 -> x2, other arithmetic: none -> 0.73 us  [per_device(): parts = parts + lax.ppermute(parts, 'seq', swaps)]
    all_to_all x1, blocking collectives: 16.3 us -> 15.6 us  [per_device(): table = lax.all_to_all(copies, 'grp', 0, 0)]
  transfers between devices with their start and end apart: 2 -> 5, of which waited for: 1 -> 4; matrix products, arithmetic and copies ran while one was open for 0% -> 0% of each run, Pallas kernels for 0% -> 0%
where the time goes in v5:
time: 65.8 us; the launch traced here: 65.1 us
  Pallas kernels  18.2 us (28%)
  starting transfers between devices  16.1 us (24%)
  blocking collectives  15.6 us (24%)
  waiting for transfers between devices  13 us (20%)
  other arithmetic  0.73 us (1%)
  between operations  0.69 us (1%)
  local copies, waits for them, and re-layouts  0.66 us (1%)
    all_to_all x1, blocking collectives, per_device(): table = lax.all_to_all(copies, 'grp', 0, 0)  15.6 us
    pallas_call x1, Pallas kernels, per_device(): pl.pallas_call(main_kernel, grid_spec=pltpu.PrefetchScalarGridSpec(num_sc...  15.1 us
    ppermute x3, starting transfers between devices, per_device(): parts = parts + lax.ppermute(parts, 'seq', swaps)  13.1 us
    ppermute x3, waiting for transfers between devices, per_device(): parts = parts + lax.ppermute(parts, 'seq', swaps)  7.92 us
    ppermute x2, waiting for transfers between devices, passed_along(): lax.ppermute(value, axis, [(source, source + steps) for source in range(f...  5.1 us
    ppermute x2, starting transfers between devices, passed_along(): lax.ppermute(value, axis, [(source, source + steps) for source in range(f...  3.02 us
    pallas_call x1, Pallas kernels, per_device(): pl.pallas_call(rims_kernel, grid_spec=pltpu.PrefetchScalarGridSpec(num_sc...  2.3 us
  transfers between devices with their start and end apart: 5, of which 4 were waited for; matrix products, arithmetic and copies ran while one was open for 0% of the time, Pallas kernels for 0%

profile of v5, /device:TPU:2, one launch (start us, length us, event | category | flops | bytes accessed | tf_op | source)
XLA Modules:
  0.0 65.1 jit_solution(7533687879512717396)
XLA Ops:
  0.6 2.3 %rims.1 = (bf16[144,256]{1,0:T(8,128)(2,1)}, bf16[144,256]{1,0:T(8,128)(2,1)}) custom-call(s32[1]{0:T(128)} %bitcast.place_ref, bf16[2048,256]{1,0:T(8,128)(2,1)} %key_any.1, bf16[2048,256]{1,0:T(8,128)(2,1)} %value_any.1, bf16[2048,256]{1,0:T(8,128)(2,1)} %query_any.1, bf16[2048,256]{1,0:T(8,128)(2,1)} %key_two_any.1, bf16[2048,256]{1,0:T(8,128)(2,1)} %cotangent_any.1, ...), custom_call_target="tpu_custom_call" | custom-call | flops 12582912 | bytes 1048576 | tf_op jit(solution)/shard_map/rims/pallas_call | solution.py:376
  2.9 1.7 %collective-permute-start = (bf16[144,256]{1,0:T(8,128)(2,1)}, bf16[144,256]{1,0:T(8,128)(2,1)S(1)}, u32[]{:S(2)}, u32[]{:S(2)}) collective-permute-start(bf16[144,256]{1,0:T(8,128)(2,1)} %get-tuple-element.19), channel_id=1, source_target_pairs={{0,32},{32,64},{64,96},{96,128},{128,160},{160,192},{192,224},{1,3... | collective-permute-start | bytes 221192 | tf_op jit(solution)/shard_map/ppermute | solution.py:34
  4.7 1.3 %collective-permute-start.1 = (bf16[144,256]{1,0:T(8,128)(2,1)}, bf16[144,256]{1,0:T(8,128)(2,1)S(1)}, u32[]{:S(2)}, u32[]{:S(2)}) collective-permute-start(bf16[144,256]{1,0:T(8,128)(2,1)} %get-tuple-element.20), channel_id=1, source_target_pairs={{32,0},{64,32},{96,64},{128,96},{160,128},{192,160},{224,192},{33,... | collective-permute-start | bytes 221192 | tf_op jit(solution)/shard_map/ppermute | solution.py:34
  6.0 0.0 collective-permute-done.tail_ref
  6.0 0.0 copy-start
  6.0 5.1 %collective-permute-done.1.head_ref = bf16[144,256]{1,0:T(8,128)(2,1)S(1)} collective-permute-done((bf16[144,256]{1,0:T(8,128)(2,1)}, bf16[144,256]{1,0:T(8,128)(2,1)S(1)}, u32[]{:S(2)}, u32[]{:S(2)}) %collective-permute-start.1) | collective-permute-done | bytes 73760 | tf_op jit(solution)/shard_map/ppermute | solution.py:34
  11.1 0.0 copy-done
  11.1 0.0 copy-start.1
  11.1 0.6 copy-done.1
  11.7 15.1 %main.1 = (bf16[2048,256]{1,0:T(8,128)(2,1)}, bf16[2048,256]{1,0:T(8,128)(2,1)}, bf16[2048,256]{1,0:T(8,128)(2,1)}, bf16[2048,256]{1,0:T(8,128)(2,1)}, bf16[2048...) custom-call(s32[1]{0:T(128)} %bitcast.place_ref, bf16[2048,256]{1,0:T(8,128)(2,1)} %query_any.1, ...), custom_call_target="tpu_custom_call" | custom-call | flops 52428800 | bytes 12582912 | tf_op jit(solution)/shard_map/main/pallas_call | solution.py:403
  26.8 4.0 %collective-permute-start.2 = (f32[16,256]{1,0:T(8,128)}, f32[16,256]{1,0:T(8,128)S(1)}, u32[]{:S(2)}, u32[]{:S(2)}) collective-permute-start(f32[16,256]{1,0:T(8,128)} %get-tuple-element.27), channel_id=1, source_target_pairs={{0,32},{32,0},{64,96},{96,64},{128,160},{160,128},{192,224},{224,1... | collective-permute-start | bytes 49160 | tf_op jit(solution)/shard_map/ppermute | solution.py:442
  30.8 1.0 %collective-permute-done.2 = f32[16,256]{1,0:T(8,128)S(1)} collective-permute-done((f32[16,256]{1,0:T(8,128)}, f32[16,256]{1,0:T(8,128)S(1)}, u32[]{:S(2)}, u32[]{:S(2)}) %collective-permute-start.2) | collective-permute-done | bytes 16416 | tf_op jit(solution)/shard_map/ppermute | solution.py:442
  31.9 0.7 %add.9 = f32[16,256]{1,0:T(8,128)S(1)} add(f32[16,256]{1,0:T(8,128)} %get-tuple-element.27, f32[16,256]{1,0:T(8,128)S(1)} %collective-permute-done.2) | non-fusion elementwise | flops 4096 | bytes 49152 | tf_op jit(solution)/shard_map/add | solution.py:442
  32.6 6.5 %collective-permute-start.3 = (f32[16,256]{1,0:T(8,128)S(1)}, f32[16,256]{1,0:T(8,128)S(1)}, u32[]{:S(2)}, u32[]{:S(2)}) collective-permute-start(f32[16,256]{1,0:T(8,128)S(1)} %add.9), channel_id=1, source_target_pairs={{0,64},{32,96},{64,0},{96,32},{128,192},{160,224},{192,128},{224,1... | collective-permute-start | bytes 49160 | tf_op jit(solution)/shard_map/ppermute | solution.py:442
  39.1 1.8 %collective-permute-done.3 = f32[16,256]{1,0:T(8,128)S(1)} collective-permute-done((f32[16,256]{1,0:T(8,128)S(1)}, f32[16,256]{1,0:T(8,128)S(1)}, u32[]{:S(2)}, u32[]{:S(2)}) %collective-permute-start.3) | collective-permute-done | bytes 16416 | tf_op jit(solution)/shard_map/ppermute | solution.py:442
  40.9 2.7 %collective-permute-start.4 = (f32[16,256]{1,0:T(8,128)S(1)}, f32[16,256]{1,0:T(8,128)S(1)}, u32[]{:S(2)}, u32[]{:S(2)}) collective-permute-start(f32[16,256]{1,0:T(8,128)S(1)} %add.10), channel_id=1, source_target_pairs={{0,128},{32,160},{64,192},{96,224},{128,0},{160,32},{192,64},{224,... | collective-permute-start | bytes 49160 | tf_op jit(solution)/shard_map/ppermute | solution.py:442
  43.5 5.1 %collective-permute-done.4 = f32[16,256]{1,0:T(8,128)S(1)} collective-permute-done((f32[16,256]{1,0:T(8,128)S(1)}, f32[16,256]{1,0:T(8,128)S(1)}, u32[]{:S(2)}, u32[]{:S(2)}) %collective-permute-start.4) | collective-permute-done | bytes 16416 | tf_op jit(solution)/shard_map/ppermute | solution.py:442
  48.7 15.6 %all_to_all.5.table_ref = bf16[32,16,256]{2,1,0:T(8,128)(2,1)S(1)} all-to-all(bf16[32,16,256]{2,1,0:T(8,128)(2,1)S(1)} %broadcast_in_dim.2), channel_id=1, replica_groups=mesh['seq'=8,'grp'=32] {'grp'}, dimensions={0} | all-to-all | bytes 524288 | tf_op jit(solution)/shard_map/all_to_all | solution.py:446
  64.3 0.8 %unpack.1 = (f32[7,8192]{1,0:T(8,128)}, f32[512,128]{1,0:T(8,128)}) custom-call(bf16[32,16,256]{2,1,0:T(8,128)(2,1)S(1)} %all_to_all.5.table_ref), custom_call_target="tpu_custom_call" | custom-call | tf_op jit(solution)/shard_map/unpack/pallas_call | solution.py:447
  (3 shorter events, 0.0 us)
Async XLA Ops:
  2.9 3.0 %collective-permute-start = (bf16[144,256]{1,0:T(8,128)(2,1)}, bf16[144,256]{1,0:T(8,128)(2,1)S(1)}, u32[]{:S(2)}, u32[]{:S(2)}) collective-permute-start(bf16[144,256]{1,0:T(8,128)(2,1)} %get-tuple-element.19), channel_id=1, source_target_pairs={{0,32},{32,64},{64,96},{96,128},{128,160},{160,192},{192,224},{1,3... | collective-permute-start | bytes 221192 | tf_op jit(solution)/shard_map/ppermute | solution.py:34
  4.7 6.4 %collective-permute-start.1 = (bf16[144,256]{1,0:T(8,128)(2,1)}, bf16[144,256]{1,0:T(8,128)(2,1)S(1)}, u32[]{:S(2)}, u32[]{:S(2)}) collective-permute-start(bf16[144,256]{1,0:T(8,128)(2,1)} %get-tuple-element.20), channel_id=1, source_target_pairs={{32,0},{64,32},{96,64},{128,96},{160,128},{192,160},{224,192},{33,... | collective-permute-start | bytes 221192 | tf_op jit(solution)/shard_map/ppermute | solution.py:34
  6.0 5.1 %copy-start = (bf16[144,256]{1,0:T(8,128)(2,1)}, bf16[144,256]{1,0:T(8,128)(2,1)S(1)}, u32[]{:S(2)}) copy-start(bf16[144,256]{1,0:T(8,128)(2,1)S(1)} %collective-permute-done.tail_ref) | copy-start | bytes 221188
  11.1 0.6 copy-start.1
  26.8 5.0 %collective-permute-start.2 = (f32[16,256]{1,0:T(8,128)}, f32[16,256]{1,0:T(8,128)S(1)}, u32[]{:S(2)}, u32[]{:S(2)}) collective-permute-start(f32[16,256]{1,0:T(8,128)} %get-tuple-element.27), channel_id=1, source_target_pairs={{0,32},{32,0},{64,96},{96,64},{128,160},{160,128},{192,224},{224,1... | collective-permute-start | bytes 49160 | tf_op jit(solution)/shard_map/ppermute | solution.py:442
  32.6 8.3 %collective-permute-start.3 = (f32[16,256]{1,0:T(8,128)S(1)}, f32[16,256]{1,0:T(8,128)S(1)}, u32[]{:S(2)}, u32[]{:S(2)}) collective-permute-start(f32[16,256]{1,0:T(8,128)S(1)} %add.9), channel_id=1, source_target_pairs={{0,64},{32,96},{64,0},{96,32},{128,192},{160,224},{192,128},{224,1... | collective-permute-start | bytes 49160 | tf_op jit(solution)/shard_map/ppermute | solution.py:442
  40.9 7.7 %collective-permute-start.4 = (f32[16,256]{1,0:T(8,128)S(1)}, f32[16,256]{1,0:T(8,128)S(1)}, u32[]{:S(2)}, u32[]{:S(2)}) collective-permute-start(f32[16,256]{1,0:T(8,128)S(1)} %add.10), channel_id=1, source_target_pairs={{0,128},{32,160},{64,192},{96,224},{128,0},{160,32},{192,64},{224,... | collective-permute-start | bytes 49160 | tf_op jit(solution)/shard_map/ppermute | solution.py:442

commit v6 on v5

--- a/solution.py
+++ b/solution.py
@@ -46,10 +46,26 @@
     return total
 
 
+def moved_lanes(tile, shift_by):
+    return pltpu.roll(tile, shift_by, 1) if shift_by else tile
+
+
 def upper_lower(coefs):
     line = jnp.concatenate([coefs, jnp.zeros_like(coefs)], axis=1)
-    table = jnp.broadcast_to(line, (BLOCK, 2 * BLOCK))
-    return narrowed(pltpu.roll(table, 0, 1, stride=1, stride_axis=0))
+    tile = jnp.broadcast_to(line, (RIM, 2 * BLOCK))
+    tile = pltpu.roll(tile, 0, 1, stride=1, stride_axis=0)
+    return narrowed(
+        jnp.concatenate([moved_lanes(tile, first) for first in range(0, BLOCK, RIM)], axis=0)
+    )
+
+
+def diagonal_sums(pairs):
+    total = sum(
+        moved_lanes(pairs[first : first + RIM], (BLOCK + 1 + first) % (2 * BLOCK))
+        for first in range(0, BLOCK, RIM)
+    )
+    total = pltpu.roll(total, 0, 1, stride=1, stride_axis=0)
+    return jnp.sum(total[:, :BLOCK], axis=0, keepdims=True)
 
 
 def dotted(left, right, dims):
@@ -246,10 +262,7 @@
             back_ref[group] = back
             ahead_ref[group] = ahead
         for group, pair in zip(groups, pairs):
-            pair = pltpu.roll(pair, BLOCK + 1, 1, stride=1, stride_axis=0)
-            lines_ref[pl.ds(group, 1)] = (
-                jnp.sum(pair[:, :BLOCK], axis=0, keepdims=True) * medium_scale
-            )
+            lines_ref[pl.ds(group, 1)] = diagonal_sums(pair) * medium_scale
         return 0
 
     lax.fori_loop(0, group_count // batch, medium_batch, 0)

time: 65.8 us -> 65.8 us (level)
  no operation moved by 1% of the time
where the time goes in v6:
time: 65.8 us; the launch traced here: 65.1 us
  Pallas kernels  18.3 us (28%)
  starting transfers between devices  16.1 us (24%)
  blocking collectives  15.6 us (24%)
  waiting for transfers between devices  13 us (20%)
  other arithmetic  0.73 us (1%)
  between operations  0.69 us (1%)
  local copies, waits for them, and re-layouts  0.66 us (1%)
    all_to_all x1, blocking collectives, per_device(): table = lax.all_to_all(copies, 'grp', 0, 0)  15.6 us
    pallas_call x1, Pallas kernels, per_device(): pl.pallas_call(main_kernel, grid_spec=pltpu.PrefetchScalarGridSpec(num_sc...  15.1 us
    ppermute x3, starting transfers between devices, per_device(): parts = parts + lax.ppermute(parts, 'seq', swaps)  13.1 us
    ppermute x3, waiting for transfers between devices, per_device(): parts = parts + lax.ppermute(parts, 'seq', swaps)  7.92 us
    ppermute x2, waiting for transfers between devices, passed_along(): lax.ppermute(value, axis, [(source, source + steps) for source in range(f...  5.1 us
    ppermute x2, starting transfers between devices, passed_along(): lax.ppermute(value, axis, [(source, source + steps) for source in range(f...  3.02 us
    pallas_call x1, Pallas kernels, per_device(): pl.pallas_call(rims_kernel, grid_spec=pltpu.PrefetchScalarGridSpec(num_sc...  2.3 us
  transfers between devices with their start and end apart: 5, of which 4 were waited for; matrix products, arithmetic and copies ran while one was open for 0% of the time, Pallas kernels for 0%

profile of v6, /device:TPU:2, one launch (start us, length us, event | category | flops | bytes accessed | tf_op | source)
XLA Modules:
  0.0 65.1 jit_solution(15201053651474997950)
XLA Ops:
  0.6 2.3 %rims.1 = (bf16[144,256]{1,0:T(8,128)(2,1)}, bf16[144,256]{1,0:T(8,128)(2,1)}) custom-call(s32[1]{0:T(128)} %bitcast.place_ref, bf16[2048,256]{1,0:T(8,128)(2,1)} %key_any.1, bf16[2048,256]{1,0:T(8,128)(2,1)} %value_any.1, bf16[2048,256]{1,0:T(8,128)(2,1)} %query_any.1, bf16[2048,256]{1,0:T(8,128)(2,1)} %key_two_any.1, bf16[2048,256]{1,0:T(8,128)(2,1)} %cotangent_any.1, ...), custom_call_target="tpu_custom_call" | custom-call | flops 12582912 | bytes 1048576 | tf_op jit(solution)/shard_map/rims/pallas_call | solution.py:389
  2.9 1.7 %collective-permute-start = (bf16[144,256]{1,0:T(8,128)(2,1)}, bf16[144,256]{1,0:T(8,128)(2,1)S(1)}, u32[]{:S(2)}, u32[]{:S(2)}) collective-permute-start(bf16[144,256]{1,0:T(8,128)(2,1)} %get-tuple-element.19), channel_id=1, source_target_pairs={{0,32},{32,64},{64,96},{96,128},{128,160},{160,192},{192,224},{1,3... | collective-permute-start | bytes 221192 | tf_op jit(solution)/shard_map/ppermute | solution.py:34
  4.7 1.3 %collective-permute-start.1 = (bf16[144,256]{1,0:T(8,128)(2,1)}, bf16[144,256]{1,0:T(8,128)(2,1)S(1)}, u32[]{:S(2)}, u32[]{:S(2)}) collective-permute-start(bf16[144,256]{1,0:T(8,128)(2,1)} %get-tuple-element.20), channel_id=1, source_target_pairs={{32,0},{64,32},{96,64},{128,96},{160,128},{192,160},{224,192},{33,... | collective-permute-start | bytes 221192 | tf_op jit(solution)/shard_map/ppermute | solution.py:34
  6.0 0.0 collective-permute-done.tail_ref
  6.0 0.0 copy-start
  6.0 5.1 %collective-permute-done.1.head_ref = bf16[144,256]{1,0:T(8,128)(2,1)S(1)} collective-permute-done((bf16[144,256]{1,0:T(8,128)(2,1)}, bf16[144,256]{1,0:T(8,128)(2,1)S(1)}, u32[]{:S(2)}, u32[]{:S(2)}) %collective-permute-start.1) | collective-permute-done | bytes 73760 | tf_op jit(solution)/shard_map/ppermute | solution.py:34
  11.1 0.0 copy-done
  11.1 0.0 copy-start.1
  11.1 0.6 copy-done.1
  11.7 15.1 %main.1 = (bf16[2048,256]{1,0:T(8,128)(2,1)}, bf16[2048,256]{1,0:T(8,128)(2,1)}, bf16[2048,256]{1,0:T(8,128)(2,1)}, bf16[2048,256]{1,0:T(8,128)(2,1)}, bf16[2048...) custom-call(s32[1]{0:T(128)} %bitcast.place_ref, bf16[2048,256]{1,0:T(8,128)(2,1)} %query_any.1, ...), custom_call_target="tpu_custom_call" | custom-call | flops 52428800 | bytes 12582912 | tf_op jit(solution)/shard_map/main/pallas_call | solution.py:416
  26.9 4.0 %collective-permute-start.2 = (f32[16,256]{1,0:T(8,128)}, f32[16,256]{1,0:T(8,128)S(1)}, u32[]{:S(2)}, u32[]{:S(2)}) collective-permute-start(f32[16,256]{1,0:T(8,128)} %get-tuple-element.27), channel_id=1, source_target_pairs={{0,32},{32,0},{64,96},{96,64},{128,160},{160,128},{192,224},{224,1... | collective-permute-start | bytes 49160 | tf_op jit(solution)/shard_map/ppermute | solution.py:455
  30.9 1.0 %collective-permute-done.2 = f32[16,256]{1,0:T(8,128)S(1)} collective-permute-done((f32[16,256]{1,0:T(8,128)}, f32[16,256]{1,0:T(8,128)S(1)}, u32[]{:S(2)}, u32[]{:S(2)}) %collective-permute-start.2) | collective-permute-done | bytes 16416 | tf_op jit(solution)/shard_map/ppermute | solution.py:455
  31.9 0.7 %add.9 = f32[16,256]{1,0:T(8,128)S(1)} add(f32[16,256]{1,0:T(8,128)} %get-tuple-element.27, f32[16,256]{1,0:T(8,128)S(1)} %collective-permute-done.2) | non-fusion elementwise | flops 4096 | bytes 49152 | tf_op jit(solution)/shard_map/add | solution.py:455
  32.6 6.5 %collective-permute-start.3 = (f32[16,256]{1,0:T(8,128)S(1)}, f32[16,256]{1,0:T(8,128)S(1)}, u32[]{:S(2)}, u32[]{:S(2)}) collective-permute-start(f32[16,256]{1,0:T(8,128)S(1)} %add.9), channel_id=1, source_target_pairs={{0,64},{32,96},{64,0},{96,32},{128,192},{160,224},{192,128},{224,1... | collective-permute-start | bytes 49160 | tf_op jit(solution)/shard_map/ppermute | solution.py:455
  39.1 1.8 %collective-permute-done.3 = f32[16,256]{1,0:T(8,128)S(1)} collective-permute-done((f32[16,256]{1,0:T(8,128)S(1)}, f32[16,256]{1,0:T(8,128)S(1)}, u32[]{:S(2)}, u32[]{:S(2)}) %collective-permute-start.3) | collective-permute-done | bytes 16416 | tf_op jit(solution)/shard_map/ppermute | solution.py:455
  40.9 2.7 %collective-permute-start.4 = (f32[16,256]{1,0:T(8,128)S(1)}, f32[16,256]{1,0:T(8,128)S(1)}, u32[]{:S(2)}, u32[]{:S(2)}) collective-permute-start(f32[16,256]{1,0:T(8,128)S(1)} %add.10), channel_id=1, source_target_pairs={{0,128},{32,160},{64,192},{96,224},{128,0},{160,32},{192,64},{224,... | collective-permute-start | bytes 49160 | tf_op jit(solution)/shard_map/ppermute | solution.py:455
  43.6 5.1 %collective-permute-done.4 = f32[16,256]{1,0:T(8,128)S(1)} collective-permute-done((f32[16,256]{1,0:T(8,128)S(1)}, f32[16,256]{1,0:T(8,128)S(1)}, u32[]{:S(2)}, u32[]{:S(2)}) %collective-permute-start.4) | collective-permute-done | bytes 16416 | tf_op jit(solution)/shard_map/ppermute | solution.py:455
  48.7 15.6 %all_to_all.5.table_ref = bf16[32,16,256]{2,1,0:T(8,128)(2,1)S(1)} all-to-all(bf16[32,16,256]{2,1,0:T(8,128)(2,1)S(1)} %broadcast_in_dim.2), channel_id=1, replica_groups=mesh['seq'=8,'grp'=32] {'grp'}, dimensions={0} | all-to-all | bytes 524288 | tf_op jit(solution)/shard_map/all_to_all | solution.py:459
  64.3 0.8 %unpack.1 = (f32[7,8192]{1,0:T(8,128)}, f32[512,128]{1,0:T(8,128)}) custom-call(bf16[32,16,256]{2,1,0:T(8,128)(2,1)S(1)} %all_to_all.5.table_ref), custom_call_target="tpu_custom_call" | custom-call | tf_op jit(solution)/shard_map/unpack/pallas_call | solution.py:460
  (3 shorter events, 0.0 us)
Async XLA Ops:
  2.9 3.0 %collective-permute-start = (bf16[144,256]{1,0:T(8,128)(2,1)}, bf16[144,256]{1,0:T(8,128)(2,1)S(1)}, u32[]{:S(2)}, u32[]{:S(2)}) collective-permute-start(bf16[144,256]{1,0:T(8,128)(2,1)} %get-tuple-element.19), channel_id=1, source_target_pairs={{0,32},{32,64},{64,96},{96,128},{128,160},{160,192},{192,224},{1,3... | collective-permute-start | bytes 221192 | tf_op jit(solution)/shard_map/ppermute | solution.py:34
  4.7 6.4 %collective-permute-start.1 = (bf16[144,256]{1,0:T(8,128)(2,1)}, bf16[144,256]{1,0:T(8,128)(2,1)S(1)}, u32[]{:S(2)}, u32[]{:S(2)}) collective-permute-start(bf16[144,256]{1,0:T(8,128)(2,1)} %get-tuple-element.20), channel_id=1, source_target_pairs={{32,0},{64,32},{96,64},{128,96},{160,128},{192,160},{224,192},{33,... | collective-permute-start | bytes 221192 | tf_op jit(solution)/shard_map/ppermute | solution.py:34
  6.0 5.1 %copy-start = (bf16[144,256]{1,0:T(8,128)(2,1)}, bf16[144,256]{1,0:T(8,128)(2,1)S(1)}, u32[]{:S(2)}) copy-start(bf16[144,256]{1,0:T(8,128)(2,1)S(1)} %collective-permute-done.tail_ref) | copy-start | bytes 221188
  11.1 0.6 copy-start.1
  26.9 5.0 %collective-permute-start.2 = (f32[16,256]{1,0:T(8,128)}, f32[16,256]{1,0:T(8,128)S(1)}, u32[]{:S(2)}, u32[]{:S(2)}) collective-permute-start(f32[16,256]{1,0:T(8,128)} %get-tuple-element.27), channel_id=1, source_target_pairs={{0,32},{32,0},{64,96},{96,64},{128,160},{160,128},{192,224},{224,1... | collective-permute-start | bytes 49160 | tf_op jit(solution)/shard_map/ppermute | solution.py:455
  32.6 8.3 %collective-permute-start.3 = (f32[16,256]{1,0:T(8,128)S(1)}, f32[16,256]{1,0:T(8,128)S(1)}, u32[]{:S(2)}, u32[]{:S(2)}) collective-permute-start(f32[16,256]{1,0:T(8,128)S(1)} %add.9), channel_id=1, source_target_pairs={{0,64},{32,96},{64,0},{96,32},{128,192},{160,224},{192,128},{224,1... | collective-permute-start | bytes 49160 | tf_op jit(solution)/shard_map/ppermute | solution.py:455
  40.9 7.7 %collective-permute-start.4 = (f32[16,256]{1,0:T(8,128)S(1)}, f32[16,256]{1,0:T(8,128)S(1)}, u32[]{:S(2)}, u32[]{:S(2)}) collective-permute-start(f32[16,256]{1,0:T(8,128)S(1)} %add.10), channel_id=1, source_target_pairs={{0,128},{32,160},{64,192},{96,224},{128,0},{160,32},{192,64},{224,... | collective-permute-start | bytes 49160 | tf_op jit(solution)/shard_map/ppermute | solution.py:455

commit v7 on v6

--- a/solution.py
+++ b/solution.py
@@ -15,7 +15,8 @@
 LANES = 128
 RIM = 8
 CHUNK = 256
-AHEAD = 4
+LOADS = ((0, 256), (256, 256), (512, 512), (1024, 1024))
+SAVES = ((1536, 512), (1024, 512), (512, 512), (256, 256), (0, 256))
 HALO = 16
 VMEM_LIMIT = 63 * 1024 * 1024
 
@@ -147,26 +148,42 @@
         output_any, query_grad_any, key_grad_any, value_grad_any, query_two_grad_any, key_two_grad_any
     )
 
-    def copies_in(chunk):
-        rows = rows_of(chunk, CHUNK)
+    def copies_in(piece):
+        rows = pl.ds(*LOADS[piece])
         return [
-            pltpu.make_async_copy(source.at[rows], buffer.at[rows], in_sems.at[place, chunk])
+            pltpu.make_async_copy(source.at[rows], buffer.at[rows], in_sems.at[place, piece])
             for place, (source, buffer) in enumerate(zip(sources, buffers))
         ]
 
-    def copies_out(chunk):
-        rows = rows_of(chunk, CHUNK)
+    def copies_out(piece):
+        rows = pl.ds(*SAVES[piece])
         return [
-            pltpu.make_async_copy(result.at[rows], target.at[rows], out_sems.at[place, chunk])
+            pltpu.make_async_copy(result.at[rows], target.at[rows], out_sems.at[place, piece])
             for place, (result, target) in enumerate(zip(results, targets))
         ]
 
-    def start_in(chunk):
-        for copy in copies_in(chunk):
+    def at_chunk(chunk, pieces, act):
+        for piece, (first, _) in enumerate(pieces):
+            if isinstance(chunk, int):
+                if chunk * CHUNK == first:
+                    act(piece)
+            else:
+                pl.when(chunk * CHUNK == first)(functools.partial(act, piece))
+
+    def load(piece):
+        for copy in copies_in(piece):
             copy.start()
 
-    for chunk in range(min(AHEAD, chunk_count)):
-        start_in(chunk)
+    def loaded(piece):
+        for copy in copies_in(piece):
+            copy.wait()
+
+    def save(piece):
+        for copy in copies_out(piece):
+            copy.start()
+
+    for piece in range(len(LOADS)):
+        load(piece)
 
     coefs_ref[...] = widened(medium_ref[...])
     unit = identity(chan_count)
@@ -179,8 +196,7 @@
         later_ref[half, row_count:] = widened(head_ref[BLOCK:, lanes])[:RIM]
 
     def forward(chunk, pair_ref):
-        for copy in copies_in(chunk):
-            copy.wait()
+        at_chunk(chunk, LOADS, loaded)
         for step in range(steps):
             index = chunk * steps + step
             rows = rows_of(index, BLOCK)
@@ -213,12 +229,6 @@
 
     def forward_pair(count, _):
         chunk = 2 * count
-        for place in range(2):
-
-            @pl.when(chunk + AHEAD + place < chunk_count)
-            def _():
-                start_in(chunk + AHEAD + place)
-
         turn(chunk, even_ref)
         forward(chunk + 1, odd_ref)
         turn(chunk + 1, odd_ref)
@@ -307,8 +317,7 @@
                 total = narrowed(total)
                 key_grad_ref[rows, lanes] = total * value_ref[rows, lanes]
                 value_grad_ref[rows, lanes] = total * key_ref[rows, lanes]
-        for copy in copies_out(chunk):
-            copy.start()
+        at_chunk(chunk, SAVES, save)
 
     def backward_pair(count, _):
         chunk = chunk_count - 1 - 2 * count
@@ -334,12 +343,9 @@
         lines += [jnp.zeros_like(lines[0]), lines_ref[half * per_half : (half + 1) * per_half]]
         parts_ref[:, half * LANES : (half + 1) * LANES] = jnp.concatenate(lines, axis=0)
 
-    def wait_out(chunk, _):
-        for copy in copies_out(chunk):
+    for piece in range(len(SAVES)):
+        for copy in copies_out(piece):
             copy.wait()
-        return 0
-
-    lax.fori_loop(0, chunk_count, wait_out, 0)
 
 
 def unpack_kernel(table_ref, short_ref, medium_ref):
@@ -428,7 +434,10 @@
             + [pltpu.VMEM((group_count, lines - GROUP, BLOCK), jnp.bfloat16)] * 2
             + [pltpu.VMEM((group_count, MR_TAPS), jnp.float32)] * 2
             + [pltpu.VMEM((halves, SE_TAPS, RIM, LANES), jnp.float32)]
-            + [pltpu.SemaphoreType.DMA((6, row_count // CHUNK))] * 2,
+            + [
+                pltpu.SemaphoreType.DMA((6, len(LOADS))),
+                pltpu.SemaphoreType.DMA((6, len(SAVES))),
+            ],
         ),
         out_shape=(wide,) * 6 + (sds((2 * RIM, chan_count), jnp.float32),),
         compiler_params=params(),

time: 65.8 us -> 65.2 us (level)
  no operation moved by 1% of the time
where the time goes in v7:
time: 65.2 us; the launch traced here: 64.6 us
  Pallas kernels  17.7 us (27%)
  starting transfers between devices  16.1 us (25%)
  blocking collectives  15.6 us (24%)
  waiting for transfers between devices  13 us (20%)
  other arithmetic  0.73 us (1%)
  between operations  0.69 us (1%)
  local copies, waits for them, and re-layouts  0.66 us (1%)
    all_to_all x1, blocking collectives, per_device(): table = lax.all_to_all(copies, 'grp', 0, 0)  15.6 us
    pallas_call x1, Pallas kernels, per_device(): pl.pallas_call(main_kernel, grid_spec=pltpu.PrefetchScalarGridSpec(num_sc...  14.5 us
    ppermute x3, starting transfers between devices, per_device(): parts = parts + lax.ppermute(parts, 'seq', swaps)  13.1 us
    ppermute x3, waiting for transfers between devices, per_device(): parts = parts + lax.ppermute(parts, 'seq', swaps)  7.94 us
    ppermute x2, waiting for transfers between devices, passed_along(): lax.ppermute(value, axis, [(source, source + steps) for source in range(f...  5.1 us
    ppermute x2, starting transfers between devices, passed_along(): lax.ppermute(value, axis, [(source, source + steps) for source in range(f...  3.02 us
    pallas_call x1, Pallas kernels, per_device(): pl.pallas_call(rims_kernel, grid_spec=pltpu.PrefetchScalarGridSpec(num_sc...  2.3 us
  transfers between devices with their start and end apart: 5, of which 4 were waited for; matrix products, arithmetic and copies ran while one was open for 0% of the time, Pallas kernels for 0%

profile of v7, /device:TPU:2, one launch (start us, length us, event | category | flops | bytes accessed | tf_op | source)
XLA Modules:
  0.0 64.6 jit_solution(15899656814281400667)
XLA Ops:
  0.6 2.3 %rims.1 = (bf16[144,256]{1,0:T(8,128)(2,1)}, bf16[144,256]{1,0:T(8,128)(2,1)}) custom-call(s32[1]{0:T(128)} %bitcast.place_ref, bf16[2048,256]{1,0:T(8,128)(2,1)} %key_any.1, bf16[2048,256]{1,0:T(8,128)(2,1)} %value_any.1, bf16[2048,256]{1,0:T(8,128)(2,1)} %query_any.1, bf16[2048,256]{1,0:T(8,128)(2,1)} %key_two_any.1, bf16[2048,256]{1,0:T(8,128)(2,1)} %cotangent_any.1, ...), custom_call_target="tpu_custom_call" | custom-call | flops 12582912 | bytes 1048576 | tf_op jit(solution)/shard_map/rims/pallas_call | solution.py:395
  2.9 1.7 %collective-permute-start = (bf16[144,256]{1,0:T(8,128)(2,1)}, bf16[144,256]{1,0:T(8,128)(2,1)S(1)}, u32[]{:S(2)}, u32[]{:S(2)}) collective-permute-start(bf16[144,256]{1,0:T(8,128)(2,1)} %get-tuple-element.19), channel_id=1, source_target_pairs={{0,32},{32,64},{64,96},{96,128},{128,160},{160,192},{192,224},{1,3... | collective-permute-start | bytes 221192 | tf_op jit(solution)/shard_map/ppermute | solution.py:35
  4.7 1.3 %collective-permute-start.1 = (bf16[144,256]{1,0:T(8,128)(2,1)}, bf16[144,256]{1,0:T(8,128)(2,1)S(1)}, u32[]{:S(2)}, u32[]{:S(2)}) collective-permute-start(bf16[144,256]{1,0:T(8,128)(2,1)} %get-tuple-element.20), channel_id=1, source_target_pairs={{32,0},{64,32},{96,64},{128,96},{160,128},{192,160},{224,192},{33,... | collective-permute-start | bytes 221192 | tf_op jit(solution)/shard_map/ppermute | solution.py:35
  6.0 0.0 collective-permute-done.tail_ref
  6.0 0.0 copy-start
  6.0 5.1 %collective-permute-done.1.head_ref = bf16[144,256]{1,0:T(8,128)(2,1)S(1)} collective-permute-done((bf16[144,256]{1,0:T(8,128)(2,1)}, bf16[144,256]{1,0:T(8,128)(2,1)S(1)}, u32[]{:S(2)}, u32[]{:S(2)}) %collective-permute-start.1) | collective-permute-done | bytes 73760 | tf_op jit(solution)/shard_map/ppermute | solution.py:35
  11.1 0.0 copy-done
  11.1 0.0 copy-start.1
  11.1 0.6 copy-done.1
  11.7 14.5 %main.1 = (bf16[2048,256]{1,0:T(8,128)(2,1)}, bf16[2048,256]{1,0:T(8,128)(2,1)}, bf16[2048,256]{1,0:T(8,128)(2,1)}, bf16[2048,256]{1,0:T(8,128)(2,1)}, bf16[2048...) custom-call(s32[1]{0:T(128)} %bitcast.place_ref, bf16[2048,256]{1,0:T(8,128)(2,1)} %query_any.1, ...), custom_call_target="tpu_custom_call" | custom-call | flops 52428800 | bytes 12582912 | tf_op jit(solution)/shard_map/main/pallas_call | solution.py:422
  26.3 4.0 %collective-permute-start.2 = (f32[16,256]{1,0:T(8,128)}, f32[16,256]{1,0:T(8,128)S(1)}, u32[]{:S(2)}, u32[]{:S(2)}) collective-permute-start(f32[16,256]{1,0:T(8,128)} %get-tuple-element.27), channel_id=1, source_target_pairs={{0,32},{32,0},{64,96},{96,64},{128,160},{160,128},{192,224},{224,1... | collective-permute-start | bytes 49160 | tf_op jit(solution)/shard_map/ppermute | solution.py:464
  30.3 1.0 %collective-permute-done.2 = f32[16,256]{1,0:T(8,128)S(1)} collective-permute-done((f32[16,256]{1,0:T(8,128)}, f32[16,256]{1,0:T(8,128)S(1)}, u32[]{:S(2)}, u32[]{:S(2)}) %collective-permute-start.2) | collective-permute-done | bytes 16416 | tf_op jit(solution)/shard_map/ppermute | solution.py:464
  31.3 0.7 %add.9 = f32[16,256]{1,0:T(8,128)S(1)} add(f32[16,256]{1,0:T(8,128)} %get-tuple-element.27, f32[16,256]{1,0:T(8,128)S(1)} %collective-permute-done.2) | non-fusion elementwise | flops 4096 | bytes 49152 | tf_op jit(solution)/shard_map/add | solution.py:464
  32.0 6.5 %collective-permute-start.3 = (f32[16,256]{1,0:T(8,128)S(1)}, f32[16,256]{1,0:T(8,128)S(1)}, u32[]{:S(2)}, u32[]{:S(2)}) collective-permute-start(f32[16,256]{1,0:T(8,128)S(1)} %add.9), channel_id=1, source_target_pairs={{0,64},{32,96},{64,0},{96,32},{128,192},{160,224},{192,128},{224,1... | collective-permute-start | bytes 49160 | tf_op jit(solution)/shard_map/ppermute | solution.py:464
  38.5 1.8 %collective-permute-done.3 = f32[16,256]{1,0:T(8,128)S(1)} collective-permute-done((f32[16,256]{1,0:T(8,128)S(1)}, f32[16,256]{1,0:T(8,128)S(1)}, u32[]{:S(2)}, u32[]{:S(2)}) %collective-permute-start.3) | collective-permute-done | bytes 16416 | tf_op jit(solution)/shard_map/ppermute | solution.py:464
  40.3 2.6 %collective-permute-start.4 = (f32[16,256]{1,0:T(8,128)S(1)}, f32[16,256]{1,0:T(8,128)S(1)}, u32[]{:S(2)}, u32[]{:S(2)}) collective-permute-start(f32[16,256]{1,0:T(8,128)S(1)} %add.10), channel_id=1, source_target_pairs={{0,128},{32,160},{64,192},{96,224},{128,0},{160,32},{192,64},{224,... | collective-permute-start | bytes 49160 | tf_op jit(solution)/shard_map/ppermute | solution.py:464
  43.0 5.1 %collective-permute-done.4 = f32[16,256]{1,0:T(8,128)S(1)} collective-permute-done((f32[16,256]{1,0:T(8,128)S(1)}, f32[16,256]{1,0:T(8,128)S(1)}, u32[]{:S(2)}, u32[]{:S(2)}) %collective-permute-start.4) | collective-permute-done | bytes 16416 | tf_op jit(solution)/shard_map/ppermute | solution.py:464
  48.1 15.6 %all_to_all.5.table_ref = bf16[32,16,256]{2,1,0:T(8,128)(2,1)S(1)} all-to-all(bf16[32,16,256]{2,1,0:T(8,128)(2,1)S(1)} %broadcast_in_dim.2), channel_id=1, replica_groups=mesh['seq'=8,'grp'=32] {'grp'}, dimensions={0} | all-to-all | bytes 524288 | tf_op jit(solution)/shard_map/all_to_all | solution.py:468
  63.7 0.8 %unpack.1 = (f32[7,8192]{1,0:T(8,128)}, f32[512,128]{1,0:T(8,128)}) custom-call(bf16[32,16,256]{2,1,0:T(8,128)(2,1)S(1)} %all_to_all.5.table_ref), custom_call_target="tpu_custom_call" | custom-call | tf_op jit(solution)/shard_map/unpack/pallas_call | solution.py:469
  (3 shorter events, 0.0 us)
Async XLA Ops:
  2.9 3.0 %collective-permute-start = (bf16[144,256]{1,0:T(8,128)(2,1)}, bf16[144,256]{1,0:T(8,128)(2,1)S(1)}, u32[]{:S(2)}, u32[]{:S(2)}) collective-permute-start(bf16[144,256]{1,0:T(8,128)(2,1)} %get-tuple-element.19), channel_id=1, source_target_pairs={{0,32},{32,64},{64,96},{96,128},{128,160},{160,192},{192,224},{1,3... | collective-permute-start | bytes 221192 | tf_op jit(solution)/shard_map/ppermute | solution.py:35
  4.7 6.4 %collective-permute-start.1 = (bf16[144,256]{1,0:T(8,128)(2,1)}, bf16[144,256]{1,0:T(8,128)(2,1)S(1)}, u32[]{:S(2)}, u32[]{:S(2)}) collective-permute-start(bf16[144,256]{1,0:T(8,128)(2,1)} %get-tuple-element.20), channel_id=1, source_target_pairs={{32,0},{64,32},{96,64},{128,96},{160,128},{192,160},{224,192},{33,... | collective-permute-start | bytes 221192 | tf_op jit(solution)/shard_map/ppermute | solution.py:35
  6.0 5.1 %copy-start = (bf16[144,256]{1,0:T(8,128)(2,1)}, bf16[144,256]{1,0:T(8,128)(2,1)S(1)}, u32[]{:S(2)}) copy-start(bf16[144,256]{1,0:T(8,128)(2,1)S(1)} %collective-permute-done.tail_ref) | copy-start | bytes 221188
  11.1 0.6 copy-start.1
  26.3 5.0 %collective-permute-start.2 = (f32[16,256]{1,0:T(8,128)}, f32[16,256]{1,0:T(8,128)S(1)}, u32[]{:S(2)}, u32[]{:S(2)}) collective-permute-start(f32[16,256]{1,0:T(8,128)} %get-tuple-element.27), channel_id=1, source_target_pairs={{0,32},{32,0},{64,96},{96,64},{128,160},{160,128},{192,224},{224,1... | collective-permute-start | bytes 49160 | tf_op jit(solution)/shard_map/ppermute | solution.py:464
  32.0 8.3 %collective-permute-start.3 = (f32[16,256]{1,0:T(8,128)S(1)}, f32[16,256]{1,0:T(8,128)S(1)}, u32[]{:S(2)}, u32[]{:S(2)}) collective-permute-start(f32[16,256]{1,0:T(8,128)S(1)} %add.9), channel_id=1, source_target_pairs={{0,64},{32,96},{64,0},{96,32},{128,192},{160,224},{192,128},{224,1... | collective-permute-start | bytes 49160 | tf_op jit(solution)/shard_map/ppermute | solution.py:464
  40.3 7.7 %collective-permute-start.4 = (f32[16,256]{1,0:T(8,128)S(1)}, f32[16,256]{1,0:T(8,128)S(1)}, u32[]{:S(2)}, u32[]{:S(2)}) collective-permute-start(f32[16,256]{1,0:T(8,128)S(1)} %add.10), channel_id=1, source_target_pairs={{0,128},{32,160},{64,192},{96,224},{128,0},{160,32},{192,64},{224,... | collective-permute-start | bytes 49160 | tf_op jit(solution)/shard_map/ppermute | solution.py:464

commit v8 on v7

--- a/solution.py
+++ b/solution.py
@@ -73,15 +73,8 @@
     return lax.dot_general(left, right, (dims, ((), ())), preferred_element_type=jnp.float32)
 
 
-def identity(count):
-    row = lax.broadcasted_iota(jnp.int32, (count, count), 0)
-    lane = lax.broadcasted_iota(jnp.int32, (count, count), 1)
-    return narrowed(widened(row == lane))
-
-
-def turned(tile, unit):
-    flat = narrowed(dotted(unit, tile, ((1,), (1,))))
-    return flat.reshape(tile.shape[1] // GROUP, GROUP, tile.shape[0])
+def turned(tile):
+    return tile.T.reshape(tile.shape[1] // GROUP, GROUP, tile.shape[0])
 
 
 def rims_kernel(
@@ -186,10 +179,8 @@
         load(piece)
 
     coefs_ref[...] = widened(medium_ref[...])
-    unit = identity(chan_count)
-    small_unit = unit[:BLOCK, :BLOCK]
-    product_ref[:, :GROUP, :] = turned(tail_ref[HALO:], unit)
-    turned_ref[:, span:, :] = turned(head_ref[:BLOCK], unit)
+    product_ref[:, :GROUP, :] = turned(tail_ref[HALO:])
+    turned_ref[:, span:, :] = turned(head_ref[:BLOCK])
     for half in range(halves):
         lanes = slice(half * LANES, (half + 1) * LANES)
         first_ref[half, :RIM] = widened(tail_ref[:HALO, lanes])[RIM:]
@@ -219,8 +210,8 @@
                 pair_ref[1, local, lanes] = cotangent_ref[rows, lanes] * query_two_ref[rows, lanes]
 
     def turn(chunk, pair_ref):
-        product_two = turned(pair_ref[0], unit)
-        grad_inner_two = turned(pair_ref[1], unit)
+        product_two = turned(pair_ref[0])
+        grad_inner_two = turned(pair_ref[1])
         for step in range(steps):
             index = chunk * steps + step
             local = slice(step * BLOCK, (step + 1) * BLOCK)
@@ -284,8 +275,8 @@
             local = slice(step * BLOCK, (step + 1) * BLOCK)
             back = back_ref[:, lines, :].reshape(chan_count, BLOCK)
             ahead = ahead_ref[:, lines, :].reshape(chan_count, BLOCK)
-            pair_ref[0, local] = narrowed(dotted(small_unit, back, ((1,), (1,))))
-            pair_ref[1, local] = narrowed(dotted(small_unit, ahead, ((1,), (1,))))
+            pair_ref[0, local] = back.T
+            pair_ref[1, local] = ahead.T
 
     def backward(chunk, pair_ref):
         for step in reversed(range(steps)):

time: 65.2 us -> 63.9 us (0.980)
  Pallas kernels: 17.7 us -> 16.3 us
    pallas_call x1, Pallas kernels: 14.5 us -> 13.2 us  [per_device(): pl.pallas_call(main_kernel, grid_spec=pltpu.PrefetchScalarGridSpec(num_sc...]
where the time goes in v8:
time: 63.9 us; the launch traced here: 63.2 us
  Pallas kernels  16.3 us (26%)
  starting transfers between devices  16.1 us (25%)
  blocking collectives  15.6 us (24%)
  waiting for transfers between devices  13 us (20%)
  other arithmetic  0.73 us (1%)
  between operations  0.69 us (1%)
  local copies, waits for them, and re-layouts  0.66 us (1%)
    all_to_all x1, blocking collectives, per_device(): table = lax.all_to_all(copies, 'grp', 0, 0)  15.6 us
    pallas_call x1, Pallas kernels, per_device(): pl.pallas_call(main_kernel, grid_spec=pltpu.PrefetchScalarGridSpec(num_sc...  13.2 us
    ppermute x3, starting transfers between devices, per_device(): parts = parts + lax.ppermute(parts, 'seq', swaps)  13.1 us
    ppermute x3, waiting for transfers between devices, per_device(): parts = parts + lax.ppermute(parts, 'seq', swaps)  7.94 us
    ppermute x2, waiting for transfers between devices, passed_along(): lax.ppermute(value, axis, [(source, source + steps) for source in range(f...  5.1 us
    ppermute x2, starting transfers between devices, passed_along(): lax.ppermute(value, axis, [(source, source + steps) for source in range(f...  3.02 us
    pallas_call x1, Pallas kernels, per_device(): pl.pallas_call(rims_kernel, grid_spec=pltpu.PrefetchScalarGridSpec(num_sc...  2.3 us
  transfers between devices with their start and end apart: 5, of which 4 were waited for; matrix products, arithmetic and copies ran while one was open for 0% of the time, Pallas kernels for 0%

profile of v8, /device:TPU:2, one launch (start us, length us, event | category | flops | bytes accessed | tf_op | source)
XLA Modules:
  0.0 63.2 jit_solution(1410454505931640600)
XLA Ops:
  0.6 2.3 %rims.1 = (bf16[144,256]{1,0:T(8,128)(2,1)}, bf16[144,256]{1,0:T(8,128)(2,1)}) custom-call(s32[1]{0:T(128)} %bitcast.place_ref, bf16[2048,256]{1,0:T(8,128)(2,1)} %key_any.1, bf16[2048,256]{1,0:T(8,128)(2,1)} %value_any.1, bf16[2048,256]{1,0:T(8,128)(2,1)} %query_any.1, bf16[2048,256]{1,0:T(8,128)(2,1)} %key_two_any.1, bf16[2048,256]{1,0:T(8,128)(2,1)} %cotangent_any.1, ...), custom_call_target="tpu_custom_call" | custom-call | flops 12582912 | bytes 1048576 | tf_op jit(solution)/shard_map/rims/pallas_call | solution.py:386
  2.9 1.7 %collective-permute-start = (bf16[144,256]{1,0:T(8,128)(2,1)}, bf16[144,256]{1,0:T(8,128)(2,1)S(1)}, u32[]{:S(2)}, u32[]{:S(2)}) collective-permute-start(bf16[144,256]{1,0:T(8,128)(2,1)} %get-tuple-element.19), channel_id=1, source_target_pairs={{0,32},{32,64},{64,96},{96,128},{128,160},{160,192},{192,224},{1,3... | collective-permute-start | bytes 221192 | tf_op jit(solution)/shard_map/ppermute | solution.py:35
  4.7 1.3 %collective-permute-start.1 = (bf16[144,256]{1,0:T(8,128)(2,1)}, bf16[144,256]{1,0:T(8,128)(2,1)S(1)}, u32[]{:S(2)}, u32[]{:S(2)}) collective-permute-start(bf16[144,256]{1,0:T(8,128)(2,1)} %get-tuple-element.20), channel_id=1, source_target_pairs={{32,0},{64,32},{96,64},{128,96},{160,128},{192,160},{224,192},{33,... | collective-permute-start | bytes 221192 | tf_op jit(solution)/shard_map/ppermute | solution.py:35
  6.0 0.0 collective-permute-done.tail_ref
  6.0 0.0 copy-start
  6.0 5.1 %collective-permute-done.1.head_ref = bf16[144,256]{1,0:T(8,128)(2,1)S(1)} collective-permute-done((bf16[144,256]{1,0:T(8,128)(2,1)}, bf16[144,256]{1,0:T(8,128)(2,1)S(1)}, u32[]{:S(2)}, u32[]{:S(2)}) %collective-permute-start.1) | collective-permute-done | bytes 73760 | tf_op jit(solution)/shard_map/ppermute | solution.py:35
  11.1 0.0 copy-done
  11.1 0.0 copy-start.1
  11.1 0.6 copy-done.1
  11.7 13.2 %main.1 = (bf16[2048,256]{1,0:T(8,128)(2,1)}, bf16[2048,256]{1,0:T(8,128)(2,1)}, bf16[2048,256]{1,0:T(8,128)(2,1)}, bf16[2048,256]{1,0:T(8,128)(2,1)}, bf16[2048...) custom-call(s32[1]{0:T(128)} %bitcast.place_ref, bf16[2048,256]{1,0:T(8,128)(2,1)} %query_any.1, ...), custom_call_target="tpu_custom_call" | custom-call | flops 52428800 | bytes 12582912 | tf_op jit(solution)/shard_map/main/pallas_call | solution.py:413
  24.9 4.0 %collective-permute-start.2 = (f32[16,256]{1,0:T(8,128)}, f32[16,256]{1,0:T(8,128)S(1)}, u32[]{:S(2)}, u32[]{:S(2)}) collective-permute-start(f32[16,256]{1,0:T(8,128)} %get-tuple-element.27), channel_id=1, source_target_pairs={{0,32},{32,0},{64,96},{96,64},{128,160},{160,128},{192,224},{224,1... | collective-permute-start | bytes 49160 | tf_op jit(solution)/shard_map/ppermute | solution.py:455
  28.9 1.0 %collective-permute-done.2 = f32[16,256]{1,0:T(8,128)S(1)} collective-permute-done((f32[16,256]{1,0:T(8,128)}, f32[16,256]{1,0:T(8,128)S(1)}, u32[]{:S(2)}, u32[]{:S(2)}) %collective-permute-start.2) | collective-permute-done | bytes 16416 | tf_op jit(solution)/shard_map/ppermute | solution.py:455
  30.0 0.7 %add.9 = f32[16,256]{1,0:T(8,128)S(1)} add(f32[16,256]{1,0:T(8,128)} %get-tuple-element.27, f32[16,256]{1,0:T(8,128)S(1)} %collective-permute-done.2) | non-fusion elementwise | flops 4096 | bytes 49152 | tf_op jit(solution)/shard_map/add | solution.py:455
  30.7 6.5 %collective-permute-start.3 = (f32[16,256]{1,0:T(8,128)S(1)}, f32[16,256]{1,0:T(8,128)S(1)}, u32[]{:S(2)}, u32[]{:S(2)}) collective-permute-start(f32[16,256]{1,0:T(8,128)S(1)} %add.9), channel_id=1, source_target_pairs={{0,64},{32,96},{64,0},{96,32},{128,192},{160,224},{192,128},{224,1... | collective-permute-start | bytes 49160 | tf_op jit(solution)/shard_map/ppermute | solution.py:455
  37.2 1.8 %collective-permute-done.3 = f32[16,256]{1,0:T(8,128)S(1)} collective-permute-done((f32[16,256]{1,0:T(8,128)S(1)}, f32[16,256]{1,0:T(8,128)S(1)}, u32[]{:S(2)}, u32[]{:S(2)}) %collective-permute-start.3) | collective-permute-done | bytes 16416 | tf_op jit(solution)/shard_map/ppermute | solution.py:455
  39.0 2.6 %collective-permute-start.4 = (f32[16,256]{1,0:T(8,128)S(1)}, f32[16,256]{1,0:T(8,128)S(1)}, u32[]{:S(2)}, u32[]{:S(2)}) collective-permute-start(f32[16,256]{1,0:T(8,128)S(1)} %add.10), channel_id=1, source_target_pairs={{0,128},{32,160},{64,192},{96,224},{128,0},{160,32},{192,64},{224,... | collective-permute-start | bytes 49160 | tf_op jit(solution)/shard_map/ppermute | solution.py:455
  41.6 5.1 %collective-permute-done.4 = f32[16,256]{1,0:T(8,128)S(1)} collective-permute-done((f32[16,256]{1,0:T(8,128)S(1)}, f32[16,256]{1,0:T(8,128)S(1)}, u32[]{:S(2)}, u32[]{:S(2)}) %collective-permute-start.4) | collective-permute-done | bytes 16416 | tf_op jit(solution)/shard_map/ppermute | solution.py:455
  46.7 15.6 %all_to_all.5.table_ref = bf16[32,16,256]{2,1,0:T(8,128)(2,1)S(1)} all-to-all(bf16[32,16,256]{2,1,0:T(8,128)(2,1)S(1)} %broadcast_in_dim.2), channel_id=1, replica_groups=mesh['seq'=8,'grp'=32] {'grp'}, dimensions={0} | all-to-all | bytes 524288 | tf_op jit(solution)/shard_map/all_to_all | solution.py:459
  62.4 0.8 %unpack.1 = (f32[7,8192]{1,0:T(8,128)}, f32[512,128]{1,0:T(8,128)}) custom-call(bf16[32,16,256]{2,1,0:T(8,128)(2,1)S(1)} %all_to_all.5.table_ref), custom_call_target="tpu_custom_call" | custom-call | tf_op jit(solution)/shard_map/unpack/pallas_call | solution.py:460
  (3 shorter events, 0.0 us)
Async XLA Ops:
  2.9 3.0 %collective-permute-start = (bf16[144,256]{1,0:T(8,128)(2,1)}, bf16[144,256]{1,0:T(8,128)(2,1)S(1)}, u32[]{:S(2)}, u32[]{:S(2)}) collective-permute-start(bf16[144,256]{1,0:T(8,128)(2,1)} %get-tuple-element.19), channel_id=1, source_target_pairs={{0,32},{32,64},{64,96},{96,128},{128,160},{160,192},{192,224},{1,3... | collective-permute-start | bytes 221192 | tf_op jit(solution)/shard_map/ppermute | solution.py:35
  4.7 6.4 %collective-permute-start.1 = (bf16[144,256]{1,0:T(8,128)(2,1)}, bf16[144,256]{1,0:T(8,128)(2,1)S(1)}, u32[]{:S(2)}, u32[]{:S(2)}) collective-permute-start(bf16[144,256]{1,0:T(8,128)(2,1)} %get-tuple-element.20), channel_id=1, source_target_pairs={{32,0},{64,32},{96,64},{128,96},{160,128},{192,160},{224,192},{33,... | collective-permute-start | bytes 221192 | tf_op jit(solution)/shard_map/ppermute | solution.py:35
  6.0 5.1 %copy-start = (bf16[144,256]{1,0:T(8,128)(2,1)}, bf16[144,256]{1,0:T(8,128)(2,1)S(1)}, u32[]{:S(2)}) copy-start(bf16[144,256]{1,0:T(8,128)(2,1)S(1)} %collective-permute-done.tail_ref) | copy-start | bytes 221188
  11.1 0.6 %copy-start.1 = (bf16[144,256]{1,0:T(8,128)(2,1)}, bf16[144,256]{1,0:T(8,128)(2,1)S(1)}, u32[]{:S(2)}) copy-start(bf16[144,256]{1,0:T(8,128)(2,1)S(1)} %collective-permute-done.1.head_ref) | copy-start | bytes 221188
  24.9 5.0 %collective-permute-start.2 = (f32[16,256]{1,0:T(8,128)}, f32[16,256]{1,0:T(8,128)S(1)}, u32[]{:S(2)}, u32[]{:S(2)}) collective-permute-start(f32[16,256]{1,0:T(8,128)} %get-tuple-element.27), channel_id=1, source_target_pairs={{0,32},{32,0},{64,96},{96,64},{128,160},{160,128},{192,224},{224,1... | collective-permute-start | bytes 49160 | tf_op jit(solution)/shard_map/ppermute | solution.py:455
  30.7 8.3 %collective-permute-start.3 = (f32[16,256]{1,0:T(8,128)S(1)}, f32[16,256]{1,0:T(8,128)S(1)}, u32[]{:S(2)}, u32[]{:S(2)}) collective-permute-start(f32[16,256]{1,0:T(8,128)S(1)} %add.9), channel_id=1, source_target_pairs={{0,64},{32,96},{64,0},{96,32},{128,192},{160,224},{192,128},{224,1... | collective-permute-start | bytes 49160 | tf_op jit(solution)/shard_map/ppermute | solution.py:455
  39.0 7.7 %collective-permute-start.4 = (f32[16,256]{1,0:T(8,128)S(1)}, f32[16,256]{1,0:T(8,128)S(1)}, u32[]{:S(2)}, u32[]{:S(2)}) collective-permute-start(f32[16,256]{1,0:T(8,128)S(1)} %add.10), channel_id=1, source_target_pairs={{0,128},{32,160},{64,192},{96,224},{128,0},{160,32},{192,64},{224,... | collective-permute-start | bytes 49160 | tf_op jit(solution)/shard_map/ppermute | solution.py:455

commit v9 on v8

--- a/solution.py
+++ b/solution.py
@@ -61,12 +61,13 @@
 
 
 def diagonal_sums(pairs):
+    width = 2 * BLOCK
     total = sum(
-        moved_lanes(pairs[first : first + RIM], (BLOCK + 1 + first) % (2 * BLOCK))
+        moved_lanes(pairs[first : first + RIM], (width - first) % width)
         for first in range(0, BLOCK, RIM)
     )
-    total = pltpu.roll(total, 0, 1, stride=1, stride_axis=0)
-    return jnp.sum(total[:, :BLOCK], axis=0, keepdims=True)
+    line = sum(moved_lanes(total[row : row + 1], (width - row) % width) for row in range(RIM))
+    return line[:, :BLOCK]
 
 
 def dotted(left, right, dims):
@@ -79,19 +80,30 @@
 
 def rims_kernel(
     place_ref,
-    key_tail, value_tail, query_tail, key_two_tail,
-    cotangent_head, query_two_head, query_head, key_two_head,
+    key_rim, value_rim, key_tail, value_tail, query_tail, key_two_tail,
+    cotangent_head, query_two_head, cotangent_rim, query_two_rim, query_head, key_two_head,
     short_ref, medium_ref, tail_ref, head_ref,
 ):
     taps = widened(short_ref[...])
-    start = 2 * BLOCK - BLOCK - HALO
-    product_one = widened(key_tail[start:]) * widened(value_tail[start:])
+    product_one = jnp.concatenate(
+        [
+            widened(key_rim[...]) * widened(value_rim[...]),
+            widened(key_tail[...]) * widened(value_tail[...]),
+        ],
+        axis=0,
+    )
     inner_one = short_causal(product_one[RIM:HALO], product_one[HALO:], taps)
-    product_two = widened(key_two_tail[BLOCK:]) * (widened(query_tail[BLOCK:]) * inner_one)
+    product_two = widened(key_two_tail[...]) * (widened(query_tail[...]) * inner_one)
     tail_ref[:HALO] = narrowed(product_one[BLOCK:])
     tail_ref[HALO:] = narrowed(product_two)
     grad_inner = narrowed(
-        widened(cotangent_head[: BLOCK + HALO]) * widened(query_two_head[: BLOCK + HALO])
+        jnp.concatenate(
+            [
+                widened(cotangent_head[...]) * widened(query_two_head[...]),
+                widened(cotangent_rim[...]) * widened(query_two_rim[...]),
+            ],
+            axis=0,
+        )
     )
     head_ref[:BLOCK] = grad_inner[:BLOCK]
     wide = widened(grad_inner)
@@ -232,17 +244,14 @@
     forward(chunk_count - 1, odd_ref)
     turn(chunk_count - 1, odd_ref)
 
-    flip_row = lax.broadcasted_iota(jnp.int32, (BLOCK, BLOCK), 0)
-    flip_lane = lax.broadcasted_iota(jnp.int32, (BLOCK, BLOCK), 1)
-    flip = narrowed(widened(flip_row + flip_lane == BLOCK - 1))
     medium_scale = 1.0 / math.sqrt(sequence_total * GROUP)
     batch = 4
 
     def medium_batch(turn, _):
         groups = [turn * batch + place for place in range(batch)]
         bands = [upper_lower(coefs_ref[pl.ds(group, 1)]) for group in groups]
-        flipped = [
-            narrowed(dotted(flip, product_ref[group, GROUP:], ((1,), (1,)))) for group in groups
+        flat = [
+            product_ref[group, GROUP:].T for group in groups
         ]
         windows = [
             jnp.concatenate(
@@ -250,7 +259,7 @@
             )
             for group in groups
         ]
-        pairs = [dotted(left, view, ((1,), (0,))) for left, view in zip(flipped, windows)]
+        pairs = [dotted(left, view, ((1,), (0,))) for left, view in zip(flat, windows)]
         backs = [
             narrowed(dotted(view, band, ((1,), (1,)))) for view, band in zip(windows, bands)
         ]
@@ -375,9 +384,11 @@
     wide = sds((row_count, chan_count), jnp.bfloat16)
     size = row_count * chan_count * 2
 
-    last = row_count // (2 * BLOCK) - 1
-    tail_spec = pl.BlockSpec((2 * BLOCK, chan_count), lambda i, at: (last, 0))
-    head_spec = pl.BlockSpec((2 * BLOCK, chan_count), lambda i, at: (0, 0))
+    last = row_count // BLOCK - 1
+    tail_spec = pl.BlockSpec((BLOCK, chan_count), lambda i, at: (last, 0))
+    head_spec = pl.BlockSpec((BLOCK, chan_count), lambda i, at: (0, 0))
+    before_spec = pl.BlockSpec((HALO, chan_count), lambda i, at: (last * (BLOCK // HALO) - 1, 0))
+    after_spec = pl.BlockSpec((HALO, chan_count), lambda i, at: (BLOCK // HALO, 0))
     rim_spec = pl.BlockSpec((HALO, chan_count), lambda i, at: (0, 0))
     halo_spec = pl.BlockSpec((HALO + BLOCK, chan_count), lambda i, at: (0, 0))
     short_spec = pl.BlockSpec((SE_TAPS, chan_count), lambda i, at: (0, at[0]))
@@ -388,7 +399,12 @@
         grid_spec=pltpu.PrefetchScalarGridSpec(
             num_scalar_prefetch=1,
             grid=(1,),
-            in_specs=[tail_spec] * 4 + [head_spec] * 2 + [rim_spec] * 2 + [short_spec, medium_spec],
+            in_specs=[before_spec] * 2
+            + [tail_spec] * 4
+            + [head_spec] * 2
+            + [after_spec] * 2
+            + [rim_spec] * 2
+            + [short_spec, medium_spec],
             out_specs=(halo_spec, halo_spec),
         ),
         out_shape=(halo, halo),
@@ -397,8 +413,8 @@
         name="rims",
     )(
         place,
-        key_first, value_first, query_first, key_second,
-        cotangent, query_second, query_first, key_second,
+        key_first, value_first, key_first, value_first, query_first, key_second,
+        cotangent, query_second, cotangent, query_second, query_first, key_second,
         short_filter, medium_filter,
     )
     tail = passed_along(tail, "seq", 1)

time: 63.9 us -> 63.8 us (level)
  no operation moved by 1% of the time
where the time goes in v9:
time: 63.8 us; the launch traced here: 63.1 us
  Pallas kernels  16.2 us (25%)
  starting transfers between devices  16.1 us (25%)
  blocking collectives  15.6 us (24%)
  waiting for transfers between devices  13.1 us (21%)
  other arithmetic  0.73 us (1%)
  between operations  0.69 us (1%)
  local copies, waits for them, and re-layouts  0.66 us (1%)
    all_to_all x1, blocking collectives, per_device(): table = lax.all_to_all(copies, 'grp', 0, 0)  15.6 us
    pallas_call x1, Pallas kernels, per_device(): pl.pallas_call(main_kernel, grid_spec=pltpu.PrefetchScalarGridSpec(num_sc...  13.2 us
    ppermute x3, starting transfers between devices, per_device(): parts = parts + lax.ppermute(parts, 'seq', swaps)  13.1 us
    ppermute x3, waiting for transfers between devices, per_device(): parts = parts + lax.ppermute(parts, 'seq', swaps)  7.95 us
    ppermute x2, waiting for transfers between devices, passed_along(): lax.ppermute(value, axis, [(source, source + steps) for source in range(f...  5.1 us
    ppermute x2, starting transfers between devices, passed_along(): lax.ppermute(value, axis, [(source, source + steps) for source in range(f...  3.02 us
    pallas_call x1, Pallas kernels, per_device(): pl.pallas_call(rims_kernel, grid_spec=pltpu.PrefetchScalarGridSpec(num_sc...  2.16 us
  transfers between devices with their start and end apart: 5, of which 4 were waited for; matrix products, arithmetic and copies ran while one was open for 0% of the time, Pallas kernels for 0%

profile of v9, /device:TPU:2, one launch (start us, length us, event | category | flops | bytes accessed | tf_op | source)
XLA Modules:
  0.0 63.1 jit_solution(909712487740579530)
XLA Ops:
  0.6 2.2 %rims.1 = (bf16[144,256]{1,0:T(8,128)(2,1)}, bf16[144,256]{1,0:T(8,128)(2,1)}) custom-call(s32[1]{0:T(128)} %bitcast.place_ref, bf16[2048,256]{1,0:T(8,128)(2,1)} %key_any.1, bf16[2048,256]{1,0:T(8,128)(2,1)} %value_any.1, bf16[2048,256]{1,0:T(8,128)(2,1)} %key_any.1, bf16[2048,256]{1,0:T(8,128)(2,1)} %value_any.1, bf16[2048,256]{1,0:T(8,128)(2,1)} %query_any.1, ...), custom_call_target="tpu_custom_call" | custom-call | flops 12582912 | bytes 1048576 | tf_op jit(solution)/shard_map/rims/pallas_call | solution.py:397
  2.8 1.7 %collective-permute-start = (bf16[144,256]{1,0:T(8,128)(2,1)}, bf16[144,256]{1,0:T(8,128)(2,1)S(1)}, u32[]{:S(2)}, u32[]{:S(2)}) collective-permute-start(bf16[144,256]{1,0:T(8,128)(2,1)} %get-tuple-element.19), channel_id=1, source_target_pairs={{0,32},{32,64},{64,96},{96,128},{128,160},{160,192},{192,224},{1,3... | collective-permute-start | bytes 221192 | tf_op jit(solution)/shard_map/ppermute | solution.py:35
  4.5 1.3 %collective-permute-start.1 = (bf16[144,256]{1,0:T(8,128)(2,1)}, bf16[144,256]{1,0:T(8,128)(2,1)S(1)}, u32[]{:S(2)}, u32[]{:S(2)}) collective-permute-start(bf16[144,256]{1,0:T(8,128)(2,1)} %get-tuple-element.20), channel_id=1, source_target_pairs={{32,0},{64,32},{96,64},{128,96},{160,128},{192,160},{224,192},{33,... | collective-permute-start | bytes 221192 | tf_op jit(solution)/shard_map/ppermute | solution.py:35
  5.8 0.0 collective-permute-done.tail_ref
  5.8 0.0 copy-start
  5.9 5.1 %collective-permute-done.1.head_ref = bf16[144,256]{1,0:T(8,128)(2,1)S(1)} collective-permute-done((bf16[144,256]{1,0:T(8,128)(2,1)}, bf16[144,256]{1,0:T(8,128)(2,1)S(1)}, u32[]{:S(2)}, u32[]{:S(2)}) %collective-permute-start.1) | collective-permute-done | bytes 73760 | tf_op jit(solution)/shard_map/ppermute | solution.py:35
  11.0 0.0 copy-done
  11.0 0.0 copy-start.1
  11.0 0.6 %copy-done.1 = bf16[144,256]{1,0:T(8,128)(2,1)} copy-done((bf16[144,256]{1,0:T(8,128)(2,1)}, bf16[144,256]{1,0:T(8,128)(2,1)S(1)}, u32[]{:S(2)}) %copy-start.1) | copy-done | bytes 73752
  11.6 13.2 %main.1 = (bf16[2048,256]{1,0:T(8,128)(2,1)}, bf16[2048,256]{1,0:T(8,128)(2,1)}, bf16[2048,256]{1,0:T(8,128)(2,1)}, bf16[2048,256]{1,0:T(8,128)(2,1)}, bf16[2048...) custom-call(s32[1]{0:T(128)} %bitcast.place_ref, bf16[2048,256]{1,0:T(8,128)(2,1)} %query_any.1, ...), custom_call_target="tpu_custom_call" | custom-call | flops 52428800 | bytes 12582912 | tf_op jit(solution)/shard_map/main/pallas_call | solution.py:429
  24.8 4.0 %collective-permute-start.2 = (f32[16,256]{1,0:T(8,128)}, f32[16,256]{1,0:T(8,128)S(1)}, u32[]{:S(2)}, u32[]{:S(2)}) collective-permute-start(f32[16,256]{1,0:T(8,128)} %get-tuple-element.27), channel_id=1, source_target_pairs={{0,32},{32,0},{64,96},{96,64},{128,160},{160,128},{192,224},{224,1... | collective-permute-start | bytes 49160 | tf_op jit(solution)/shard_map/ppermute | solution.py:471
  28.8 1.0 %collective-permute-done.2 = f32[16,256]{1,0:T(8,128)S(1)} collective-permute-done((f32[16,256]{1,0:T(8,128)}, f32[16,256]{1,0:T(8,128)S(1)}, u32[]{:S(2)}, u32[]{:S(2)}) %collective-permute-start.2) | collective-permute-done | bytes 16416 | tf_op jit(solution)/shard_map/ppermute | solution.py:471
  29.9 0.7 %add.9 = f32[16,256]{1,0:T(8,128)S(1)} add(f32[16,256]{1,0:T(8,128)} %get-tuple-element.27, f32[16,256]{1,0:T(8,128)S(1)} %collective-permute-done.2) | non-fusion elementwise | flops 4096 | bytes 49152 | tf_op jit(solution)/shard_map/add | solution.py:471
  30.6 6.5 %collective-permute-start.3 = (f32[16,256]{1,0:T(8,128)S(1)}, f32[16,256]{1,0:T(8,128)S(1)}, u32[]{:S(2)}, u32[]{:S(2)}) collective-permute-start(f32[16,256]{1,0:T(8,128)S(1)} %add.9), channel_id=1, source_target_pairs={{0,64},{32,96},{64,0},{96,32},{128,192},{160,224},{192,128},{224,1... | collective-permute-start | bytes 49160 | tf_op jit(solution)/shard_map/ppermute | solution.py:471
  37.1 1.8 %collective-permute-done.3 = f32[16,256]{1,0:T(8,128)S(1)} collective-permute-done((f32[16,256]{1,0:T(8,128)S(1)}, f32[16,256]{1,0:T(8,128)S(1)}, u32[]{:S(2)}, u32[]{:S(2)}) %collective-permute-start.3) | collective-permute-done | bytes 16416 | tf_op jit(solution)/shard_map/ppermute | solution.py:471
  38.9 2.6 %collective-permute-start.4 = (f32[16,256]{1,0:T(8,128)S(1)}, f32[16,256]{1,0:T(8,128)S(1)}, u32[]{:S(2)}, u32[]{:S(2)}) collective-permute-start(f32[16,256]{1,0:T(8,128)S(1)} %add.10), channel_id=1, source_target_pairs={{0,128},{32,160},{64,192},{96,224},{128,0},{160,32},{192,64},{224,... | collective-permute-start | bytes 49160 | tf_op jit(solution)/shard_map/ppermute | solution.py:471
  41.5 5.1 %collective-permute-done.4 = f32[16,256]{1,0:T(8,128)S(1)} collective-permute-done((f32[16,256]{1,0:T(8,128)S(1)}, f32[16,256]{1,0:T(8,128)S(1)}, u32[]{:S(2)}, u32[]{:S(2)}) %collective-permute-start.4) | collective-permute-done | bytes 16416 | tf_op jit(solution)/shard_map/ppermute | solution.py:471
  46.6 15.6 %all_to_all.5.table_ref = bf16[32,16,256]{2,1,0:T(8,128)(2,1)S(1)} all-to-all(bf16[32,16,256]{2,1,0:T(8,128)(2,1)S(1)} %broadcast_in_dim.2), channel_id=1, replica_groups=mesh['seq'=8,'grp'=32] {'grp'}, dimensions={0} | all-to-all | bytes 524288 | tf_op jit(solution)/shard_map/all_to_all | solution.py:475
  62.3 0.8 %unpack.1 = (f32[7,8192]{1,0:T(8,128)}, f32[512,128]{1,0:T(8,128)}) custom-call(bf16[32,16,256]{2,1,0:T(8,128)(2,1)S(1)} %all_to_all.5.table_ref), custom_call_target="tpu_custom_call" | custom-call | tf_op jit(solution)/shard_map/unpack/pallas_call | solution.py:476
  (3 shorter events, 0.0 us)
Async XLA Ops:
  2.8 3.0 %collective-permute-start = (bf16[144,256]{1,0:T(8,128)(2,1)}, bf16[144,256]{1,0:T(8,128)(2,1)S(1)}, u32[]{:S(2)}, u32[]{:S(2)}) collective-permute-start(bf16[144,256]{1,0:T(8,128)(2,1)} %get-tuple-element.19), channel_id=1, source_target_pairs={{0,32},{32,64},{64,96},{96,128},{128,160},{160,192},{192,224},{1,3... | collective-permute-start | bytes 221192 | tf_op jit(solution)/shard_map/ppermute | solution.py:35
  4.5 6.4 %collective-permute-start.1 = (bf16[144,256]{1,0:T(8,128)(2,1)}, bf16[144,256]{1,0:T(8,128)(2,1)S(1)}, u32[]{:S(2)}, u32[]{:S(2)}) collective-permute-start(bf16[144,256]{1,0:T(8,128)(2,1)} %get-tuple-element.20), channel_id=1, source_target_pairs={{32,0},{64,32},{96,64},{128,96},{160,128},{192,160},{224,192},{33,... | collective-permute-start | bytes 221192 | tf_op jit(solution)/shard_map/ppermute | solution.py:35
  5.8 5.1 %copy-start = (bf16[144,256]{1,0:T(8,128)(2,1)}, bf16[144,256]{1,0:T(8,128)(2,1)S(1)}, u32[]{:S(2)}) copy-start(bf16[144,256]{1,0:T(8,128)(2,1)S(1)} %collective-permute-done.tail_ref) | copy-start | bytes 221188
  11.0 0.6 %copy-start.1 = (bf16[144,256]{1,0:T(8,128)(2,1)}, bf16[144,256]{1,0:T(8,128)(2,1)S(1)}, u32[]{:S(2)}) copy-start(bf16[144,256]{1,0:T(8,128)(2,1)S(1)} %collective-permute-done.1.head_ref) | copy-start | bytes 221188
  24.8 5.0 %collective-permute-start.2 = (f32[16,256]{1,0:T(8,128)}, f32[16,256]{1,0:T(8,128)S(1)}, u32[]{:S(2)}, u32[]{:S(2)}) collective-permute-start(f32[16,256]{1,0:T(8,128)} %get-tuple-element.27), channel_id=1, source_target_pairs={{0,32},{32,0},{64,96},{96,64},{128,160},{160,128},{192,224},{224,1... | collective-permute-start | bytes 49160 | tf_op jit(solution)/shard_map/ppermute | solution.py:471
  30.6 8.3 %collective-permute-start.3 = (f32[16,256]{1,0:T(8,128)S(1)}, f32[16,256]{1,0:T(8,128)S(1)}, u32[]{:S(2)}, u32[]{:S(2)}) collective-permute-start(f32[16,256]{1,0:T(8,128)S(1)} %add.9), channel_id=1, source_target_pairs={{0,64},{32,96},{64,0},{96,32},{128,192},{160,224},{192,128},{224,1... | collective-permute-start | bytes 49160 | tf_op jit(solution)/shard_map/ppermute | solution.py:471
  38.9 7.7 %collective-permute-start.4 = (f32[16,256]{1,0:T(8,128)S(1)}, f32[16,256]{1,0:T(8,128)S(1)}, u32[]{:S(2)}, u32[]{:S(2)}) collective-permute-start(f32[16,256]{1,0:T(8,128)S(1)} %add.10), channel_id=1, source_target_pairs={{0,128},{32,160},{64,192},{96,224},{128,0},{160,32},{192,64},{224,... | collective-permute-start | bytes 49160 | tf_op jit(solution)/shard_map/ppermute | solution.py:471
